TPU v7x, 32 devices: a whole 2x2x4 slice. The times are simulated.
32 devices in a mesh: lat: 4 (over y, x), lon: 8 (over z, core).
Axes of the slice: x: 2, y: 2, z: 4, core: 2. Of those that a mesh axis runs over, the one named last changes fastest.
Arguments:
- obs_features: bfloat16 [65536, 128], P(('lat', 'lon')), may hold values from -6 to 6
- obs_dest: int32 [65536, 1], P(('lat', 'lon')), may hold values from 0 to 31; in each aligned block of 2048 rows (0 to 2047, 2048 to 4095, ...) at most 128 rows name the same one
- obs_cells: int32 [65536, 4], P(('lat', 'lon')), may hold values from 0 to 8099, as said below
- obs_gauss: int32 [65536, 4], P(('lat', 'lon')), may hold values from 0 to 31
- row_counts: int32 [32], P(('lat', 'lon')), may hold values from 512 to 2048, as said below
- background: bfloat16 [360, 720, 256], P('lat', 'lon'), may hold values from -6 to 6
- w_in: bfloat16 [128, 256], replicated, may hold values from -0.5 to 0.5
- w_bg: bfloat16 [256, 256], replicated, may hold values from -0.375 to 0.375
- w_dens: float32 [256], replicated, may hold values from -6 to 6
- conv_one: bfloat16 [3, 3, 256, 256], replicated, may hold values from -0.125 to 0.125
- conv_two: bfloat16 [3, 3, 256, 256], replicated, may hold values from -0.125 to 0.125
Outputs:
- encoded: bfloat16 [360, 720, 256], P('lat', 'lon')
Inputs may be any that keep to these rules, and one draw needn't show every extreme that they name: `obs_cells`: each row names the four cells of a 2 by 2 square of its destination tile of 90 x 90 cells, flattened row-major: c, c + 1, c + 90, c + 91. `obs_dest`: among the rows of one device, no tile is named by more than 128 rows; some tile is named by exactly 128. `row_counts`: some device has all 2048 rows live.
All inputs are finite; a program needn't handle non-finite values.
Results may differ from a plain program's by a relative error of at most 0.0054.
Values may be sent and summed in bfloat16 or wider, within the bound.
No kernel may reach another device: no remote copies, remote signals or barrier semaphores. Data moves between devices by JAX's collectives and lax.ppermute only.
A program may use at most 192 MiB of HBM per device.

v0:
```python
import jax
import jax.numpy as jnp
from jax import lax
from jax.sharding import PartitionSpec as P

KCELL = 4
GBINS = 32


def with_halo(cells, sides, width, closed):
    for axis, dim in sides:
        count = lax.axis_size(axis)
        ends = count if closed else count - 1
        head = lax.slice_in_dim(cells, 0, width, axis=dim)
        tail = lax.slice_in_dim(cells, cells.shape[dim] - width, cells.shape[dim], axis=dim)
        cells = jnp.concatenate(
            [
                lax.ppermute(tail, axis, [(i, (i + 1) % count) for i in range(ends)]),
                cells,
                lax.ppermute(head, axis, [((i + 1) % count, i) for i in range(ends)]),
            ],
            axis=dim,
        )
    return cells


def shifted(value, axis, steps):
    count = lax.axis_size(axis)
    pairs = [(source, (source + steps) % count) for source in range(count)]
    return lax.ppermute(value, axis, pairs)


def extend(field):
    wide = with_halo(field, (("lon", 1),), 1, True)
    tall = with_halo(wide, (("lat", 0),), 1, False)
    rims = jnp.stack([wide[0], wide[-1]])
    across = shifted(rims, "lon", lax.axis_size("lon") // 2)
    lat_index = lax.axis_index("lat")
    top = jnp.where(lat_index == 0, across[0], tall[0])
    bottom = jnp.where(lat_index == lax.axis_size("lat") - 1, across[1], tall[-1])
    return jnp.concatenate([top[None], tall[1:-1], bottom[None]], axis=0)


def convolve(field, weights):
    lat_rows, lon_cols, chans = field.shape
    padded = extend(field)
    total = jnp.zeros((lat_rows * lon_cols, chans), jnp.float32)
    for row_off in range(3):
        for col_off in range(3):
            window = padded[row_off : row_off + lat_rows, col_off : col_off + lon_cols].reshape(
                lat_rows * lon_cols, chans
            )
            total = total + jnp.dot(
                window, weights[row_off, col_off], preferred_element_type=jnp.float32
            )
    return total.reshape(lat_rows, lon_cols, chans)


def shards(
    obs_features,
    obs_dest,
    obs_cells,
    obs_gauss,
    row_counts,
    background,
    w_in,
    w_bg,
    w_dens,
    conv_one,
    conv_two,
):
    nrows, nfeat = obs_features.shape
    lat_rows, lon_cols, chans = background.shape
    devices = lax.axis_size(("lat", "lon"))
    capacity = 2 * nrows // devices
    live = (jnp.arange(nrows, dtype=jnp.int32) < row_counts[0]).astype(jnp.int32)
    dest = obs_dest[:, 0]
    onehot = (dest[:, None] == jnp.arange(devices, dtype=jnp.int32)[None, :]).astype(jnp.int32)
    before = jnp.cumsum(onehot, axis=0) - onehot
    placing = jnp.sum(before * onehot, axis=1)
    position = dest * capacity + placing
    ints = jnp.concatenate([obs_cells, obs_gauss, live[:, None]], axis=1)
    width_int = ints.shape[1]
    send_feat = jnp.zeros((devices * capacity, nfeat), jnp.bfloat16).at[position].set(obs_features)
    send_int = jnp.zeros((devices * capacity, width_int), jnp.int32).at[position].set(ints)
    got_feat, got_int = (
        lax.all_to_all(
            send_feat.reshape(devices, capacity, nfeat),
            ("lat", "lon"),
            split_axis=0,
            concat_axis=0,
            tiled=True,
        ),
        lax.all_to_all(
            send_int.reshape(devices, capacity, width_int),
            ("lat", "lon"),
            split_axis=0,
            concat_axis=0,
            tiled=True,
        ),
    )
    slots = devices * capacity
    got_feat = got_feat.reshape(slots, nfeat)
    got_int = got_int.reshape(slots, width_int)
    got_cells = got_int[:, 0:KCELL]
    ratio = got_int[:, KCELL : 2 * KCELL].astype(jnp.float32) / GBINS
    weight = (
        jnp.exp(-3.0 * ratio * ratio) * got_int[:, 2 * KCELL : 2 * KCELL + 1].astype(jnp.float32)
    ).astype(jnp.bfloat16)
    ncells = lat_rows * lon_cols
    block = 512
    nblocks = -(-ncells // block)

    def one_block(begin):
        cell_ids = begin + jnp.arange(block, dtype=jnp.int32)
        spread = jnp.zeros((block, slots), jnp.bfloat16)
        for slot in range(KCELL):
            hit = got_cells[:, slot][None, :] == cell_ids[:, None]
            spread = spread + jnp.where(hit, weight[:, slot][None, :], jnp.zeros((), jnp.bfloat16))
        block_sums = jnp.dot(spread, got_feat, preferred_element_type=jnp.float32)
        block_dens = jnp.sum(spread.astype(jnp.float32), axis=1)
        return (block_sums, block_dens)

    starts = jnp.arange(0, nblocks * block, block, dtype=jnp.int32)
    sums, density = lax.map(one_block, starts)
    sums = sums.reshape(nblocks * block, nfeat)[:ncells]
    density = density.reshape(nblocks * block)[:ncells]
    normalized = (sums / (density + 1.0)[:, None]).astype(jnp.bfloat16)
    start = jnp.dot(normalized, w_in, preferred_element_type=jnp.float32)
    start = start + jnp.dot(
        background.reshape(ncells, chans), w_bg, preferred_element_type=jnp.float32
    )
    start = start + density[:, None] * w_dens[None, :]
    first = start.astype(jnp.bfloat16).reshape(lat_rows, lon_cols, chans)
    hidden = jax.nn.gelu(convolve(first, conv_one)).astype(jnp.bfloat16)
    return (first.astype(jnp.float32) + convolve(hidden, conv_two)).astype(jnp.bfloat16)


def solution(mesh):
    in_specs = (
        P(("lat", "lon"), None),
        P(("lat", "lon"), None),
        P(("lat", "lon"), None),
        P(("lat", "lon"), None),
        P(("lat", "lon")),
        P("lat", "lon", None),
        P(),
        P(),
        P(),
        P(),
        P(),
    )
    out_specs = P("lat", "lon", None)
    return jax.shard_map(shards, mesh=mesh, in_specs=in_specs, out_specs=out_specs, check_vma=False)
```

profile of v0, /device:TPU:0, one launch (start us, length us, event | category | flops | bytes accessed | tf_op | source)
XLA Modules:
  0.0 614.1 jit_solution(16576663583556943783)
XLA Ops:
  0.8 9.1 %reduce-window.6 = s32[32,16,128]{2,1,0:T(8,128)S(1)} reduce-window(s32[32,16,128]{2,1,0:T(8,128)S(1)} %fusion.46, s32[]{:T(128)} %constant.24.clone.1), window={size=1x1x128 pad=0_0x0_0x127_0}, to_apply=%region_0.0 | reduce-window | flops 8323072 | bytes 524292 | tf_op jit(solution)/shard_map/reduce-window
  21.4 7.3 %all-to-all-start = ((s32[32,128,9]{1,2,0:T(8,128)}), s32[32,128,9]{1,2,0:T(8,128)S(1)}, u32[]{:S(2)}, u32[]{:S(2)}) async-start(s32[32,128,9]{1,2,0:T(8,128)} %copy.28), calls=%async_computation | async-start | bytes 524288 | tf_op jit(solution)/shard_map/all_to_all | solution.py:94
  35.6 7.2 %scatter_custom_fusion.1 = bf16[4096,128]{1,0:T(8,128)(2,1)} fusion(s32[2048]{0:T(1024)S(1)} %bitcast.173, bf16[2048,128]{1,0:T(8,128)(2,1)} %param.13, bf16[]{:T(256)} %constant.31.clone.1), kind=kCustom, calls=%fused_computation.71 | custom fusion | bytes 1049088 | tf_op jit(solution)/shard_map/scatter | solution.py:84
  55.9 20.6 %all-to-all-done.1 = bf16[32,128,128]{2,1,0:T(8,128)(2,1)S(1)} async-done(((bf16[32,128,128]{2,1,0:T(8,128)(2,1)}), bf16[32,128,128]{2,1,0:T(8,128)(2,1)S(1)}, u32[]{:S(2)}, u32[]{:S(2)}) %all-to-all-start.1) | async-done | bytes 1048608 | tf_op jit(solution)/shard_map/all_to_all | solution.py:87
  76.5 196.3 %while.12 = (s32[]{:T(128)}, f32[16,512,128]{2,1,0:T(8,128)}, f32[16,512]{1,0:T(8,128)S(1)}, s32[4096,4]{0,1:T(4,128)S(1)}, s32[16]{0:T(128)S(1)}, /*index=5*/bf...) while((s32[]{:T(128)}, f32[16,512,128]{2,1,0:T(8,128)}, ...), condition=%wide.region_7.8_spmd, body=%wide.region_5.7_spmd.sunk | while | flops 587202560 | bytes 1716849 | solution.py:125
  272.8 11.0 %fusion.17 = bf16[8100,256]{1,0:T(8,128)(2,1)} fusion(f32[8100,256]{1,0:T(8,128)} %fusion.99, bf16[128,256]{1,0:T(8,128)(2,1)S(1)} %copy-done.9, f32[256]{0:T(256)S(1)} %copy-done.10, f32[8100]{0:T(1024)S(1)} %get-tuple-element.100, f32[8192,128]{1,0:T(8,128)} %bitcast.174, f32[8100]{0:T(1024)S(1)} %get-tuple-element.99), kind=kOutput, calls=%fused_computation.39 | convolution fusion | flops 541209600 | bytes 16726304 | tf_op jit(solution)/shard_map/dot_general | solution.py:129
  305.2 7.1 %pad_maximum_fusion.4 = (bf16[90,90,256]{2,1,0:T(8,128)(2,1)}, bf16[90,90,256]{2,1,0:T(8,128)(2,1)}) fusion(bf16[90,1,256]{2,1,0:T(2,128)(2,1)S(1)} %collective-permute-done.1, bf16[90,90,256]{2,1,0:T(8,128)(2,1)S(1)} %bitcast.142, bf16[90,1,256]{2,1,0:T(2,128)(2,1)S(1)} %collective-permute-done), kind=kLoop, calls=%fused_computation.63 | loop fusion | flops 16588800 | bytes 12533760 | tf_op jit(solution)/shard_map/concatenate | solution.py:16
  319.2 7.0 %reshape.134 = bf16[8100,256]{1,0:T(8,128)(2,1)} reshape(bf16[90,90,256]{2,1,0:T(8,128)(2,1)} %get-tuple-element.91) | data formatting | bytes 8294400 | tf_op jit(solution)/shard_map/reshape | solution.py:50
  326.2 9.8 %maximum_maximum_fusion = (bf16[91,92,256]{2,1,0:T(8,128)(2,1)S(1)}, bf16[91,92,256]{2,1,0:T(8,128)(2,1)S(1)}) fusion(bf16[90,1,256]{2,1,0:T(2,128)(2,1)S(1)} %collective-permute-done.1, bf16[90,90,256]{2,1,0:T(8,128)(2,1)} %reshape.129, bf16[90,1,256]{2,1,0:T(2,128)(2,1)S(1)} %collective-permute-done, bf16[1,92,256]{2,1,0:T(8,128)(2,1)S(1)} %get-tuple-element.97, ...), kind=kLoop, calls=%fused_computation.57 | loop fusion | flops 34291712 | bytes 12906496 | tf_op jit(solution)/shard_map/concatenate | solution.py:41
  336.0 11.7 %fusion.95 = (bf16[90,90,256]{2,1,0:T(8,128)(2,1)}, bf16[90,90,256]{2,1,0:T(8,128)(2,1)}, bf16[90,90,256]{2,1,0:T(8,128)(2,1)}, bf16[90,90,256]{2,1,0:T(8,128)(2...) fusion(bf16[91,92,256]{2,1,0:T(8,128)(2,1)S(1)} %get-tuple-element.72, ...), kind=kLoop, calls=%fused_computation.150 | loop fusion | bytes 49766400 | tf_op jit(solution)/shard_map/slice | solution.py:50
  347.7 6.9 %reshape.130 = bf16[8100,256]{1,0:T(8,128)(2,1)} reshape(bf16[90,90,256]{2,1,0:T(8,128)(2,1)} %get-tuple-element.101) | data formatting | bytes 8294400 | tf_op jit(solution)/shard_map/reshape | solution.py:50
  361.3 6.9 %reshape.131 = bf16[8100,256]{1,0:T(8,128)(2,1)} reshape(bf16[90,90,256]{2,1,0:T(8,128)(2,1)} %get-tuple-element.102) | data formatting | bytes 8294400 | tf_op jit(solution)/shard_map/reshape | solution.py:50
  375.1 6.9 %reshape.135 = bf16[8100,256]{1,0:T(8,128)(2,1)} reshape(bf16[90,90,256]{2,1,0:T(8,128)(2,1)} %get-tuple-element.83) | data formatting | bytes 8294400 | tf_op jit(solution)/shard_map/reshape | solution.py:50
  388.7 6.9 %reshape.136 = bf16[8100,256]{1,0:T(8,128)(2,1)} reshape(bf16[90,90,256]{2,1,0:T(8,128)(2,1)} %get-tuple-element.82) | data formatting | bytes 8294400 | tf_op jit(solution)/shard_map/reshape | solution.py:50
  395.6 7.1 %reshape.137 = bf16[8100,256]{1,0:T(8,128)(2,1)} reshape(bf16[90,90,256]{2,1,0:T(8,128)(2,1)} %get-tuple-element.81) | data formatting | bytes 8294400 | tf_op jit(solution)/shard_map/reshape | solution.py:50
  429.3 9.5 %reshape.138 = f32[90,90,256]{2,1,0:T(8,128)} reshape(f32[8100,256]{1,0:T(8,128)} %convolution_add_fusion.7) | data formatting | bytes 16588800 | tf_op jit(solution)/shard_map/reshape | solution.py:56
  460.8 7.2 %pad_maximum_fusion.2 = (bf16[90,90,256]{2,1,0:T(8,128)(2,1)}, bf16[90,90,256]{2,1,0:T(8,128)(2,1)}) fusion(bf16[90,1,256]{2,1,0:T(2,128)(2,1)S(1)} %collective-permute-done.6, bf16[90,90,256]{2,1,0:T(8,128)(2,1)S(1)} %fusion.25, bf16[90,1,256]{2,1,0:T(2,128)(2,1)S(1)} %collective-permute-done.5), kind=kLoop, calls=%fused_computation.61 | loop fusion | flops 16588800 | bytes 12533760 | tf_op jit(solution)/shard_map/concatenate | solution.py:16
  481.9 11.0 %maximum_maximum_fusion.1 = (bf16[91,92,256]{2,1,0:T(8,128)(2,1)S(1)}, bf16[91,92,256]{2,1,0:T(8,128)(2,1)}) fusion(bf16[90,1,256]{2,1,0:T(2,128)(2,1)S(1)} %collective-permute-done.6, bf16[90,90,256]{2,1,0:T(8,128)(2,1)} %copy-done.2, bf16[90,1,256]{2,1,0:T(2,128)(2,1)S(1)} %collective-permute-done.5, bf16[1,92,256]{2,1,0:T(8,128)(2,1)S(1)} %get-tuple-element.95, ...), kind=kLoop, calls=%fused_computation.59 | loop fusion | flops 34291712 | bytes 12906496 | tf_op jit(solution)/shard_map/concatenate | solution.py:41
  492.9 7.9 %fusion.94 = (bf16[90,90,256]{2,1,0:T(8,128)(2,1)}, bf16[90,90,256]{2,1,0:T(8,128)(2,1)}, bf16[90,90,256]{2,1,0:T(8,128)(2,1)}) fusion(bf16[91,92,256]{2,1,0:T(8,128)(2,1)S(1)} %get-tuple-element.67), kind=kLoop, calls=%fused_computation.149 | loop fusion | bytes 24883200 | tf_op jit(solution)/shard_map/slice | solution.py:50
  500.8 6.9 %reshape.139 = bf16[8100,256]{1,0:T(8,128)(2,1)} reshape(bf16[90,90,256]{2,1,0:T(8,128)(2,1)} %get-tuple-element.80) | data formatting | bytes 8294400 | tf_op jit(solution)/shard_map/reshape | solution.py:50
  528.2 12.3 %fusion.93 = (bf16[90,90,256]{2,1,0:T(8,128)(2,1)}, bf16[90,90,256]{2,1,0:T(8,128)(2,1)}, bf16[90,90,256]{2,1,0:T(8,128)(2,1)}) fusion(bf16[91,92,256]{2,1,0:T(8,128)(2,1)} %get-tuple-element.68), kind=kLoop, calls=%fused_computation.148 | loop fusion | bytes 24883200 | tf_op jit(solution)/shard_map/slice | solution.py:50
  560.9 6.9 %reshape.146 = bf16[8100,256]{1,0:T(8,128)(2,1)} reshape(bf16[90,90,256]{2,1,0:T(8,128)(2,1)} %get-tuple-element.75) | data formatting | bytes 8294400 | tf_op jit(solution)/shard_map/reshape | solution.py:50
  595.6 9.5 %reshape.147 = f32[90,90,256]{2,1,0:T(8,128)} reshape(f32[8100,256]{1,0:T(8,128)} %convolution_add_fusion.1) | data formatting | bytes 16588800 | tf_op jit(solution)/shard_map/reshape | solution.py:56
  605.1 8.5 %add_convert_fusion = bf16[90,90,256]{2,1,0:T(8,128)(2,1)} fusion(f32[90,90,256]{2,1,0:T(8,128)} %reshape.147, bf16[90,90,256]{2,1,0:T(8,128)(2,1)} %reshape.129), kind=kLoop, calls=%fused_computation.48 | loop fusion | flops 6220800 | bytes 16588800 | tf_op jit(solution)/shard_map/convert_element_type | solution.py:136
  (232 shorter events, 406.5 us)
Async XLA Ops:
  0.0 48.9 %copy-start = (bf16[256,256]{1,0:T(8,128)(2,1)S(1)}, bf16[256,256]{1,0:T(8,128)(2,1)}, u32[]{:S(2)}) copy-start(bf16[256,256]{1,0:T(8,128)(2,1)} %param.20) | copy-start | bytes 393220
  21.4 21.5 %all-to-all-start = ((s32[32,128,9]{1,2,0:T(8,128)}), s32[32,128,9]{1,2,0:T(8,128)S(1)}, u32[]{:S(2)}, u32[]{:S(2)}) async-start(s32[32,128,9]{1,2,0:T(8,128)} %copy.28), calls=%async_computation | async-start | bytes 524288 | tf_op jit(solution)/shard_map/all_to_all | solution.py:94
  42.8 33.6 %all-to-all-start.1 = ((bf16[32,128,128]{2,1,0:T(8,128)(2,1)}), bf16[32,128,128]{2,1,0:T(8,128)(2,1)S(1)}, u32[]{:S(2)}, u32[]{:S(2)}) async-start(bf16[32,128,128]{2,1,0:T(8,128)(2,1)} %bitcast.17), calls=%async_computation.1 | async-start | bytes 2097152 | tf_op jit(solution)/shard_map/all_to_all | solution.py:87
  76.5 196.3 %copy-start.9 = (bf16[128,256]{1,0:T(8,128)(2,1)S(1)}, bf16[128,256]{1,0:T(8,128)(2,1)}, u32[]{:S(2)}) copy-start(bf16[128,256]{1,0:T(8,128)(2,1)} %param.19) | copy-start | bytes 196612
  76.5 196.3 %copy-start.10 = (f32[256]{0:T(256)S(1)}, f32[256]{0:T(256)}, u32[]{:S(2)}) copy-start(f32[256]{0:T(256)} %param.21) | copy-start | bytes 3076
  291.9 10.3 %collective-permute-start = (bf16[90,1,256]{2,1,0:T(2,128)(2,1)S(1)}, bf16[90,1,256]{2,1,0:T(2,128)(2,1)S(1)}, u32[]{:S(2)}, u32[]{:S(2)}) collective-permute-start(bf16[90,1,256]{2,1,0:T(2,128)(2,1)S(1)} %get-tuple-element.93), channel_id=1, source_target_pairs={{0,1},{1,2},{2,3},{3,4},{4,5},{5,6},{6,7},{7,0},{8,9},{9,10},{10,1... | collective-permute-start | bytes 138248 | tf_op jit(solution)/shard_map/ppermute | solution.py:18
  292.0 10.2 %slice-start = ((s8[4423680]{0:T(1024)(128)(4,1)}), s8[4194304]{0:T(1024)(128)(4,1)S(1)}, s32[]{:S(2)}) async-start(s8[4423680]{0:T(1024)(128)(4,1)} %bitcast.141), calls=%async_computation.2 | async-start | bytes 8388608
  292.0 10.2 %slice-start.1 = ((s8[4423680]{0:T(1024)(128)(4,1)}), s8[229376]{0:T(1024)(128)(4,1)S(1)}, s32[]{:S(2)}) async-start(s8[4423680]{0:T(1024)(128)(4,1)} %bitcast.141), calls=%async_computation.3 | async-start | bytes 458752
  292.0 10.2 %collective-permute-start.1 = (bf16[90,1,256]{2,1,0:T(2,128)(2,1)S(1)}, bf16[90,1,256]{2,1,0:T(2,128)(2,1)S(1)}, u32[]{:S(2)}, u32[]{:S(2)}) collective-permute-start(bf16[90,1,256]{2,1,0:T(2,128)(2,1)S(1)} %get-tuple-element.94), channel_id=1, source_target_pairs={{1,0},{2,1},{3,2},{4,3},{5,4},{6,5},{7,6},{0,7},{9,8},{10,9},{11,1... | collective-permute-start | bytes 138248 | tf_op jit(solution)/shard_map/ppermute | solution.py:20
  302.3 23.9 %collective-permute-start.3 = (bf16[1,92,256]{2,1,0:T(8,128)(2,1)S(1)}, bf16[1,92,256]{2,1,0:T(8,128)(2,1)S(1)}, u32[]{:S(2)}, u32[]{:S(2)}) collective-permute-start(bf16[1,92,256]{2,1,0:T(8,128)(2,1)S(1)} %get-tuple-element.73), channel_id=1, source_target_pairs={{0,8},{8,16},{16,24},{1,9},{9,17},{17,25},{2,10},{10,18},{18,26},{... | collective-permute-start | bytes 141320 | tf_op jit(solution)/shard_map/ppermute | solution.py:18
  303.8 22.3 %collective-permute-start.4 = (bf16[1,92,256]{2,1,0:T(8,128)(2,1)S(1)}, bf16[1,92,256]{2,1,0:T(8,128)(2,1)S(1)}, u32[]{:S(2)}, u32[]{:S(2)}) collective-permute-start(bf16[1,92,256]{2,1,0:T(8,128)(2,1)S(1)} %get-tuple-element.74), channel_id=1, source_target_pairs={{8,0},{16,8},{24,16},{9,1},{17,9},{25,17},{10,2},{18,10},{26,18},{... | collective-permute-start | bytes 141320 | tf_op jit(solution)/shard_map/ppermute | solution.py:20
  305.1 21.0 %collective-permute-start.2 = (bf16[2,92,256]{2,1,0:T(8,128)(2,1)S(1)}, bf16[2,92,256]{2,1,0:T(8,128)(2,1)S(1)}, u32[]{:S(2)}, u32[]{:S(2)}) collective-permute-start(bf16[2,92,256]{2,1,0:T(8,128)(2,1)S(1)} %pad_maximum_fusion.6), channel_id=1, source_target_pairs={{0,4},{1,5},{2,6},{3,7},{4,0},{5,1},{6,2},{7,3},{8,12},{9,13},{10,... | collective-permute-start | bytes 282632 | tf_op jit(solution)/shard_map/ppermute | solution.py:30
  402.7 8.6 %slice-start.2 = ((s8[8298496]{0:T(1024)(128)(4,1)}), s8[4194304]{0:T(1024)(128)(4,1)S(1)}, s32[]{:S(2)}) async-start(s8[8298496]{0:T(1024)(128)(4,1)} %bitcast.143), calls=%async_computation.4 | async-start | bytes 8388608
  414.8 6.6 %copy-start.5 = (bf16[8100,256]{1,0:T(8,128)(2,1)S(1)}, bf16[8100,256]{1,0:T(8,128)(2,1)}, u32[]{:S(2)}) copy-start(bf16[8100,256]{1,0:T(8,128)(2,1)} %reshape.136) | copy-start | bytes 12441604
  438.8 8.9 %copy-start.3 = (f32[8100,256]{1,0:T(8,128)S(1)}, f32[8100,256]{1,0:T(8,128)}, u32[]{:S(2)}) copy-start(f32[8100,256]{1,0:T(8,128)} %convolution_add_fusion.7) | copy-start | bytes 24883204
  443.9 16.9 %copy-start.2 = (bf16[90,90,256]{2,1,0:T(8,128)(2,1)}, bf16[90,90,256]{2,1,0:T(8,128)(2,1)S(1)}, u32[]{:S(2)}) copy-start(bf16[90,90,256]{2,1,0:T(8,128)(2,1)S(1)} %fusion.25) | copy-start | bytes 12441604
  444.1 9.3 %collective-permute-start.5 = (bf16[90,1,256]{2,1,0:T(2,128)(2,1)S(1)}, bf16[90,1,256]{2,1,0:T(2,128)(2,1)S(1)}, u32[]{:S(2)}, u32[]{:S(2)}) collective-permute-start(bf16[90,1,256]{2,1,0:T(2,128)(2,1)S(1)} %get-tuple-element.89), channel_id=1, source_target_pairs={{0,1},{1,2},{2,3},{3,4},{4,5},{5,6},{6,7},{7,0},{8,9},{9,10},{10,1... | collective-permute-start | bytes 138248 | tf_op jit(solution)/shard_map/ppermute | solution.py:18
  444.1 9.3 %collective-permute-start.6 = (bf16[90,1,256]{2,1,0:T(2,128)(2,1)S(1)}, bf16[90,1,256]{2,1,0:T(2,128)(2,1)S(1)}, u32[]{:S(2)}, u32[]{:S(2)}) collective-permute-start(bf16[90,1,256]{2,1,0:T(2,128)(2,1)S(1)} %get-tuple-element.90), channel_id=1, source_target_pairs={{1,0},{2,1},{3,2},{4,3},{5,4},{6,5},{7,6},{0,7},{9,8},{10,9},{11,1... | collective-permute-start | bytes 138248 | tf_op jit(solution)/shard_map/ppermute | solution.py:20
  453.5 28.4 %collective-permute-start.8 = (bf16[1,92,256]{2,1,0:T(8,128)(2,1)S(1)}, bf16[1,92,256]{2,1,0:T(8,128)(2,1)S(1)}, u32[]{:S(2)}, u32[]{:S(2)}) collective-permute-start(bf16[1,92,256]{2,1,0:T(8,128)(2,1)S(1)} %get-tuple-element.69), channel_id=1, source_target_pairs={{0,8},{8,16},{16,24},{1,9},{9,17},{17,25},{2,10},{10,18},{18,26},{... | collective-permute-start | bytes 141320 | tf_op jit(solution)/shard_map/ppermute | solution.py:18
  458.4 23.5 %collective-permute-start.9 = (bf16[1,92,256]{2,1,0:T(8,128)(2,1)S(1)}, bf16[1,92,256]{2,1,0:T(8,128)(2,1)S(1)}, u32[]{:S(2)}, u32[]{:S(2)}) collective-permute-start(bf16[1,92,256]{2,1,0:T(8,128)(2,1)S(1)} %get-tuple-element.70), channel_id=1, source_target_pairs={{8,0},{16,8},{24,16},{9,1},{17,9},{25,17},{10,2},{18,10},{26,18},{... | collective-permute-start | bytes 141320 | tf_op jit(solution)/shard_map/ppermute | solution.py:20
  459.7 22.2 %collective-permute-start.7 = (bf16[2,92,256]{2,1,0:T(8,128)(2,1)S(1)}, bf16[2,92,256]{2,1,0:T(8,128)(2,1)S(1)}, u32[]{:S(2)}, u32[]{:S(2)}) collective-permute-start(bf16[2,92,256]{2,1,0:T(8,128)(2,1)S(1)} %pad_maximum_fusion.7), channel_id=1, source_target_pairs={{0,4},{1,5},{2,6},{3,7},{4,0},{5,1},{6,2},{7,3},{8,12},{9,13},{10,... | collective-permute-start | bytes 282632 | tf_op jit(solution)/shard_map/ppermute | solution.py:30
  574.0 8.6 %slice-start.4 = ((s8[8298496]{0:T(1024)(128)(4,1)}), s8[4194304]{0:T(1024)(128)(4,1)S(1)}, s32[]{:S(2)}) async-start(s8[8298496]{0:T(1024)(128)(4,1)} %bitcast.145), calls=%async_computation.6 | async-start | bytes 8388608
  576.5 6.1 slice-start.5
  605.1 8.5 %copy-start.1 = (bf16[256,256]{1,0:T(8,128)(2,1)S(1)}, bf16[256,256]{1,0:T(8,128)(2,1)}, u32[]{:S(2)}) copy-start(bf16[256,256]{1,0:T(8,128)(2,1)} %param.20) | copy-start | bytes 393220
  (5 other events, 20.6 us)
where the time goes:
time: 624 us; the launch traced here: 614 us
  local copies, waits for them, and re-layouts  208 us (33%)
  matrix products  194 us (31%)
  other arithmetic  158 us (25%)
  starting transfers between devices  30.8 us (5%)
  waiting for transfers between devices  20.6 us (3%)
    reshape x16, local copies, waits for them, and re-layouts, convolve(): padded[row_off:row_off + lat_rows, col_off:col_off + lon_cols]  111 us
    dot_general x18, matrix products, convolve(): jnp.dot(window, weights[row_off, col_off], preferred_element_type=jnp.flo...  93 us
    reduce_sum x16, other arithmetic, one_block(): block_dens = jnp.sum(spread.astype(jnp.float32), axis=1)  85.8 us
    dot_general x16, matrix products, one_block(): block_sums = jnp.dot(spread, got_feat, preferred_element_type=jnp.float32)  83.8 us
    slice x3, local copies, waits for them, and re-layouts, convolve(): padded[row_off:row_off + lat_rows, col_off:col_off + lon_cols]  31.9 us
    concatenate x2, other arithmetic, extend(): return jnp.concatenate([top[None], tall[1:-1], bottom[None]], axis=0)  20.8 us
    all_to_all x1, waiting for transfers between devices, shards(): lax.all_to_all(send_feat.reshape(devices, capacity, nfeat), ('lat', 'lon'...  20.6 us
    reshape x2, local copies, waits for them, and re-layouts, convolve(): return total.reshape(lat_rows, lon_cols, chans)  19 us
  transfers between devices with their start and end apart: 12, of which 1 were waited for; matrix products, arithmetic and copies ran while one was open for 12% of the time, Pallas kernels for 0%

commit v1 on v0

v1 whole, which is shorter than its diff:
```python
import functools

import jax
import jax.numpy as jnp
from jax import lax
from jax.experimental import pallas as pl
from jax.experimental.pallas import tpu as pltpu
from jax.sharding import PartitionSpec as P

KCELL = 4
GBINS = 32
META = 16
GROUP = 6
CHUNK = 256
BF = jnp.bfloat16
F32 = jnp.float32


def params(mib):
    return pltpu.CompilerParams(vmem_limit_bytes=mib * 1024 * 1024)


def dot(a, b):
    return jnp.dot(a, b, preferred_element_type=F32)


def pack_kernel(devices, cap, cols, count_ref, dest_ref, cells_ref, gauss_ref, feat_ref, send_ref, ext_ref):
    nrows, nfeat = feat_ref.shape
    step = 256
    dest = dest_ref[...]
    row_id = lax.broadcasted_iota(jnp.int32, (1, nrows), 1)
    dest = jnp.where(row_id < count_ref[0], dest, devices)
    earlier = (
        lax.broadcasted_iota(jnp.int32, (step, step), 0) < lax.broadcasted_iota(jnp.int32, (step, step), 1)
    ).astype(F32).astype(BF)
    tile_id = lax.broadcasted_iota(jnp.int32, (devices, step), 0)
    carry = jnp.zeros((devices, 1), F32)
    ranks = []
    for begin in range(0, nrows, step):
        hot = (tile_id == dest[:, begin : begin + step]).astype(F32)
        before = dot(hot.astype(BF), earlier) + carry
        ranks.append(jnp.sum(before * hot, axis=0, keepdims=True))
        carry = carry + jnp.sum(hot, axis=1, keepdims=True)
    rank = jnp.concatenate(ranks, axis=1)
    base = cells_ref[0:1, :]
    lat = jnp.floor((base.astype(F32) + 0.5) * (1.0 / cols))
    lon = base.astype(F32) - lat * cols
    ratio = gauss_ref[...].astype(F32) * (1.0 / GBINS)
    weight = jnp.exp(-3.0 * ratio * ratio)
    meta = jnp.concatenate([lat, lon, weight, jnp.zeros((nfeat - 2 - KCELL, nrows), F32)], axis=0)
    ext_ref[:, :nfeat] = feat_ref[...]
    ext_ref[:, nfeat:] = meta.T.astype(BF)
    slot = lax.broadcasted_iota(jnp.int32, (cap, nrows), 0).astype(F32)

    def one(d, _):
        key = jnp.where(dest == d, rank, -1.0)
        pick = (slot == key).astype(F32).astype(BF)
        got = dot(pick, ext_ref[...])
        send_ref[d, 0:cap, :] = got[:, :nfeat].astype(BF)
        side = got[:, nfeat:]
        if cap < nfeat:
            side = jnp.concatenate([side, jnp.zeros((nfeat - cap, nfeat), F32)], axis=0)
        send_ref[d, cap : cap + META, :] = side.T[0:META].astype(BF)
        return 0

    lax.fori_loop(0, devices, one, 0)


def pack(count, dest, cells, gauss, feats, devices, cap, cols):
    nrows, nfeat = feats.shape
    return pl.pallas_call(
        functools.partial(pack_kernel, devices, cap, cols),
        out_shape=jax.ShapeDtypeStruct((devices, cap + META, nfeat), BF),
        in_specs=[pl.BlockSpec(memory_space=pltpu.SMEM)] + [pl.BlockSpec(memory_space=pltpu.VMEM)] * 4,
        out_specs=pl.BlockSpec(memory_space=pltpu.VMEM),
        scratch_shapes=[pltpu.VMEM((nrows, 2 * nfeat), BF)],
        compiler_params=params(48),
    )(count, dest, cells, gauss, feats)


def grid_kernel(
    devices, cap, wide, recv_ref, back_ref, w_in_ref, w_bg_ref, w_dens_ref, first_ref, edge_ref,
    feat_ref, meta_ref, acc_ref, back_scr, edge_scr, count_ref,
):
    group = pl.program_id(0)
    nfeat = recv_ref.shape[2]
    rows, cols, chans = back_ref.shape
    tiles = meta_ref.shape[0]

    @pl.when(group == 0)
    def _():
        meta_ref[...] = jnp.zeros(meta_ref.shape, F32)
        feat_ref[:, nfeat:] = jnp.ones((feat_ref.shape[0], nfeat), BF)
        lane = lax.broadcasted_iota(jnp.int32, (8, nfeat), 1)

        def count(s, _):
            side = recv_ref[s, cap : cap + META, :].astype(F32)
            count_ref[s] = jnp.sum((side[2:3] > 0).astype(jnp.int32))
            return 0

        lax.fori_loop(0, devices, count, 0, unroll=devices <= 32)

        def compact(s, begin):
            begin = pl.multiple_of(begin, 16)
            feat_ref[pl.ds(begin, cap), 0:nfeat] = recv_ref[s, 0:cap, :]
            side = recv_ref[s, cap : cap + META, :].astype(F32)[0:8]
            tile, shift = begin // nfeat, begin % nfeat
            moved = pltpu.roll(side, shift, axis=1)
            meta_ref[tile] = jnp.where(lane >= shift, moved, meta_ref[tile])
            meta_ref[tile + 1] = jnp.where(lane < shift, moved, 0.0)
            return begin + (count_ref[s] + 15) // 16 * 16

        total = lax.fori_loop(0, devices, compact, 0)
        last = pl.multiple_of(total, 16)
        feat_ref[pl.ds(last, CHUNK), 0:nfeat] = jnp.zeros((CHUNK, nfeat), BF)
        count_ref[devices] = (total + CHUNK - 1) // CHUNK

    acc_ref[...] = jnp.zeros(acc_ref.shape, F32)
    col_id = lax.broadcasted_iota(jnp.int32, (wide, CHUNK), 0).astype(F32)

    def chunk(k, _):
        side = jnp.concatenate([meta_ref[k * (CHUNK // nfeat) + q] for q in range(CHUNK // nfeat)], axis=1)
        lat, lon = side[0:1], side[1:2]
        here = (col_id == lon + 2.0).astype(F32).astype(BF)
        after = (col_id == lon + 3.0).astype(F32).astype(BF)
        parts = []
        for i in range(rows):
            row = (group * rows + i).astype(F32)
            same, above = lat == row, lat == row - 1.0
            left = jnp.where(same, side[2:3], jnp.where(above, side[4:5], 0.0)).astype(BF)
            right = jnp.where(same, side[3:4], jnp.where(above, side[5:6], 0.0)).astype(BF)
            parts.append(here * left + after * right)
        spread = jnp.concatenate(parts, axis=0)
        begin = pl.multiple_of(k * CHUNK, CHUNK)
        acc_ref[...] += dot(spread, feat_ref[pl.ds(begin, CHUNK), :])
        return 0

    lax.fori_loop(0, count_ref[devices], chunk, 0)
    for i in range(rows):
        back_scr[i * wide : i * wide + cols, :] = back_ref[i]
    start = pltpu.roll(dot(back_scr[...], w_bg_ref[...]), 2, axis=0)
    density = acc_ref[:, nfeat:]
    normalized = (acc_ref[:, :nfeat] / (density + 1.0)).astype(BF)
    start = start + dot(normalized, w_in_ref[...])
    start = start + jnp.concatenate([density] * (chans // nfeat), axis=1) * w_dens_ref[...]
    first = start.astype(BF)
    for i in range(rows):
        first_ref[i] = first[i * wide : (i + 1) * wide]
        for k, col in enumerate((2, 3, cols, cols + 1)):
            edge_scr[k, pl.ds(group * rows + i, 1), :] = start[i * wide + col : i * wide + col + 1]

    @pl.when(group == pl.num_programs(0) - 1)
    def _():
        edge_ref[...] = edge_scr[...].astype(BF)


def gridded(recv, background, w_in, w_bg, w_dens, cap, wide):
    devices, _, nfeat = recv.shape
    lat_rows, cols, chans = background.shape
    slots = devices * cap
    tall = -(-lat_rows // 16) * 16
    whole = pl.BlockSpec(memory_space=pltpu.VMEM)
    return pl.pallas_call(
        functools.partial(grid_kernel, devices, cap, wide),
        grid=(lat_rows // GROUP,),
        out_shape=(
            jax.ShapeDtypeStruct((lat_rows, wide, chans), BF),
            jax.ShapeDtypeStruct((4, tall, chans), BF),
        ),
        in_specs=[
            whole,
            pl.BlockSpec((GROUP, cols, chans), lambda g: (g, 0, 0)),
            whole,
            whole,
            whole,
        ],
        out_specs=(
            pl.BlockSpec((GROUP, wide, chans), lambda g: (g, 0, 0)),
            pl.BlockSpec((4, tall, chans), lambda g: (0, 0, 0)),
        ),
        scratch_shapes=[
            pltpu.VMEM((slots + 2 * CHUNK, 2 * nfeat), BF),
            pltpu.VMEM((slots // nfeat + 4, 8, nfeat), F32),
            pltpu.VMEM((GROUP * wide, 2 * nfeat), F32),
            pltpu.VMEM((GROUP * wide, chans), BF),
            pltpu.VMEM((4, tall, chans), F32),
            pltpu.SMEM((devices + 1,), jnp.int32),
        ],
        compiler_params=params(48),
    )(recv, background, w_in, w_bg, w_dens)


def three(value):
    size = value.shape[0]
    return [value.astype(BF), pltpu.roll(value, size - 1, axis=0).astype(BF), pltpu.roll(value, size - 2, axis=0).astype(BF)]


def conv_kernel(
    pole_ref, first_ref, west_ref, east_ref, north_ref, south_ref, one_ref, two_ref, out_ref,
    wide_in, wide_hid, cols_scr,
):
    group = pl.program_id(0)
    lat_rows, wide, chans = first_ref.shape
    rows, cols, _ = out_ref.shape
    block = rows * wide

    def put(ref, begin, size, value):
        for b, part in enumerate(three(value)):
            ref[pl.ds(begin, size), b * chans : (b + 1) * chans] = part

    @pl.when(group == 0)
    def _():
        cols_scr[0:2] = west_ref[...].astype(F32)
        cols_scr[2:4] = east_ref[...].astype(F32)
        row_id = lax.broadcasted_iota(jnp.int32, (wide, chans), 0)

        def load(r, _):
            value = first_ref[r].astype(F32)
            for k, col in enumerate((0, 1, cols + 2, cols + 3)):
                value = jnp.where(row_id == col, cols_scr[k, pl.ds(r, 1), :], value)
            put(wide_in, pl.multiple_of((r + 2) * wide, 16), wide, value)
            return 0

        lax.fori_loop(0, lat_rows, load, 0)
        put(wide_in, wide, wide, north_ref[0].astype(F32))
        put(wide_in, 0, wide, north_ref[1].astype(F32))
        put(wide_in, (lat_rows + 2) * wide, wide, south_ref[0].astype(F32))
        put(wide_in, (lat_rows + 3) * wide, wide, south_ref[1].astype(F32))
        for side, begin in ((0, 0), (1, lat_rows + 1)):
            total = jnp.zeros((wide, chans), F32)
            for a in range(3):
                pick = jnp.where(pole_ref[side] == 1, 2 - a, a)
                total = total + dot(wide_in[(begin + a) * wide : (begin + a + 1) * wide, :], one_ref[pick])
            put(wide_hid, begin * wide, wide, jax.nn.gelu(total))

        def hidden(g, _):
            begin = pl.multiple_of((g * rows + 1) * wide, 16)
            total = dot(wide_in[pl.ds(begin, block), :], one_ref[0])
            total = total + dot(wide_in[pl.ds(begin + wide, block), :], one_ref[1])
            total = total + dot(wide_in[pl.ds(begin + 2 * wide, block), :], one_ref[2])
            put(wide_hid, begin, block, jax.nn.gelu(total))
            return 0

        lax.fori_loop(0, lat_rows // rows, hidden, 0)

    begin = pl.multiple_of(group * block, 16)
    total = wide_in[pl.ds(begin + 2 * wide, block), 2 * chans :].astype(F32)
    total = total + dot(wide_hid[pl.ds(begin, block), :], two_ref[0])
    total = total + dot(wide_hid[pl.ds(begin + wide, block), :], two_ref[1])
    total = total + dot(wide_hid[pl.ds(begin + 2 * wide, block), :], two_ref[2])
    result = total.astype(BF)
    for i in range(rows):
        out_ref[i] = result[i * wide : i * wide + cols]


def convolved(poles, first, west, east, north, south, one, two, cols):
    lat_rows, wide, chans = first.shape
    whole = pl.BlockSpec(memory_space=pltpu.VMEM)
    return pl.pallas_call(
        conv_kernel,
        grid=(lat_rows // GROUP,),
        out_shape=jax.ShapeDtypeStruct((lat_rows, cols, chans), BF),
        in_specs=[pl.BlockSpec(memory_space=pltpu.SMEM)] + [whole] * 7,
        out_specs=pl.BlockSpec((GROUP, cols, chans), lambda g: (g, 0, 0)),
        scratch_shapes=[
            pltpu.VMEM(((lat_rows + 4) * wide, 3 * chans), BF),
            pltpu.VMEM(((lat_rows + 2) * wide, 3 * chans), BF),
            pltpu.VMEM((4, west.shape[1], chans), F32),
        ],
        compiler_params=params(60),
    )(poles, first, west, east, north, south, one, two)


def row_pairs(lat_count, lon_count):
    half = lon_count // 2

    def flat(lat, lon):
        return lat * lon_count + lon % lon_count

    inner, outer = [], []
    for lon in range(lon_count):
        for lat in range(0, lat_count, 2):
            inner += [(flat(lat, lon), flat(lat + 1, lon)), (flat(lat + 1, lon), flat(lat, lon))]
        for lat in range(1, lat_count - 1, 2):
            outer += [(flat(lat, lon), flat(lat + 1, lon)), (flat(lat + 1, lon), flat(lat, lon))]
        outer += [(flat(lat, lon), flat(lat, lon + half)) for lat in (0, lat_count - 1)]
    return inner, outer


def shards(
    obs_features,
    obs_dest,
    obs_cells,
    obs_gauss,
    row_counts,
    background,
    w_in,
    w_bg,
    w_dens,
    conv_one,
    conv_two,
):
    nrows, nfeat = obs_features.shape
    lat_rows, cols, chans = background.shape
    axes = ("lat", "lon")
    devices = lax.axis_size(axes)
    lat_count, lon_count = lax.axis_size("lat"), lax.axis_size("lon")
    cap = 2 * nrows // devices
    wide = -(-(cols + 4) // 16) * 16
    send = pack(
        row_counts, obs_dest.reshape(1, nrows), obs_cells.T, obs_gauss.T, obs_features, devices, cap, cols
    )
    recv = lax.all_to_all(send, axes, split_axis=0, concat_axis=0, tiled=True)
    first, edges = gridded(recv, background, w_in, w_bg, w_dens.reshape(1, chans), cap, wide)
    west = lax.ppermute(edges[2:4], "lon", [(i, (i + 1) % lon_count) for i in range(lon_count)])
    east = lax.ppermute(edges[0:2], "lon", [((i + 1) % lon_count, i) for i in range(lon_count)])
    lat_index = lax.axis_index("lat")
    even = lat_index % 2 == 0

    def rows_at(near, far):
        body = jnp.stack([first[near], first[far]])[:, 2 : cols + 2]
        left = jnp.stack([west[:, near], west[:, far]])
        right = jnp.stack([east[:, near], east[:, far]])
        fill = jnp.zeros((2, wide - cols - 4, chans), BF)
        return jnp.concatenate([left, body, right, fill], axis=1)

    top, bottom = rows_at(0, 1), rows_at(lat_rows - 1, lat_rows - 2)
    inner, outer = row_pairs(lat_count, lon_count)
    by_inner = lax.ppermute(jnp.where(even, bottom, top), axes, inner)
    by_outer = lax.ppermute(jnp.where(even, top, bottom), axes, outer)
    north = jnp.where(even, by_outer, by_inner)
    south = jnp.where(even, by_inner, by_outer)
    poles = jnp.stack([lat_index == 0, lat_index == lat_count - 1]).astype(jnp.int32)
    return convolved(
        poles,
        first,
        west,
        east,
        north,
        south,
        conv_one.reshape(3, 3 * chans, chans),
        conv_two.reshape(3, 3 * chans, chans),
        cols,
    )


def solution(mesh):
    rows = P(("lat", "lon"), None)
    in_specs = (rows, rows, rows, rows, P(("lat", "lon")), P("lat", "lon", None), P(), P(), P(), P(), P())
    return jax.shard_map(
        shards, mesh=mesh, in_specs=in_specs, out_specs=P("lat", "lon", None), check_vma=False
    )
```

time: 624 us -> 155 us (0.25); the launches traced: 614 us -> 155 us
  local copies, waits for them, and re-layouts: 208 us -> 7.38 us
  matrix products: 194 us -> 0 us
  other arithmetic: 158 us -> 1.55 us
  Pallas kernels: 0 us -> 87 us
  waiting for transfers between devices: 20.6 us -> 38.3 us
  starting transfers between devices: 30.8 us -> 20 us
    dot_general x36 -> x0, matrix products: 194 us -> none  [the longest x18 93 us: convolve(): jnp.dot(window, weights[row_off, col_off], preferred_element_type=jnp.flo...]
    reshape x21 -> x0, local copies, waits for them, and re-layouts: 145 us -> none  [the longest x16 111 us: convolve(): padded[row_off:row_off + lat_rows, col_off:col_off + lon_cols]]
    pallas_call x0 -> x3, Pallas kernels: none -> 87 us  [the longest x1 39.1 us: gridded(): pl.pallas_call(functools.partial(grid_kernel, devices, cap, wide), grid=(...]
    reduce_sum x17 -> x0, other arithmetic: 86.6 us -> none  [the longest x16 85.8 us: one_block(): block_dens = jnp.sum(spread.astype(jnp.float32), axis=1)]
    slice x39 -> x3, local copies, waits for them, and re-layouts: 37.2 us -> 0.17 us  [the longest x1 0.14 us: shards(): edges[0:2]]
    concatenate x7 -> x0, other arithmetic: 35.9 us -> none  [the longest x2 20.8 us: extend(): return jnp.concatenate([top[None], tall[1:-1], bottom[None]], axis=0)]
    convert_element_type x6 -> x1, other arithmetic: 14.5 us -> 0.65 us  [shards(): jnp.stack([lat_index == 0, lat_index == lat_count - 1]).astype(jnp.int32)]
    scatter x2 -> x0, local copies, waits for them, and re-layouts: 13.3 us -> none  [the longest x1 7.23 us: shards(): jnp.zeros((devices * capacity, nfeat), jnp.bfloat16).at[position]]
  transfers between devices with their start and end apart: 12 -> 5, of which waited for: 1 -> 4; matrix products, arithmetic and copies ran while one was open for 12% -> 1% of each run, Pallas kernels for 0% -> 0%
where the time goes in v1:
time: 155 us
  Pallas kernels  87 us (56%)
  waiting for transfers between devices  38.3 us (25%)
  starting transfers between devices  20 us (13%)
  local copies, waits for them, and re-layouts  7.38 us (5%)
  other arithmetic  1.55 us (1%)
    pallas_call x1, Pallas kernels, gridded(): pl.pallas_call(functools.partial(grid_kernel, devices, cap, wide), grid=(...  39.1 us
    pallas_call x1, Pallas kernels, convolved(): pl.pallas_call(conv_kernel, grid=(lat_rows // GROUP,), out_shape=jax.Shap...  35.2 us
    all_to_all x1, waiting for transfers between devices, shards(): recv = lax.all_to_all(send, axes, split_axis=0, concat_axis=0, tiled=True)  30.3 us
    pallas_call x1, Pallas kernels, pack(): pl.pallas_call(functools.partial(pack_kernel, devices, cap, cols), out_sh...  12.6 us
    ppermute x1, starting transfers between devices, shards(): lax.ppermute(edges[0:2], 'lon', [((i + 1) % lon_count, i) for i in range(...  10.8 us
    all_to_all x1, starting transfers between devices, shards(): recv = lax.all_to_all(send, axes, split_axis=0, concat_axis=0, tiled=True)  7.3 us
    unnamed x16, local copies, waits for them, and re-layouts  5.67 us
    ppermute x1, waiting for transfers between devices, shards(): by_outer = lax.ppermute(jnp.where(even, top, bottom), axes, outer)  3.78 us
  transfers between devices with their start and end apart: 5, of which 4 were waited for; matrix products, arithmetic and copies ran while one was open for 1% of the time, Pallas kernels for 0%

profile of v1, /device:TPU:0, one launch (start us, length us, event | category | flops | bytes accessed | tf_op | source)
XLA Modules:
  0.0 154.9 jit_solution(325617075296358539)
XLA Ops:
  0.7 1.0 copy-done.1
  1.7 0.8 copy-done.4
  2.5 0.8 copy-done.5
  3.2 0.7 copy-done.6
  3.9 12.6 %shard_map.109 = bf16[32,144,128]{2,1,0:T(8,128)(2,1)} custom-call(s32[1]{0:T(128)S(6)} %copy.16.count_ref, s32[1,2048]{1,0:T(1,128)S(1)} %bitcast.26, s32[4,2048]{1,0:T(4,128)S(1)} %bitcast.24, s32[4,2048]{1,0:T(4,128)S(1)} %bitcast.25, bf16[2048,128]{1,0:T(8,128)(2,1)S(1)} %copy-done.1), custom_call_target="tpu_custom_call" | custom-call | tf_op jit(solution)/shard_map/pallas_call | solution.py:71
  16.5 7.3 %all-to-all-start = ((bf16[32,144,128]{2,1,0:T(8,128)(2,1)}), bf16[32,144,128]{2,1,0:T(8,128)(2,1)S(1)}, u32[]{:S(2)}, u32[]{:S(2)}) async-start(bf16[32,144,128]{2,1,0:T(8,128)(2,1)} %shard_map.109), calls=%async_computation | async-start | bytes 2359296 | tf_op jit(solution)/shard_map/all_to_all | solution.py:313
  23.9 30.3 %all-to-all-done.recv_ref = bf16[32,144,128]{2,1,0:T(8,128)(2,1)S(1)} async-done(((bf16[32,144,128]{2,1,0:T(8,128)(2,1)}), bf16[32,144,128]{2,1,0:T(8,128)(2,1)S(1)}, u32[]{:S(2)}, u32[]{:S(2)}) %all-to-all-start) | async-done | bytes 1179680 | tf_op jit(solution)/shard_map/all_to_all | solution.py:313
  54.2 0.9 copy-done.2
  55.1 0.8 copy-done.3
  56.0 0.7 copy-done.7
  56.7 39.1 %shard_map.110 = (bf16[90,96,256]{2,1,0:T(8,128)(2,1)S(1)}, bf16[4,96,256]{2,1,0:T(8,128)(2,1)S(1)}) custom-call(bf16[32,144,128]{2,1,0:T(8,128)(2,1)S(1)} %all-to-all-done.recv_ref, bf16[90,90,256]{2,1,0:T(8,128)(2,1)} %back_ref.1, bf16[128,256]{1,0:T(8,128)(2,1)S(1)} %copy-done.3, bf16[256,256]{1,0:T(8,128)(2,1)S(1)} %copy-done.2, f32[1,256]{1,0:T(1,128)S(1)} %bitcast.27), custom_call_target="tpu_custom_call" | custom-call | tf_op jit(solution)/shard_map/pallas_call | solution.py:163
  95.8 0.2 copy.12
  96.0 0.1 fusion.8
  96.1 10.8 %collective-permute-start.1 = (bf16[2,96,256]{2,0,1:T(2,128)(2,1)S(1)}, bf16[2,96,256]{2,0,1:T(2,128)(2,1)S(1)}, u32[]{:S(2)}, u32[]{:S(2)}) collective-permute-start(bf16[2,96,256]{2,0,1:T(2,128)(2,1)S(1)} %get-tuple-element.13), channel_id=1, source_target_pairs={{1,0},{2,1},{3,2},{4,3},{5,4},{6,5},{7,6},{0,7},{9,8},{10,9},{11,1... | collective-permute-start | bytes 294920 | tf_op jit(solution)/shard_map/ppermute | solution.py:316
  107.0 1.7 %collective-permute-start = (bf16[2,96,256]{2,0,1:T(2,128)(2,1)S(1)}, bf16[2,96,256]{2,0,1:T(2,128)(2,1)S(1)}, u32[]{:S(2)}, u32[]{:S(2)}) collective-permute-start(bf16[2,96,256]{2,0,1:T(2,128)(2,1)S(1)} %get-tuple-element.14), channel_id=1, source_target_pairs={{0,1},{1,2},{2,3},{3,4},{4,5},{5,6},{6,7},{7,0},{8,9},{9,10},{10,1... | collective-permute-start | bytes 294920 | tf_op jit(solution)/shard_map/ppermute | solution.py:315
  108.7 0.5 collective-permute-done.1
  109.2 3.7 %collective-permute-done = bf16[2,96,256]{2,0,1:T(2,128)(2,1)S(1)} collective-permute-done((bf16[2,96,256]{2,0,1:T(2,128)(2,1)S(1)}, bf16[2,96,256]{2,0,1:T(2,128)(2,1)S(1)}, u32[]{:S(2)}, u32[]{:S(2)}) %collective-permute-start) | collective-permute-done | bytes 98336 | tf_op jit(solution)/shard_map/ppermute | solution.py:315
  113.0 0.1 broadcast_select_fusion.3
  113.3 0.7 add_convert_fusion.pole_ref
  113.9 0.6 copy.15.east_ref
  114.6 0.6 copy.14.west_ref
  115.2 3.8 %collective-permute-done.2 = bf16[2,96,256]{2,1,0:T(8,128)(2,1)S(1)} collective-permute-done((bf16[2,96,256]{2,1,0:T(8,128)(2,1)S(1)}, bf16[2,96,256]{2,1,0:T(8,128)(2,1)S(1)}, u32[]{:S(2)}, u32[]{:S(2)}) %collective-permute-start.2) | collective-permute-done | bytes 98336 | tf_op jit(solution)/shard_map/ppermute | solution.py:330
  119.0 0.7 broadcast_select_fusion
  119.7 35.2 %shard_map.111 = bf16[90,90,256]{2,1,0:T(8,128)(2,1)} custom-call(s32[2]{0:T(128)} %add_convert_fusion.pole_ref, bf16[90,96,256]{2,1,0:T(8,128)(2,1)} %copy-done, bf16[2,96,256]{2,1,0:T(8,128)(2,1)} %copy.14.west_ref, bf16[2,96,256]{2,1,0:T(8,128)(2,1)} %copy.15.east_ref, bf16[2,96,256]{2,1,0:T(8,128)(2,1)} %get-tuple-element.12.north_ref, ...), custom_call_target="tpu_custom_call" | custom-call | tf_op jit(solution)/shard_map/pallas_call | solution.py:259
  (19 shorter events, 0.4 us)
Async XLA Ops:
  0.7 1.0 copy-start.1
  1.7 0.8 copy-start.4
  2.5 0.8 copy-start.5
  3.2 0.7 copy-start.6
  16.5 37.7 %all-to-all-start = ((bf16[32,144,128]{2,1,0:T(8,128)(2,1)}), bf16[32,144,128]{2,1,0:T(8,128)(2,1)S(1)}, u32[]{:S(2)}, u32[]{:S(2)}) async-start(bf16[32,144,128]{2,1,0:T(8,128)(2,1)} %shard_map.109), calls=%async_computation | async-start | bytes 2359296 | tf_op jit(solution)/shard_map/all_to_all | solution.py:313
  54.2 0.9 copy-start.2
  55.1 0.8 copy-start.3
  56.0 0.7 copy-start.7
  95.8 11.2 %copy-start = (bf16[90,96,256]{2,1,0:T(8,128)(2,1)}, bf16[90,96,256]{2,1,0:T(8,128)(2,1)S(1)}, u32[]{:S(2)}) copy-start(bf16[90,96,256]{2,1,0:T(8,128)(2,1)S(1)} %get-tuple-element.7.first_ref) | copy-start | bytes 13271044
  96.1 13.1 %collective-permute-start.1 = (bf16[2,96,256]{2,0,1:T(2,128)(2,1)S(1)}, bf16[2,96,256]{2,0,1:T(2,128)(2,1)S(1)}, u32[]{:S(2)}, u32[]{:S(2)}) collective-permute-start(bf16[2,96,256]{2,0,1:T(2,128)(2,1)S(1)} %get-tuple-element.13), channel_id=1, source_target_pairs={{1,0},{2,1},{3,2},{4,3},{5,4},{6,5},{7,6},{0,7},{9,8},{10,9},{11,1... | collective-permute-start | bytes 294920 | tf_op jit(solution)/shard_map/ppermute | solution.py:316
  107.0 5.9 %collective-permute-start = (bf16[2,96,256]{2,0,1:T(2,128)(2,1)S(1)}, bf16[2,96,256]{2,0,1:T(2,128)(2,1)S(1)}, u32[]{:S(2)}, u32[]{:S(2)}) collective-permute-start(bf16[2,96,256]{2,0,1:T(2,128)(2,1)S(1)} %get-tuple-element.14), channel_id=1, source_target_pairs={{0,1},{1,2},{2,3},{3,4},{4,5},{5,6},{6,7},{7,0},{8,9},{9,10},{10,1... | collective-permute-start | bytes 294920 | tf_op jit(solution)/shard_map/ppermute | solution.py:315
  113.1 5.9 %collective-permute-start.2 = (bf16[2,96,256]{2,1,0:T(8,128)(2,1)S(1)}, bf16[2,96,256]{2,1,0:T(8,128)(2,1)S(1)}, u32[]{:S(2)}, u32[]{:S(2)}) collective-permute-start(bf16[2,96,256]{2,1,0:T(8,128)(2,1)S(1)} %broadcast_select_fusion.3), channel_id=1, source_target_pairs={{8,16},{16,8},{0,4},{24,28},{9,17},{17,9},{1,5},{25,29},{10,18},{1... | collective-permute-start | bytes 294920 | tf_op jit(solution)/shard_map/ppermute | solution.py:330
  113.2 5.8 %collective-permute-start.3 = (bf16[2,96,256]{2,1,0:T(8,128)(2,1)S(1)}, bf16[2,96,256]{2,1,0:T(8,128)(2,1)S(1)}, u32[]{:S(2)}, u32[]{:S(2)}) collective-permute-start(bf16[2,96,256]{2,1,0:T(8,128)(2,1)S(1)} %broadcast_select_fusion.2), channel_id=1, source_target_pairs={{0,8},{8,0},{16,24},{24,16},{1,9},{9,1},{17,25},{25,17},{2,10},{10... | collective-permute-start | bytes 294920 | tf_op jit(solution)/shard_map/ppermute | solution.py:329

commit v2 on v1

--- a/solution.py
+++ b/solution.py
@@ -11,6 +11,7 @@
 GBINS = 32
 META = 16
 GROUP = 6
+BAND = 18
 CHUNK = 256
 BF = jnp.bfloat16
 F32 = jnp.float32
@@ -24,132 +25,202 @@
     return jnp.dot(a, b, preferred_element_type=F32)
 
 
-def pack_kernel(devices, cap, cols, count_ref, dest_ref, cells_ref, gauss_ref, feat_ref, send_ref, ext_ref):
+def pack_kernel(
+    devices, cap, cols, bands, count_ref, dest_ref, cells_ref, gauss_ref, feat_ref, send_ref,
+    ext_ref, hot_ref, sorted_ref, place_ref, place_smem, sem,
+):
     nrows, nfeat = feat_ref.shape
     step = 256
+    classes = 2 * bands
+    kinds = devices * classes
     dest = dest_ref[...]
     row_id = lax.broadcasted_iota(jnp.int32, (1, nrows), 1)
-    dest = jnp.where(row_id < count_ref[0], dest, devices)
-    earlier = (
-        lax.broadcasted_iota(jnp.int32, (step, step), 0) < lax.broadcasted_iota(jnp.int32, (step, step), 1)
-    ).astype(F32).astype(BF)
-    tile_id = lax.broadcasted_iota(jnp.int32, (devices, step), 0)
-    carry = jnp.zeros((devices, 1), F32)
-    ranks = []
-    for begin in range(0, nrows, step):
-        hot = (tile_id == dest[:, begin : begin + step]).astype(F32)
-        before = dot(hot.astype(BF), earlier) + carry
-        ranks.append(jnp.sum(before * hot, axis=0, keepdims=True))
-        carry = carry + jnp.sum(hot, axis=1, keepdims=True)
-    rank = jnp.concatenate(ranks, axis=1)
-    base = cells_ref[0:1, :]
-    lat = jnp.floor((base.astype(F32) + 0.5) * (1.0 / cols))
-    lon = base.astype(F32) - lat * cols
+    base = cells_ref[0:1, :].astype(F32)
+    lat = jnp.floor((base + 0.5) * (1.0 / cols))
+    lon = base - lat * cols
+    band = jnp.floor((lat + 0.5) * (1.0 / BAND))
+    kind = 2.0 * band + (lat == band * BAND + (BAND - 1)).astype(F32)
+    kind = dest * classes + kind.astype(jnp.int32)
+    kind = jnp.where(row_id < count_ref[0], kind, kinds)
     ratio = gauss_ref[...].astype(F32) * (1.0 / GBINS)
     weight = jnp.exp(-3.0 * ratio * ratio)
     meta = jnp.concatenate([lat, lon, weight, jnp.zeros((nfeat - 2 - KCELL, nrows), F32)], axis=0)
     ext_ref[:, :nfeat] = feat_ref[...]
     ext_ref[:, nfeat:] = meta.T.astype(BF)
-    slot = lax.broadcasted_iota(jnp.int32, (cap, nrows), 0).astype(F32)
+    hot_ref[...] = (lax.broadcasted_iota(jnp.int32, (kinds, nrows), 0) == kind).astype(F32).astype(BF)
+    counts = dot(hot_ref[...], jnp.ones((nrows, nfeat), BF))
+    ka = lax.broadcasted_iota(jnp.int32, (kinds, kinds), 0)
+    kb = lax.broadcasted_iota(jnp.int32, (kinds, kinds), 1)
+    da, db = ka // classes, kb // classes
+    within = ((da == db) & (kb < ka)).astype(F32).astype(BF)
+    together = (da == db).astype(F32).astype(BF)
+    ahead = ((db < da) & (kb % classes == 0)).astype(F32).astype(BF)
+    loads = dot(together, counts.astype(BF))
+    padded = jnp.floor((loads + 7.0) * 0.125) * 8.0
+    begins = dot(ahead, padded.astype(BF))
+    mine = begins + dot(within, counts.astype(BF))
+    kind_id = lax.broadcasted_iota(jnp.int32, (kinds, nfeat), 0)
+    lane_id = lax.broadcasted_iota(jnp.int32, (kinds, nfeat), 1)
+    lead = kind_id == lane_id * classes
+    place_ref[0:1, :] = jnp.sum(jnp.where(lead, begins, 0.0), axis=0, keepdims=True).astype(jnp.int32)
+    place_ref[1:2, :] = jnp.sum(jnp.where(lead, loads, 0.0), axis=0, keepdims=True).astype(jnp.int32)
+    copy = pltpu.make_async_copy(place_ref, place_smem, sem)
+    copy.start()
+    earlier = (
+        lax.broadcasted_iota(jnp.int32, (step, step), 0) < lax.broadcasted_iota(jnp.int32, (step, step), 1)
+    ).astype(F32).astype(BF)
+    carry = mine[:, 0:1]
+    places = []
+    for begin in range(0, nrows, step):
+        hot = hot_ref[:, begin : begin + step]
+        before = dot(hot, earlier) + carry
+        hot = hot.astype(F32)
+        places.append(
+            jnp.sum(before * hot, axis=0, keepdims=True) + jnp.sum(hot, axis=0, keepdims=True) - 1.0
+        )
+        carry = carry + jnp.sum(hot, axis=1, keepdims=True)
+    place = jnp.concatenate(places, axis=1)
+    live = row_id < count_ref[0]
+    place = jnp.where(live, place, -1.0)
+    slot = lax.broadcasted_iota(jnp.int32, (step, nrows), 0).astype(F32)
+    span = sorted_ref.shape[0]
+    for k in range(-(-(nrows + 8 * devices) // step)):
+        pick = (slot == place - k * step).astype(F32).astype(BF)
+        sorted_ref[k * step : (k + 1) * step, :] = dot(pick, ext_ref[...])
+    tail = -(-(nrows + 8 * devices) // step) * step
+    sorted_ref[tail:span, :] = jnp.zeros((span - tail, 2 * nfeat), F32)
+    copy.wait()
+    side_lane = lax.broadcasted_iota(jnp.int32, (META, nfeat), 1)
 
     def one(d, _):
-        key = jnp.where(dest == d, rank, -1.0)
-        pick = (slot == key).astype(F32).astype(BF)
-        got = dot(pick, ext_ref[...])
+        begin = pl.multiple_of(place_smem[0, d], 8)
+        got = sorted_ref[pl.ds(begin, cap), :]
         send_ref[d, 0:cap, :] = got[:, :nfeat].astype(BF)
         side = got[:, nfeat:]
         if cap < nfeat:
             side = jnp.concatenate([side, jnp.zeros((nfeat - cap, nfeat), F32)], axis=0)
-        send_ref[d, cap : cap + META, :] = side.T[0:META].astype(BF)
+        side = jnp.where(side_lane < place_smem[1, d], side.T[0:META], 0.0)
+        send_ref[d, cap : cap + META, :] = side.astype(BF)
         return 0
 
-    lax.fori_loop(0, devices, one, 0)
-
-
-def pack(count, dest, cells, gauss, feats, devices, cap, cols):
+    lax.fori_loop(0, devices, one, 0, unroll=4)
+
+
+def pack(count, dest, cells, gauss, feats, devices, cap, cols, bands):
     nrows, nfeat = feats.shape
+    span = -(-(nrows + 8 * devices) // 256) * 256 + cap
+    kinds = devices * 2 * bands
     return pl.pallas_call(
-        functools.partial(pack_kernel, devices, cap, cols),
+        functools.partial(pack_kernel, devices, cap, cols, bands),
         out_shape=jax.ShapeDtypeStruct((devices, cap + META, nfeat), BF),
         in_specs=[pl.BlockSpec(memory_space=pltpu.SMEM)] + [pl.BlockSpec(memory_space=pltpu.VMEM)] * 4,
         out_specs=pl.BlockSpec(memory_space=pltpu.VMEM),
-        scratch_shapes=[pltpu.VMEM((nrows, 2 * nfeat), BF)],
-        compiler_params=params(48),
+        scratch_shapes=[
+            pltpu.VMEM((nrows, 2 * nfeat), BF),
+            pltpu.VMEM((kinds, nrows), BF),
+            pltpu.VMEM((span, 2 * nfeat), F32),
+            pltpu.VMEM((8, nfeat), jnp.int32),
+            pltpu.SMEM((8, nfeat), jnp.int32),
+            pltpu.SemaphoreType.DMA,
+        ],
+        compiler_params=params(56),
     )(count, dest, cells, gauss, feats)
 
 
 def grid_kernel(
-    devices, cap, wide, recv_ref, back_ref, w_in_ref, w_bg_ref, w_dens_ref, first_ref, edge_ref,
-    feat_ref, meta_ref, acc_ref, back_scr, edge_scr, count_ref,
+    devices, cap, wide, lat_bands, recv_ref, back_ref, w_in_ref, w_bg_ref, w_dens_ref, first_ref, edge_ref,
+    rows_ref, lats_ref, feat_ref, meta_ref, acc_ref, back_scr, edge_scr, ends_ref, ends_smem, sem,
 ):
-    group = pl.program_id(0)
+    band = pl.program_id(0)
+    bands = pl.num_programs(0)
     nfeat = recv_ref.shape[2]
     rows, cols, chans = back_ref.shape
-    tiles = meta_ref.shape[0]
-
-    @pl.when(group == 0)
+    slots = devices * cap
+
+    @pl.when(band == 0)
     def _():
-        meta_ref[...] = jnp.zeros(meta_ref.shape, F32)
-        feat_ref[:, nfeat:] = jnp.ones((feat_ref.shape[0], nfeat), BF)
-        lane = lax.broadcasted_iota(jnp.int32, (8, nfeat), 1)
-
-        def count(s, _):
+        feat_ref[...] = jnp.zeros(feat_ref.shape, F32)
+        rows_ref[slots:, :] = jnp.zeros((rows_ref.shape[0] - slots, nfeat), F32)
+
+        def widen(s, _):
+            rows_ref[pl.ds(pl.multiple_of(s * cap, cap), cap), :] = recv_ref[s, 0:cap, :].astype(F32)
             side = recv_ref[s, cap : cap + META, :].astype(F32)
-            count_ref[s] = jnp.sum((side[2:3] > 0).astype(jnp.int32))
+            lats_ref[pl.ds(s, 1), :] = jnp.where(side[2:3] > 0, side[0:1], 1e6)
             return 0
 
-        lax.fori_loop(0, devices, count, 0, unroll=devices <= 32)
-
-        def compact(s, begin):
-            begin = pl.multiple_of(begin, 16)
-            feat_ref[pl.ds(begin, cap), 0:nfeat] = recv_ref[s, 0:cap, :]
-            side = recv_ref[s, cap : cap + META, :].astype(F32)[0:8]
-            tile, shift = begin // nfeat, begin % nfeat
-            moved = pltpu.roll(side, shift, axis=1)
-            meta_ref[tile] = jnp.where(lane >= shift, moved, meta_ref[tile])
-            meta_ref[tile + 1] = jnp.where(lane < shift, moved, 0.0)
-            return begin + (count_ref[s] + 15) // 16 * 16
-
-        total = lax.fori_loop(0, devices, compact, 0)
-        last = pl.multiple_of(total, 16)
-        feat_ref[pl.ds(last, CHUNK), 0:nfeat] = jnp.zeros((CHUNK, nfeat), BF)
-        count_ref[devices] = (total + CHUNK - 1) // CHUNK
-
+        lax.fori_loop(0, devices, widen, 0, unroll=4)
+        lats = lats_ref[...]
+        lane = lax.broadcasted_iota(jnp.int32, (devices, nfeat), 1)
+        ends = jnp.zeros((devices, nfeat), F32)
+        for b in range(lat_bands):
+            low = jnp.sum((lats < b * rows - 1.0).astype(F32), axis=1, keepdims=True)
+            high = jnp.sum((lats < (b + 1.0) * rows).astype(F32), axis=1, keepdims=True)
+            ends = jnp.where(lane == 2 * b, low, jnp.where(lane == 2 * b + 1, high, ends))
+        ends_ref[...] = ends.astype(jnp.int32)
+        copy = pltpu.make_async_copy(ends_ref, ends_smem, sem)
+        copy.start()
+        copy.wait()
+
+    meta_ref[...] = jnp.zeros(meta_ref.shape, F32)
+    lane = lax.broadcasted_iota(jnp.int32, (8, nfeat), 1)
+
+    def compact(s, out):
+        out = pl.multiple_of(out, 8)
+        low, high = ends_smem[s, 2 * band], ends_smem[s, 2 * band + 1]
+        source = pl.multiple_of(low // 8 * 8, 8)
+        feat_ref[pl.ds(out, cap), :] = rows_ref[pl.ds(pl.multiple_of(s * cap + source, 8), cap), :]
+        side = recv_ref[s, cap : cap + META, :].astype(F32)[0:8]
+        side = jnp.where((lane >= low) & (lane < high), side, 0.0)
+        shift = out - source + nfeat
+        tile, shift = shift // nfeat, shift % nfeat
+        moved = pltpu.roll(side, shift, axis=1)
+        meta_ref[tile] += jnp.where(lane >= shift, moved, 0.0)
+        meta_ref[tile + 1] += jnp.where(lane < shift, moved, 0.0)
+        return out + (high - source + 7) // 8 * 8
+
+    total = lax.fori_loop(0, devices, compact, 0, unroll=4)
     acc_ref[...] = jnp.zeros(acc_ref.shape, F32)
     col_id = lax.broadcasted_iota(jnp.int32, (wide, CHUNK), 0).astype(F32)
 
     def chunk(k, _):
-        side = jnp.concatenate([meta_ref[k * (CHUNK // nfeat) + q] for q in range(CHUNK // nfeat)], axis=1)
+        side = jnp.concatenate(
+            [meta_ref[1 + k * (CHUNK // nfeat) + q] for q in range(CHUNK // nfeat)], axis=1
+        )
         lat, lon = side[0:1], side[1:2]
         here = (col_id == lon + 2.0).astype(F32).astype(BF)
         after = (col_id == lon + 3.0).astype(F32).astype(BF)
         parts = []
         for i in range(rows):
-            row = (group * rows + i).astype(F32)
+            row = (band * rows + i).astype(F32)
             same, above = lat == row, lat == row - 1.0
             left = jnp.where(same, side[2:3], jnp.where(above, side[4:5], 0.0)).astype(BF)
             right = jnp.where(same, side[3:4], jnp.where(above, side[5:6], 0.0)).astype(BF)
             parts.append(here * left + after * right)
         spread = jnp.concatenate(parts, axis=0)
         begin = pl.multiple_of(k * CHUNK, CHUNK)
-        acc_ref[...] += dot(spread, feat_ref[pl.ds(begin, CHUNK), :])
+        values = jnp.concatenate(
+            [feat_ref[pl.ds(begin, CHUNK), :].astype(BF), jnp.ones((CHUNK, nfeat), BF)], axis=1
+        )
+        acc_ref[...] += dot(spread, values)
         return 0
 
-    lax.fori_loop(0, count_ref[devices], chunk, 0)
-    for i in range(rows):
-        back_scr[i * wide : i * wide + cols, :] = back_ref[i]
-    start = pltpu.roll(dot(back_scr[...], w_bg_ref[...]), 2, axis=0)
-    density = acc_ref[:, nfeat:]
-    normalized = (acc_ref[:, :nfeat] / (density + 1.0)).astype(BF)
-    start = start + dot(normalized, w_in_ref[...])
-    start = start + jnp.concatenate([density] * (chans // nfeat), axis=1) * w_dens_ref[...]
-    first = start.astype(BF)
-    for i in range(rows):
-        first_ref[i] = first[i * wide : (i + 1) * wide]
-        for k, col in enumerate((2, 3, cols, cols + 1)):
-            edge_scr[k, pl.ds(group * rows + i, 1), :] = start[i * wide + col : i * wide + col + 1]
-
-    @pl.when(group == pl.num_programs(0) - 1)
+    lax.fori_loop(0, (total + CHUNK - 1) // CHUNK, chunk, 0)
+    for g in range(0, rows, GROUP):
+        for i in range(GROUP):
+            back_scr[i * wide : i * wide + cols, :] = back_ref[g + i]
+        sums = acc_ref[g * wide : (g + GROUP) * wide, :]
+        start = pltpu.roll(dot(back_scr[...], w_bg_ref[...]), 2, axis=0)
+        density = sums[:, nfeat:]
+        normalized = (sums[:, :nfeat] / (density + 1.0)).astype(BF)
+        start = start + dot(normalized, w_in_ref[...])
+        start = start + jnp.concatenate([density] * (chans // nfeat), axis=1) * w_dens_ref[...]
+        first = start.astype(BF)
+        for i in range(GROUP):
+            first_ref[band * rows + g + i] = first[i * wide : (i + 1) * wide]
+            for k, col in enumerate((2, 3, cols, cols + 1)):
+                edge_scr[k, pl.ds(band * rows + g + i, 1), :] = start[i * wide + col : i * wide + col + 1]
+
+    @pl.when(band == bands - 1)
     def _():
         edge_ref[...] = edge_scr[...].astype(BF)
 
@@ -161,32 +232,33 @@
     tall = -(-lat_rows // 16) * 16
     whole = pl.BlockSpec(memory_space=pltpu.VMEM)
     return pl.pallas_call(
-        functools.partial(grid_kernel, devices, cap, wide),
-        grid=(lat_rows // GROUP,),
+        functools.partial(grid_kernel, devices, cap, wide, lat_rows // BAND),
+        grid=(lat_rows // BAND,),
         out_shape=(
             jax.ShapeDtypeStruct((lat_rows, wide, chans), BF),
             jax.ShapeDtypeStruct((4, tall, chans), BF),
         ),
         in_specs=[
             whole,
-            pl.BlockSpec((GROUP, cols, chans), lambda g: (g, 0, 0)),
+            pl.BlockSpec((BAND, cols, chans), lambda g: (g, 0, 0)),
             whole,
             whole,
             whole,
         ],
-        out_specs=(
-            pl.BlockSpec((GROUP, wide, chans), lambda g: (g, 0, 0)),
-            pl.BlockSpec((4, tall, chans), lambda g: (0, 0, 0)),
-        ),
+        out_specs=(whole, whole),
         scratch_shapes=[
-            pltpu.VMEM((slots + 2 * CHUNK, 2 * nfeat), BF),
-            pltpu.VMEM((slots // nfeat + 4, 8, nfeat), F32),
-            pltpu.VMEM((GROUP * wide, 2 * nfeat), F32),
+            pltpu.VMEM((slots + cap, nfeat), F32),
+            pltpu.VMEM((devices, nfeat), F32),
+            pltpu.VMEM((slots + cap + CHUNK, nfeat), F32),
+            pltpu.VMEM((slots // nfeat + 6, 8, nfeat), F32),
+            pltpu.VMEM((BAND * wide, 2 * nfeat), F32),
             pltpu.VMEM((GROUP * wide, chans), BF),
             pltpu.VMEM((4, tall, chans), F32),
-            pltpu.SMEM((devices + 1,), jnp.int32),
+            pltpu.VMEM((devices, nfeat), jnp.int32),
+            pltpu.SMEM((devices, nfeat), jnp.int32),
+            pltpu.SemaphoreType.DMA,
         ],
-        compiler_params=params(48),
+        compiler_params=params(40),
     )(recv, background, w_in, w_bg, w_dens)
 
 
@@ -267,7 +339,7 @@
             pltpu.VMEM(((lat_rows + 2) * wide, 3 * chans), BF),
             pltpu.VMEM((4, west.shape[1], chans), F32),
         ],
-        compiler_params=params(60),
+        compiler_params=params(44),
     )(poles, first, west, east, north, south, one, two)
 
 
@@ -308,7 +380,8 @@
     cap = 2 * nrows // devices
     wide = -(-(cols + 4) // 16) * 16
     send = pack(
-        row_counts, obs_dest.reshape(1, nrows), obs_cells.T, obs_gauss.T, obs_features, devices, cap, cols
+        row_counts, obs_dest.reshape(1, nrows), obs_cells.T, obs_gauss.T, obs_features, devices, cap, cols,
+        lat_rows // BAND,
     )
     recv = lax.all_to_all(send, axes, split_axis=0, concat_axis=0, tiled=True)
     first, edges = gridded(recv, background, w_in, w_bg, w_dens.reshape(1, chans), cap, wide)

time: 155 us -> 113 us (0.73)
  Pallas kernels: 87 us -> 57.2 us
  starting transfers between devices: 20 us -> 9.11 us
  local copies, waits for them, and re-layouts: 7.38 us -> 5.14 us
  waiting for transfers between devices: 38.3 us -> 40.1 us
    pallas_call x2, Pallas kernels: 51.8 us -> 24.5 us  [the longest x1 17.2 us: gridded(): pl.pallas_call(functools.partial(grid_kernel, devices, cap, wide, lat_row...]
    ppermute x1, starting transfers between devices: 10.8 us -> 0.06 us  [shards(): lax.ppermute(edges[0:2], 'lon', [((i + 1) % lon_count, i) for i in range(...]
    pallas_call x1, Pallas kernels: 35.2 us -> 32.7 us  [convolved(): pl.pallas_call(conv_kernel, grid=(lat_rows // GROUP,), out_shape=jax.Shap...]
    ppermute x1, waiting for transfers between devices: 0.5 us -> 2.29 us  [shards(): lax.ppermute(edges[0:2], 'lon', [((i + 1) % lon_count, i) for i in range(...]
    unnamed x16 -> x12, local copies, waits for them, and re-layouts: 5.67 us -> 4.69 us
  transfers between devices with their start and end apart: 5 -> 5, of which waited for: 4 -> 4; matrix products, arithmetic and copies ran while one was open for 1% -> 0% of each run, Pallas kernels for 0% -> 0%
where the time goes in v2:
time: 113 us
  Pallas kernels  57.2 us (51%)
  waiting for transfers between devices  40.1 us (35%)
  starting transfers between devices  9.11 us (8%)
  local copies, waits for them, and re-layouts  5.14 us (5%)
    pallas_call x1, Pallas kernels, convolved(): pl.pallas_call(conv_kernel, grid=(lat_rows // GROUP,), out_shape=jax.Shap...  32.7 us
    all_to_all x1, waiting for transfers between devices, shards(): recv = lax.all_to_all(send, axes, split_axis=0, concat_axis=0, tiled=True)  30.3 us
    pallas_call x1, Pallas kernels, gridded(): pl.pallas_call(functools.partial(grid_kernel, devices, cap, wide, lat_row...  17.2 us
    pallas_call x1, Pallas kernels, pack(): pl.pallas_call(functools.partial(pack_kernel, devices, cap, cols, bands),...  7.32 us
    all_to_all x1, starting transfers between devices, shards(): recv = lax.all_to_all(send, axes, split_axis=0, concat_axis=0, tiled=True)  7.29 us
    unnamed x12, local copies, waits for them, and re-layouts  4.69 us
    ppermute x1, waiting for transfers between devices, shards(): by_outer = lax.ppermute(jnp.where(even, top, bottom), axes, outer)  4.44 us
    ppermute x1, waiting for transfers between devices, shards(): lax.ppermute(edges[2:4], 'lon', [(i, (i + 1) % lon_count) for i in range(...  3.06 us
  transfers between devices with their start and end apart: 5, of which 4 were waited for; matrix products, arithmetic and copies ran while one was open for 0% of the time, Pallas kernels for 0%

profile of v2, /device:TPU:0, one launch (start us, length us, event | category | flops | bytes accessed | tf_op | source)
XLA Modules:
  0.0 112.6 jit_solution(6390034046665954434)
XLA Ops:
  0.7 7.3 %shard_map.109 = bf16[32,144,128]{2,1,0:T(8,128)(2,1)} custom-call(s32[1]{0:T(128)S(6)} %copy.16.count_ref, s32[1,2048]{1,0:T(1,128)} %bitcast.29, s32[4,2048]{1,0:T(4,128)} %bitcast.27, s32[4,2048]{1,0:T(4,128)} %bitcast.28, bf16[2048,128]{1,0:T(8,128)(2,1)} %feat_ref.1), custom_call_target="tpu_custom_call" | custom-call | tf_op jit(solution)/shard_map/pallas_call | solution.py:113
  8.0 0.0 copy-start.1
  8.0 0.0 copy-start.2
  8.0 7.3 %all-to-all-start = ((bf16[32,144,128]{2,1,0:T(8,128)(2,1)}), bf16[32,144,128]{2,1,0:T(8,128)(2,1)S(1)}, u32[]{:S(2)}, u32[]{:S(2)}) async-start(bf16[32,144,128]{2,1,0:T(8,128)(2,1)} %shard_map.109), calls=%async_computation | async-start | bytes 2359296 | tf_op jit(solution)/shard_map/all_to_all | solution.py:386
  15.3 0.1 pad.13.clone
  15.4 30.3 %all-to-all-done.recv_ref = bf16[32,144,128]{2,1,0:T(8,128)(2,1)S(1)} async-done(((bf16[32,144,128]{2,1,0:T(8,128)(2,1)}), bf16[32,144,128]{2,1,0:T(8,128)(2,1)S(1)}, u32[]{:S(2)}, u32[]{:S(2)}) %all-to-all-start) | async-done | bytes 1179680 | tf_op jit(solution)/shard_map/all_to_all | solution.py:386
  45.7 2.3 %copy-done = bf16[90,90,256]{2,1,0:T(8,128)(2,1)S(1)} copy-done((bf16[90,90,256]{2,1,0:T(8,128)(2,1)S(1)}, bf16[90,90,256]{2,1,0:T(8,128)(2,1)}, u32[]{:S(2)}) %copy-start) | copy-done | bytes 4147224
  48.0 0.9 copy-done.3
  48.9 0.8 copy-done.4
  49.7 0.7 copy-done.5
  50.4 17.2 %shard_map.110 = (bf16[90,96,256]{2,1,0:T(8,128)(2,1)S(1)}, bf16[4,96,256]{2,1,0:T(8,128)(2,1)S(1)}) custom-call(bf16[32,144,128]{2,1,0:T(8,128)(2,1)S(1)} %all-to-all-done.recv_ref, bf16[90,90,256]{2,1,0:T(8,128)(2,1)S(1)} %copy-done, bf16[128,256]{1,0:T(8,128)(2,1)S(1)} %copy-done.4, bf16[256,256]{1,0:T(8,128)(2,1)S(1)} %copy-done.3, f32[1,256]{1,0:T(1,128)S(1)} %bitcast.26), custom_call_target="tpu_custom_call" | custom-call | tf_op jit(solution)/shard_map/pallas_call | solution.py:234
  67.5 0.2 copy.12
  67.7 0.1 fusion.8
  67.8 0.1 collective-permute-start.1
  68.0 0.5 collective-permute-start
  68.5 2.3 %collective-permute-done.1 = bf16[2,96,256]{2,0,1:T(2,128)(2,1)S(1)} collective-permute-done((bf16[2,96,256]{2,0,1:T(2,128)(2,1)S(1)}, bf16[2,96,256]{2,0,1:T(2,128)(2,1)S(1)}, u32[]{:S(2)}, u32[]{:S(2)}) %collective-permute-start.1) | collective-permute-done | bytes 98336 | tf_op jit(solution)/shard_map/ppermute | solution.py:389
  70.8 3.1 %collective-permute-done = bf16[2,96,256]{2,0,1:T(2,128)(2,1)S(1)} collective-permute-done((bf16[2,96,256]{2,0,1:T(2,128)(2,1)S(1)}, bf16[2,96,256]{2,0,1:T(2,128)(2,1)S(1)}, u32[]{:S(2)}, u32[]{:S(2)}) %collective-permute-start) | collective-permute-done | bytes 98336 | tf_op jit(solution)/shard_map/ppermute | solution.py:388
  73.9 0.1 broadcast_select_fusion.2
  74.0 0.1 broadcast_select_fusion.3
  74.1 0.1 collective-permute-start.2
  74.2 1.2 %collective-permute-start.3 = (bf16[2,96,256]{2,1,0:T(8,128)(2,1)S(1)}, bf16[2,96,256]{2,1,0:T(8,128)(2,1)S(1)}, u32[]{:S(2)}, u32[]{:S(2)}) collective-permute-start(bf16[2,96,256]{2,1,0:T(8,128)(2,1)S(1)} %broadcast_select_fusion.2), channel_id=1, source_target_pairs={{0,8},{8,0},{16,24},{24,16},{1,9},{9,1},{17,25},{25,17},{2,10},{10... | collective-permute-start | bytes 294920 | tf_op jit(solution)/shard_map/ppermute | solution.py:402
  75.3 0.1 add_convert_fusion.pole_ref
  75.4 4.4 %collective-permute-done.2 = bf16[2,96,256]{2,1,0:T(8,128)(2,1)S(1)} collective-permute-done((bf16[2,96,256]{2,1,0:T(8,128)(2,1)S(1)}, bf16[2,96,256]{2,1,0:T(8,128)(2,1)S(1)}, u32[]{:S(2)}, u32[]{:S(2)}) %collective-permute-start.2) | collective-permute-done | bytes 98336 | tf_op jit(solution)/shard_map/ppermute | solution.py:403
  79.9 32.7 %shard_map.111 = bf16[90,90,256]{2,1,0:T(8,128)(2,1)} custom-call(s32[2]{0:T(128)S(1)} %add_convert_fusion.pole_ref, bf16[90,96,256]{2,1,0:T(8,128)(2,1)S(1)} %get-tuple-element.7.first_ref, bf16[2,96,256]{2,1,0:T(8,128)(2,1)S(1)} %copy.14.west_ref, bf16[2,96,256]{2,1,0:T(8,128)(2,1)S(1)} %copy.15.east_ref, ...), custom_call_target="tpu_custom_call" | custom-call | tf_op jit(solution)/shard_map/pallas_call | solution.py:331
  (15 shorter events, 0.1 us)
Async XLA Ops:
  8.0 71.9 %copy-start.1 = (bf16[3,3,256,256]{3,2,1,0:T(8,128)(2,1)S(1)}, bf16[3,3,256,256]{3,2,1,0:T(8,128)(2,1)}, u32[]{:S(2)}) copy-start(bf16[3,3,256,256]{3,2,1,0:T(8,128)(2,1)} %param.20) | copy-start | bytes 3538948
  8.0 71.9 %copy-start.2 = (bf16[3,3,256,256]{3,2,1,0:T(8,128)(2,1)S(1)}, bf16[3,3,256,256]{3,2,1,0:T(8,128)(2,1)}, u32[]{:S(2)}) copy-start(bf16[3,3,256,256]{3,2,1,0:T(8,128)(2,1)} %param.21) | copy-start | bytes 3538948
  8.0 37.7 %all-to-all-start = ((bf16[32,144,128]{2,1,0:T(8,128)(2,1)}), bf16[32,144,128]{2,1,0:T(8,128)(2,1)S(1)}, u32[]{:S(2)}, u32[]{:S(2)}) async-start(bf16[32,144,128]{2,1,0:T(8,128)(2,1)} %shard_map.109), calls=%async_computation | async-start | bytes 2359296 | tf_op jit(solution)/shard_map/all_to_all | solution.py:386
  45.7 2.3 %copy-start = (bf16[90,90,256]{2,1,0:T(8,128)(2,1)S(1)}, bf16[90,90,256]{2,1,0:T(8,128)(2,1)}, u32[]{:S(2)}) copy-start(bf16[90,90,256]{2,1,0:T(8,128)(2,1)} %back_ref.1) | copy-start | bytes 12441604
  47.9 0.9 copy-start.3
  48.9 0.8 copy-start.4
  49.7 0.7 copy-start.5
  67.8 2.9 %collective-permute-start.1 = (bf16[2,96,256]{2,0,1:T(2,128)(2,1)S(1)}, bf16[2,96,256]{2,0,1:T(2,128)(2,1)S(1)}, u32[]{:S(2)}, u32[]{:S(2)}) collective-permute-start(bf16[2,96,256]{2,0,1:T(2,128)(2,1)S(1)} %get-tuple-element.13), channel_id=1, source_target_pairs={{1,0},{2,1},{3,2},{4,3},{5,4},{6,5},{7,6},{0,7},{9,8},{10,9},{11,1... | collective-permute-start | bytes 294920 | tf_op jit(solution)/shard_map/ppermute | solution.py:389
  68.0 5.9 %collective-permute-start = (bf16[2,96,256]{2,0,1:T(2,128)(2,1)S(1)}, bf16[2,96,256]{2,0,1:T(2,128)(2,1)S(1)}, u32[]{:S(2)}, u32[]{:S(2)}) collective-permute-start(bf16[2,96,256]{2,0,1:T(2,128)(2,1)S(1)} %get-tuple-element.14), channel_id=1, source_target_pairs={{0,1},{1,2},{2,3},{3,4},{4,5},{5,6},{6,7},{7,0},{8,9},{9,10},{10,1... | collective-permute-start | bytes 294920 | tf_op jit(solution)/shard_map/ppermute | solution.py:388
  74.1 5.8 %collective-permute-start.2 = (bf16[2,96,256]{2,1,0:T(8,128)(2,1)S(1)}, bf16[2,96,256]{2,1,0:T(8,128)(2,1)S(1)}, u32[]{:S(2)}, u32[]{:S(2)}) collective-permute-start(bf16[2,96,256]{2,1,0:T(8,128)(2,1)S(1)} %broadcast_select_fusion.3), channel_id=1, source_target_pairs={{8,16},{16,8},{0,4},{24,28},{9,17},{17,9},{1,5},{25,29},{10,18},{1... | collective-permute-start | bytes 294920 | tf_op jit(solution)/shard_map/ppermute | solution.py:403
  74.2 5.7 %collective-permute-start.3 = (bf16[2,96,256]{2,1,0:T(8,128)(2,1)S(1)}, bf16[2,96,256]{2,1,0:T(8,128)(2,1)S(1)}, u32[]{:S(2)}, u32[]{:S(2)}) collective-permute-start(bf16[2,96,256]{2,1,0:T(8,128)(2,1)S(1)} %broadcast_select_fusion.2), channel_id=1, source_target_pairs={{0,8},{8,0},{16,24},{24,16},{1,9},{9,1},{17,25},{25,17},{2,10},{10... | collective-permute-start | bytes 294920 | tf_op jit(solution)/shard_map/ppermute | solution.py:402

commit v3 on v2

--- a/solution.py
+++ b/solution.py
@@ -13,6 +13,7 @@
 GROUP = 6
 BAND = 18
 CHUNK = 256
+FINISH = 15
 BF = jnp.bfloat16
 F32 = jnp.float32
 
@@ -127,14 +128,45 @@
     )(count, dest, cells, gauss, feats)
 
 
+def back_kernel(wide, back_ref, w_in_ref, w_bg_ref, w_dens_ref, out_ref, w_in_out, w_dens_out, scr):
+    band = pl.program_id(0)
+    rows, cols, chans = back_ref.shape
+    for i in range(rows):
+        scr[i * wide : i * wide + cols, :] = back_ref[i]
+    begin = pl.multiple_of(band * rows * wide, 16)
+    out_ref[pl.ds(begin, rows * wide), :] = pltpu.roll(dot(scr[...], w_bg_ref[...]), 2, axis=0)
+    w_in_out[...] = w_in_ref[...]
+    w_dens_out[...] = w_dens_ref[...]
+
+
+def projected(background, w_in, w_bg, w_dens, wide):
+    lat_rows, cols, chans = background.shape
+    whole = pl.BlockSpec(memory_space=pltpu.VMEM)
+    return pl.pallas_call(
+        functools.partial(back_kernel, wide),
+        grid=(lat_rows // BAND,),
+        out_shape=(
+            jax.ShapeDtypeStruct((lat_rows * wide, chans), F32),
+            jax.ShapeDtypeStruct(w_in.shape, BF),
+            jax.ShapeDtypeStruct(w_dens.shape, F32),
+        ),
+        in_specs=[pl.BlockSpec((BAND, cols, chans), lambda g: (g, 0, 0)), whole, whole, whole],
+        out_specs=(whole, whole, whole),
+        scratch_shapes=[pltpu.VMEM((BAND * wide, chans), BF)],
+        compiler_params=params(24),
+    )(background, w_in, w_bg, w_dens)
+
+
 def grid_kernel(
-    devices, cap, wide, lat_bands, recv_ref, back_ref, w_in_ref, w_bg_ref, w_dens_ref, first_ref, edge_ref,
-    rows_ref, lats_ref, feat_ref, meta_ref, acc_ref, back_scr, edge_scr, ends_ref, ends_smem, sem,
+    devices, cap, wide, cols, lat_bands, recv_ref, back_ref, w_in_ref, w_dens_ref,
+    first_ref, west_ref, east_ref, inner_ref, outer_ref, corner_ref,
+    rows_ref, lats_ref, feat_ref, meta_ref, acc_ref, edge_scr, ends_ref, ends_smem, sem,
 ):
     band = pl.program_id(0)
     bands = pl.num_programs(0)
     nfeat = recv_ref.shape[2]
-    rows, cols, chans = back_ref.shape
+    lat_rows, _, chans = first_ref.shape
+    rows = lat_rows // lat_bands
     slots = devices * cap
 
     @pl.when(band == 0)
@@ -206,10 +238,9 @@
 
     lax.fori_loop(0, (total + CHUNK - 1) // CHUNK, chunk, 0)
     for g in range(0, rows, GROUP):
-        for i in range(GROUP):
-            back_scr[i * wide : i * wide + cols, :] = back_ref[g + i]
         sums = acc_ref[g * wide : (g + GROUP) * wide, :]
-        start = pltpu.roll(dot(back_scr[...], w_bg_ref[...]), 2, axis=0)
+        begin = pl.multiple_of((band * rows + g) * wide, 16)
+        start = back_ref[pl.ds(begin, GROUP * wide), :]
         density = sums[:, nfeat:]
         normalized = (sums[:, :nfeat] / (density + 1.0)).astype(BF)
         start = start + dot(normalized, w_in_ref[...])
@@ -222,140 +253,226 @@
 
     @pl.when(band == bands - 1)
     def _():
-        edge_ref[...] = edge_scr[...].astype(BF)
-
-
-def gridded(recv, background, w_in, w_bg, w_dens, cap, wide):
+        west_ref[...] = edge_scr[0:2].astype(BF)
+        east_ref[...] = edge_scr[2:4].astype(BF)
+        even = lax.axis_index("lat") % 2 == 0
+        for k in range(2):
+            top, bottom = first_ref[k].astype(F32), first_ref[lat_rows - 1 - k].astype(F32)
+            inner = jnp.where(even, bottom, top).astype(BF)
+            outer = jnp.where(even, top, bottom).astype(BF)
+            inner_ref[k] = inner
+            outer_ref[k] = outer
+            corner_ref[0, k] = inner[:16]
+            corner_ref[1, k] = inner[wide - 16 :]
+            corner_ref[2, k] = outer[:16]
+            corner_ref[3, k] = outer[wide - 16 :]
+
+
+def gridded(recv, back, w_in, w_dens, cap, wide, lat_rows, cols):
     devices, _, nfeat = recv.shape
-    lat_rows, cols, chans = background.shape
+    chans = back.shape[1]
     slots = devices * cap
     tall = -(-lat_rows // 16) * 16
     whole = pl.BlockSpec(memory_space=pltpu.VMEM)
     return pl.pallas_call(
-        functools.partial(grid_kernel, devices, cap, wide, lat_rows // BAND),
+        functools.partial(grid_kernel, devices, cap, wide, cols, lat_rows // BAND),
         grid=(lat_rows // BAND,),
         out_shape=(
             jax.ShapeDtypeStruct((lat_rows, wide, chans), BF),
-            jax.ShapeDtypeStruct((4, tall, chans), BF),
+            jax.ShapeDtypeStruct((2, tall, chans), BF),
+            jax.ShapeDtypeStruct((2, tall, chans), BF),
+            jax.ShapeDtypeStruct((2, wide, chans), BF),
+            jax.ShapeDtypeStruct((2, wide, chans), BF),
+            jax.ShapeDtypeStruct((4, 2, 16, chans), BF),
         ),
-        in_specs=[
-            whole,
-            pl.BlockSpec((BAND, cols, chans), lambda g: (g, 0, 0)),
-            whole,
-            whole,
-            whole,
-        ],
-        out_specs=(whole, whole),
+        in_specs=[whole] * 4,
+        out_specs=(whole,) * 6,
         scratch_shapes=[
             pltpu.VMEM((slots + cap, nfeat), F32),
             pltpu.VMEM((devices, nfeat), F32),
             pltpu.VMEM((slots + cap + CHUNK, nfeat), F32),
             pltpu.VMEM((slots // nfeat + 6, 8, nfeat), F32),
             pltpu.VMEM((BAND * wide, 2 * nfeat), F32),
-            pltpu.VMEM((GROUP * wide, chans), BF),
             pltpu.VMEM((4, tall, chans), F32),
             pltpu.VMEM((devices, nfeat), jnp.int32),
             pltpu.SMEM((devices, nfeat), jnp.int32),
             pltpu.SemaphoreType.DMA,
         ],
-        compiler_params=params(40),
-    )(recv, background, w_in, w_bg, w_dens)
-
-
-def three(value):
-    size = value.shape[0]
-    return [value.astype(BF), pltpu.roll(value, size - 1, axis=0).astype(BF), pltpu.roll(value, size - 2, axis=0).astype(BF)]
-
-
-def conv_kernel(
-    pole_ref, first_ref, west_ref, east_ref, north_ref, south_ref, one_ref, two_ref, out_ref,
-    wide_in, wide_hid, cols_scr,
+        compiler_params=params(32),
+    )(recv, back, w_in, w_dens)
+
+
+def put(ref, begin, value):
+    size, chans = value.shape
+    for b in range(3):
+        part = value if b == 0 else pltpu.roll(value, size - b, axis=0)
+        ref[pl.ds(begin, size), b * chans : (b + 1) * chans] = part.astype(BF)
+
+
+def taps(ref, begin, size, wide, w_ref):
+    field = jnp.concatenate([ref[pl.ds(begin + a * wide, size), :] for a in range(3)], axis=1)
+    return dot(field, w_ref[...].reshape(field.shape[1], w_ref.shape[2]))
+
+
+def inside_kernel(split, first_ref, one_ref, hid_ref, field):
+    lat_rows, wide, chans = first_ref.shape
+
+    def load(r, _):
+        put(field, pl.multiple_of(r * wide, 16), first_ref[r].astype(F32))
+        return 0
+
+    lax.fori_loop(0, lat_rows, load, 0, unroll=6)
+    size = (lat_rows - 2) // split * wide
+
+    def hidden(g, _):
+        begin = pl.multiple_of(g * size, 16)
+        total = taps(field, begin, size, wide, one_ref)
+        put(hid_ref, pl.multiple_of(begin + 2 * wide, 16), jax.nn.gelu(total))
+        return 0
+
+    lax.fori_loop(0, split, hidden, 0)
+
+
+def inside(first, one):
+    lat_rows, wide, chans = first.shape
+    whole = pl.BlockSpec(memory_space=pltpu.VMEM)
+    split = next(n for n in (4, 2, 1) if (lat_rows - 2) % n == 0)
+    return pl.pallas_call(
+        functools.partial(inside_kernel, split),
+        out_shape=jax.ShapeDtypeStruct(((lat_rows + 2) * wide, 3 * chans), BF),
+        in_specs=[whole] * 2,
+        out_specs=whole,
+        scratch_shapes=[pltpu.VMEM((lat_rows * wide, 3 * chans), BF)],
+        compiler_params=params(30),
+    )(first, one)
+
+
+def finish_kernel(
+    lat_count, hid_in, first_ref, own_west, own_east, west_ref, east_ref, inner_ref, outer_ref,
+    inner_left, inner_right, outer_left, outer_right, one_ref, two_ref, out_ref, hid_ref, rim, cols_scr,
 ):
     group = pl.program_id(0)
     lat_rows, wide, chans = first_ref.shape
     rows, cols, _ = out_ref.shape
     block = rows * wide
 
-    def put(ref, begin, size, value):
-        for b, part in enumerate(three(value)):
-            ref[pl.ds(begin, size), b * chans : (b + 1) * chans] = part
-
     @pl.when(group == 0)
     def _():
-        cols_scr[0:2] = west_ref[...].astype(F32)
-        cols_scr[2:4] = east_ref[...].astype(F32)
+        lat_index = lax.axis_index("lat")
+        even = lat_index % 2 == 0
         row_id = lax.broadcasted_iota(jnp.int32, (wide, chans), 0)
-
-        def load(r, _):
+        short_id = lax.broadcasted_iota(jnp.int32, (16, chans), 0)
+
+        def edge_row(first_half, k):
+            def pick(inner, outer):
+                return jnp.where(even == first_half, outer[k].astype(F32), inner[k].astype(F32))
+
+            middle = pick(inner_ref, outer_ref)
+            left = pltpu.roll(pick(inner_left, outer_left), (wide - cols) % 16, axis=0)
+            right = pltpu.roll(pick(inner_right, outer_right), (cols - (wide - 16)) % 16, axis=0)
+            head = jnp.where(short_id < 2, left, middle[:16])
+            at = short_id + (wide - 16)
+            tail = jnp.where((at == cols + 2) | (at == cols + 3), right, middle[wide - 16 :])
+            return jnp.concatenate([head, middle[16 : wide - 16], tail], axis=0)
+
+        def own_row(r):
             value = first_ref[r].astype(F32)
-            for k, col in enumerate((0, 1, cols + 2, cols + 3)):
-                value = jnp.where(row_id == col, cols_scr[k, pl.ds(r, 1), :], value)
-            put(wide_in, pl.multiple_of((r + 2) * wide, 16), wide, value)
-            return 0
-
-        lax.fori_loop(0, lat_rows, load, 0)
-        put(wide_in, wide, wide, north_ref[0].astype(F32))
-        put(wide_in, 0, wide, north_ref[1].astype(F32))
-        put(wide_in, (lat_rows + 2) * wide, wide, south_ref[0].astype(F32))
-        put(wide_in, (lat_rows + 3) * wide, wide, south_ref[1].astype(F32))
-        for side, begin in ((0, 0), (1, lat_rows + 1)):
+            sides = [west_ref[0], west_ref[1], east_ref[0], east_ref[1]]
+            for side, col in zip(sides, (0, 1, cols + 2, cols + 3)):
+                value = jnp.where(row_id == col, side.astype(F32)[r : r + 1], value)
+            return value
+
+        lines = [edge_row(True, 1), edge_row(True, 0), own_row(0), own_row(1)]
+        lines += [own_row(lat_rows - 2), own_row(lat_rows - 1), edge_row(False, 0), edge_row(False, 1)]
+        for n, line in enumerate(lines):
+            put(rim, n * wide, line)
+        for begin, index, pole in ((0, 0, lat_index == 0), (5, lat_rows + 1, lat_index == lat_count - 1)):
             total = jnp.zeros((wide, chans), F32)
             for a in range(3):
-                pick = jnp.where(pole_ref[side] == 1, 2 - a, a)
-                total = total + dot(wide_in[(begin + a) * wide : (begin + a + 1) * wide, :], one_ref[pick])
-            put(wide_hid, begin * wide, wide, jax.nn.gelu(total))
-
-        def hidden(g, _):
-            begin = pl.multiple_of((g * rows + 1) * wide, 16)
-            total = dot(wide_in[pl.ds(begin, block), :], one_ref[0])
-            total = total + dot(wide_in[pl.ds(begin + wide, block), :], one_ref[1])
-            total = total + dot(wide_in[pl.ds(begin + 2 * wide, block), :], one_ref[2])
-            put(wide_hid, begin, block, jax.nn.gelu(total))
+                tap = jnp.where(pole, 2 - a, a)
+                total = total + dot(rim[(begin + a) * wide : (begin + a + 1) * wide, :], one_ref[tap])
+            put(hid_ref, index * wide, jax.nn.gelu(total))
+        total = jnp.zeros((2 * wide, chans), F32)
+        for a in range(3):
+            pair = [rim[(n + a) * wide : (n + a + 1) * wide, :] for n in (1, 4)]
+            total = total + dot(jnp.concatenate(pair, axis=0), one_ref[a])
+        total = jax.nn.gelu(total)
+        put(hid_ref, wide, total[:wide])
+        put(hid_ref, lat_rows * wide, total[wide:])
+
+        lines = [west_ref[0], west_ref[1], own_west[0], own_west[1]]
+        lines += [own_east[0], own_east[1], east_ref[0], east_ref[1]]
+        windows = [jnp.concatenate(lines[n : n + 3], axis=1) for n in (0, 1, 4, 5)]
+        windows = jnp.concatenate(windows, axis=0)
+        size = windows.shape[0]
+        total = pltpu.roll(dot(windows, one_ref[0]), 1, axis=0) + dot(windows, one_ref[1])
+        total = total + pltpu.roll(dot(windows, one_ref[2]), size - 1, axis=0)
+        total = jax.nn.gelu(total)
+        tall = size // 4
+        for n in range(4):
+            cols_scr[n] = total[n * tall : (n + 1) * tall]
+        last = wide - 16
+
+        def patch(r, _):
+            fixes = [cols_scr[n, pl.ds(r, 1), :] for n in range(4)]
+            begin = pl.multiple_of((r + 1) * wide, 16)
+            for b in range(3):
+                lanes = slice(b * chans, (b + 1) * chans)
+                for start in (0, last):
+                    edits = [
+                        (col - b - start, fix)
+                        for col, fix in zip((0, 1, cols, cols + 1), fixes)
+                        if 0 <= col - b - start < 16
+                    ]
+                    if edits:
+                        value = hid_ref[pl.ds(begin + start, 16), lanes].astype(F32)
+                        for at, fix in edits:
+                            value = jnp.where(short_id == at, fix, value)
+                        hid_ref[pl.ds(begin + start, 16), lanes] = value.astype(BF)
             return 0
 
-        lax.fori_loop(0, lat_rows // rows, hidden, 0)
+        lax.fori_loop(1, lat_rows - 1, patch, 0, unroll=8)
 
     begin = pl.multiple_of(group * block, 16)
-    total = wide_in[pl.ds(begin + 2 * wide, block), 2 * chans :].astype(F32)
-    total = total + dot(wide_hid[pl.ds(begin, block), :], two_ref[0])
-    total = total + dot(wide_hid[pl.ds(begin + wide, block), :], two_ref[1])
-    total = total + dot(wide_hid[pl.ds(begin + 2 * wide, block), :], two_ref[2])
+    total = taps(hid_ref, begin, block, wide, two_ref)
+    own = first_ref[pl.ds(group * rows, rows)].reshape(block, chans).astype(F32)
+    total = total + pltpu.roll(own, block - 2, axis=0)
     result = total.astype(BF)
     for i in range(rows):
         out_ref[i] = result[i * wide : i * wide + cols]
 
 
-def convolved(poles, first, west, east, north, south, one, two, cols):
+def finished(hid, first, sides, one, two, cols, lat_count):
     lat_rows, wide, chans = first.shape
     whole = pl.BlockSpec(memory_space=pltpu.VMEM)
-    return pl.pallas_call(
-        conv_kernel,
-        grid=(lat_rows // GROUP,),
-        out_shape=jax.ShapeDtypeStruct((lat_rows, cols, chans), BF),
-        in_specs=[pl.BlockSpec(memory_space=pltpu.SMEM)] + [whole] * 7,
-        out_specs=pl.BlockSpec((GROUP, cols, chans), lambda g: (g, 0, 0)),
+    out, _ = pl.pallas_call(
+        functools.partial(finish_kernel, lat_count),
+        grid=(lat_rows // FINISH,),
+        out_shape=(
+            jax.ShapeDtypeStruct((lat_rows, cols, chans), BF),
+            jax.ShapeDtypeStruct(hid.shape, BF),
+        ),
+        in_specs=[whole] * (4 + len(sides)),
+        out_specs=(pl.BlockSpec((FINISH, cols, chans), lambda g: (g, 0, 0)), whole),
+        input_output_aliases={0: 1},
         scratch_shapes=[
-            pltpu.VMEM(((lat_rows + 4) * wide, 3 * chans), BF),
-            pltpu.VMEM(((lat_rows + 2) * wide, 3 * chans), BF),
-            pltpu.VMEM((4, west.shape[1], chans), F32),
+            pltpu.VMEM((8 * wide, 3 * chans), BF),
+            pltpu.VMEM((4, sides[0].shape[1], chans), F32),
         ],
-        compiler_params=params(44),
-    )(poles, first, west, east, north, south, one, two)
+        compiler_params=params(26),
+    )(hid, first, *sides, one, two)
+    return out
 
 
 def row_pairs(lat_count, lon_count):
     half = lon_count // 2
-
-    def flat(lat, lon):
-        return lat * lon_count + lon % lon_count
-
     inner, outer = [], []
     for lon in range(lon_count):
         for lat in range(0, lat_count, 2):
-            inner += [(flat(lat, lon), flat(lat + 1, lon)), (flat(lat + 1, lon), flat(lat, lon))]
+            inner += [((lat, lon), (lat + 1, lon)), ((lat + 1, lon), (lat, lon))]
         for lat in range(1, lat_count - 1, 2):
-            outer += [(flat(lat, lon), flat(lat + 1, lon)), (flat(lat + 1, lon), flat(lat, lon))]
-        outer += [(flat(lat, lon), flat(lat, lon + half)) for lat in (0, lat_count - 1)]
+            outer += [((lat, lon), (lat + 1, lon)), ((lat + 1, lon), (lat, lon))]
+        outer += [((lat, lon), (lat, lon + half)) for lat in (0, lat_count - 1)]
     return inner, outer
 
 
@@ -384,37 +501,36 @@
         lat_rows // BAND,
     )
     recv = lax.all_to_all(send, axes, split_axis=0, concat_axis=0, tiled=True)
-    first, edges = gridded(recv, background, w_in, w_bg, w_dens.reshape(1, chans), cap, wide)
-    west = lax.ppermute(edges[2:4], "lon", [(i, (i + 1) % lon_count) for i in range(lon_count)])
-    east = lax.ppermute(edges[0:2], "lon", [((i + 1) % lon_count, i) for i in range(lon_count)])
-    lat_index = lax.axis_index("lat")
-    even = lat_index % 2 == 0
-
-    def rows_at(near, far):
-        body = jnp.stack([first[near], first[far]])[:, 2 : cols + 2]
-        left = jnp.stack([west[:, near], west[:, far]])
-        right = jnp.stack([east[:, near], east[:, far]])
-        fill = jnp.zeros((2, wide - cols - 4, chans), BF)
-        return jnp.concatenate([left, body, right, fill], axis=1)
-
-    top, bottom = rows_at(0, 1), rows_at(lat_rows - 1, lat_rows - 2)
+    back, w_in, w_dens = projected(background, w_in, w_bg, w_dens.reshape(1, chans), wide)
+    first, own_west, own_east, inner_row, outer_row, corners = gridded(
+        recv, back, w_in, w_dens, cap, wide, lat_rows, cols
+    )
     inner, outer = row_pairs(lat_count, lon_count)
-    by_inner = lax.ppermute(jnp.where(even, bottom, top), axes, inner)
-    by_outer = lax.ppermute(jnp.where(even, top, bottom), axes, outer)
-    north = jnp.where(even, by_outer, by_inner)
-    south = jnp.where(even, by_inner, by_outer)
-    poles = jnp.stack([lat_index == 0, lat_index == lat_count - 1]).astype(jnp.int32)
-    return convolved(
-        poles,
-        first,
-        west,
-        east,
-        north,
-        south,
-        conv_one.reshape(3, 3 * chans, chans),
-        conv_two.reshape(3, 3 * chans, chans),
-        cols,
+
+    def moved(value, pairs, turn):
+        flat = [
+            (source[0] * lon_count + source[1], to[0] * lon_count + (to[1] + turn) % lon_count)
+            for source, to in pairs
+        ]
+        return lax.ppermute(value, axes, flat)
+
+    here = [((lat, lon), (lat, lon)) for lat in range(lat_count) for lon in range(lon_count)]
+    sides = (
+        own_west,
+        own_east,
+        moved(own_east, here, 1),
+        moved(own_west, here, -1),
+        moved(inner_row, inner, 0),
+        moved(outer_row, outer, 0),
+        moved(corners[1], inner, 1),
+        moved(corners[0], inner, -1),
+        moved(corners[3], outer, 1),
+        moved(corners[2], outer, -1),
     )
+    one = conv_one.reshape(3, 3 * chans, chans)
+    two = conv_two.reshape(3, 3 * chans, chans)
+    hid = inside(first, one)
+    return finished(hid, first, sides, one, two, cols, lat_count)
 
 
 def solution(mesh):

time: 113 us -> 116 us (1.027)
  waiting for transfers between devices: 40.1 us -> 25.7 us
  starting transfers between devices: 9.11 us -> 21.8 us
  local copies, waits for them, and re-layouts: 5.14 us -> 13.9 us
  Pallas kernels: 57.2 us -> 53.3 us
    ppermute x4 -> x8, starting transfers between devices: 1.82 us -> 14.4 us  [moved(): return lax.ppermute(value, axes, flat)]
    all_to_all x1, waiting for transfers between devices: 30.3 us -> 20.2 us  [shards(): recv = lax.all_to_all(send, axes, split_axis=0, concat_axis=0, tiled=True)]
    unnamed x12 -> x20, local copies, waits for them, and re-layouts: 4.69 us -> 13.9 us
    ppermute x4 -> x8, waiting for transfers between devices: 9.79 us -> 5.4 us  [moved(): return lax.ppermute(value, axes, flat)]
    pallas_call x2 -> x4, Pallas kernels: 49.9 us -> 46 us  [the longest x1 15.6 us: inside(): pl.pallas_call(functools.partial(inside_kernel, split), out_shape=jax.Sha...]
  transfers between devices with their start and end apart: 5 -> 9, of which waited for: 4 -> 4; matrix products, arithmetic and copies ran while one was open for 0% -> 0% of each run, Pallas kernels for 0% -> 15%
where the time goes in v3:
time: 116 us; the launch traced here: 115 us
  Pallas kernels  53.3 us (46%)
  waiting for transfers between devices  25.7 us (22%)
  starting transfers between devices  21.8 us (19%)
  local copies, waits for them, and re-layouts  13.9 us (12%)
    all_to_all x1, waiting for transfers between devices, shards(): recv = lax.all_to_all(send, axes, split_axis=0, concat_axis=0, tiled=True)  20.2 us
    pallas_call x1, Pallas kernels, inside(): pl.pallas_call(functools.partial(inside_kernel, split), out_shape=jax.Sha...  15.6 us
    pallas_call x1, Pallas kernels, finished(): pl.pallas_call(functools.partial(finish_kernel, lat_count), grid=(lat_row...  15.2 us
    ppermute x8, starting transfers between devices, moved(): return lax.ppermute(value, axes, flat)  14.4 us
    unnamed x20, local copies, waits for them, and re-layouts  13.9 us
    pallas_call x1, Pallas kernels, gridded(): pl.pallas_call(functools.partial(grid_kernel, devices, cap, wide, cols, l...  13.2 us
    pallas_call x1, Pallas kernels, pack(): pl.pallas_call(functools.partial(pack_kernel, devices, cap, cols, bands),...  7.31 us
    all_to_all x1, starting transfers between devices, shards(): recv = lax.all_to_all(send, axes, split_axis=0, concat_axis=0, tiled=True)  7.31 us
  transfers between devices with their start and end apart: 9, of which 4 were waited for; matrix products, arithmetic and copies ran while one was open for 0% of the time, Pallas kernels for 15%

profile of v3, /device:TPU:0, one launch (start us, length us, event | category | flops | bytes accessed | tf_op | source)
XLA Modules:
  0.0 115.4 jit_solution(1388456029225579592)
XLA Ops:
  0.7 7.3 %shard_map.109 = bf16[32,144,128]{2,1,0:T(8,128)(2,1)} custom-call(s32[1]{0:T(128)S(6)} %copy.14.count_ref, s32[1,2048]{1,0:T(1,128)} %bitcast.20, s32[4,2048]{1,0:T(4,128)} %bitcast.18, s32[4,2048]{1,0:T(4,128)} %bitcast.19, bf16[2048,128]{1,0:T(8,128)(2,1)} %feat_ref.1), custom_call_target="tpu_custom_call" | custom-call | tf_op jit(solution)/shard_map/pallas_call | solution.py:114
  8.0 7.3 %all-to-all-start = ((bf16[32,144,128]{2,1,0:T(8,128)(2,1)}), bf16[32,144,128]{2,1,0:T(8,128)(2,1)S(1)}, u32[]{:S(2)}, u32[]{:S(2)}) async-start(bf16[32,144,128]{2,1,0:T(8,128)(2,1)} %shard_map.109), calls=%async_computation | async-start | bytes 2359296 | tf_op jit(solution)/shard_map/all_to_all | solution.py:503
  15.3 0.0 copy-start.5
  15.3 2.2 %copy-done.5 = bf16[90,90,256]{2,1,0:T(8,128)(2,1)S(1)} copy-done((bf16[90,90,256]{2,1,0:T(8,128)(2,1)S(1)}, bf16[90,90,256]{2,1,0:T(8,128)(2,1)}, u32[]{:S(2)}) %copy-start.5) | copy-done | bytes 4147224
  17.5 0.9 copy-done.7
  18.5 0.8 copy-done.8
  19.3 0.7 copy-done.9
  20.0 2.0 %shard_map.110 = (f32[8640,256]{1,0:T(8,128)S(1)}, bf16[128,256]{1,0:T(8,128)(2,1)S(1)}, f32[1,256]{1,0:T(1,128)S(1)}) custom-call(bf16[90,90,256]{2,1,0:T(8,128)(2,1)S(1)} %copy-done.5, bf16[128,256]{1,0:T(8,128)(2,1)S(1)} %copy-done.8, bf16[256,256]{1,0:T(8,128)(2,1)S(1)} %copy-done.7, f32[1,256]{1,0:T(1,128)S(1)} %bitcast.17), custom_call_target="tpu_custom_call" | custom-call | tf_op jit(solution)/shard_map/pallas_call | solution.py:145
  22.0 3.4 %copy-done = f32[8640,256]{1,0:T(8,128)} copy-done((f32[8640,256]{1,0:T(8,128)}, f32[8640,256]{1,0:T(8,128)S(1)}, u32[]{:S(2)}) %copy-start) | copy-done | bytes 8847384
  25.4 20.2 %all-to-all-done.recv_ref = bf16[32,144,128]{2,1,0:T(8,128)(2,1)S(1)} async-done(((bf16[32,144,128]{2,1,0:T(8,128)(2,1)}), bf16[32,144,128]{2,1,0:T(8,128)(2,1)S(1)}, u32[]{:S(2)}, u32[]{:S(2)}) %all-to-all-start) | async-done | bytes 1179680 | tf_op jit(solution)/shard_map/all_to_all | solution.py:503
  45.7 1.0 copy-done.3
  46.7 3.5 %copy-done.1 = f32[8640,256]{1,0:T(8,128)S(1)} copy-done((f32[8640,256]{1,0:T(8,128)S(1)}, f32[8640,256]{1,0:T(8,128)}, u32[]{:S(2)}) %copy-start.1) | copy-done | bytes 8847384
  50.2 1.3 %copy-done.4 = bf16[32,144,128]{2,1,0:T(8,128)(2,1)S(1)} copy-done((bf16[32,144,128]{2,1,0:T(8,128)(2,1)S(1)}, bf16[32,144,128]{2,1,0:T(8,128)(2,1)}, u32[]{:S(2)}) %copy-start.4) | copy-done | bytes 1179672
  51.5 13.2 %shard_map.111 = (bf16[90,96,256]{2,1,0:T(8,128)(2,1)S(1)}, bf16[2,96,256]{2,1,0:T(8,128)(2,1)S(1)}, bf16[2,96,256]{2,1,0:T(8,128)(2,1)S(1)}, bf16[2,96,256]{2,1...) custom-call(bf16[32,144,128]{2,1,0:T(8,128)(2,1)S(1)} %copy-done.4, ...), custom_call_target="tpu_custom_call" | custom-call | tf_op jit(solution)/shard_map/pallas_call | solution.py:277
  64.7 2.1 %collective-permute-start.2 = (bf16[2,96,256]{2,1,0:T(8,128)(2,1)S(1)}, bf16[2,96,256]{2,1,0:T(8,128)(2,1)S(1)}, u32[]{:S(2)}, u32[]{:S(2)}) collective-permute-start(bf16[2,96,256]{2,1,0:T(8,128)(2,1)S(1)} %get-tuple-element.21), channel_id=1, source_target_pairs={{0,8},{8,0},{16,24},{24,16},{1,9},{9,1},{17,25},{25,17},{2,10},{10... | collective-permute-start | bytes 294920 | tf_op jit(solution)/shard_map/ppermute | solution.py:515
  66.8 0.5 collective-permute-start
  67.4 2.7 %collective-permute-start.7 = (bf16[2,16,256]{2,1,0:T(8,128)(2,1)S(1)}, bf16[2,16,256]{2,1,0:T(8,128)(2,1)S(1)}, u32[]{:S(2)}, u32[]{:S(2)}) collective-permute-start(bf16[2,16,256]{2,1,0:T(8,128)(2,1)S(1)} %get-tuple-element.25), channel_id=1, source_target_pairs={{8,23},{16,15},{0,3},{24,27},{9,16},{17,8},{1,4},{25,28},{10,17},{... | collective-permute-start | bytes 49160 | tf_op jit(solution)/shard_map/ppermute | solution.py:515
  70.1 2.5 %collective-permute-done.7.outer_right = bf16[2,16,256]{2,1,0:T(8,128)(2,1)S(1)} collective-permute-done((bf16[2,16,256]{2,1,0:T(8,128)(2,1)S(1)}, bf16[2,16,256]{2,1,0:T(8,128)(2,1)S(1)}, u32[]{:S(2)}, u32[]{:S(2)}) %collective-permute-start.7) | collective-permute-done | bytes 16416 | tf_op jit(solution)/shard_map/ppermute | solution.py:515
  72.6 3.6 %collective-permute-start.6 = (bf16[2,16,256]{2,1,0:T(8,128)(2,1)S(1)}, bf16[2,16,256]{2,1,0:T(8,128)(2,1)S(1)}, u32[]{:S(2)}, u32[]{:S(2)}) collective-permute-start(bf16[2,16,256]{2,1,0:T(8,128)(2,1)S(1)} %get-tuple-element.26), channel_id=1, source_target_pairs={{8,17},{16,9},{0,5},{24,29},{9,18},{17,10},{1,6},{25,30},{10,19},{... | collective-permute-start | bytes 49160 | tf_op jit(solution)/shard_map/ppermute | solution.py:515
  76.2 1.4 %collective-permute-done.6.outer_left = bf16[2,16,256]{2,1,0:T(8,128)(2,1)S(1)} collective-permute-done((bf16[2,16,256]{2,1,0:T(8,128)(2,1)S(1)}, bf16[2,16,256]{2,1,0:T(8,128)(2,1)S(1)}, u32[]{:S(2)}, u32[]{:S(2)}) %collective-permute-start.6) | collective-permute-done | bytes 16416 | tf_op jit(solution)/shard_map/ppermute | solution.py:515
  77.6 5.5 %collective-permute-start.5 = (bf16[2,16,256]{2,1,0:T(8,128)(2,1)S(1)}, bf16[2,16,256]{2,1,0:T(8,128)(2,1)S(1)}, u32[]{:S(2)}, u32[]{:S(2)}) collective-permute-start(bf16[2,16,256]{2,1,0:T(8,128)(2,1)S(1)} %get-tuple-element.27), channel_id=1, source_target_pairs={{0,15},{8,7},{16,31},{24,23},{1,8},{9,0},{17,24},{25,16},{2,9},{10... | collective-permute-start | bytes 49160 | tf_op jit(solution)/shard_map/ppermute | solution.py:515
  83.1 1.4 %collective-permute-done.5.inner_right = bf16[2,16,256]{2,1,0:T(8,128)(2,1)S(1)} collective-permute-done((bf16[2,16,256]{2,1,0:T(8,128)(2,1)S(1)}, bf16[2,16,256]{2,1,0:T(8,128)(2,1)S(1)}, u32[]{:S(2)}, u32[]{:S(2)}) %collective-permute-start.5) | collective-permute-done | bytes 16416 | tf_op jit(solution)/shard_map/ppermute | solution.py:515
  84.5 15.6 %shard_map.112.hid_in = bf16[8832,768]{1,0:T(8,128)(2,1)S(1)} custom-call(bf16[90,96,256]{2,1,0:T(8,128)(2,1)S(1)} %get-tuple-element.18.first_ref, bf16[3,768,256]{2,1,0:T(8,128)(2,1)S(1)} %bitcast.14), custom_call_target="tpu_custom_call" | custom-call | tf_op jit(solution)/shard_map/pallas_call | solution.py:340
  100.2 15.2 %shard_map.113 = (bf16[90,90,256]{2,1,0:T(8,128)(2,1)}, bf16[8832,768]{1,0:T(8,128)(2,1)S(1)}) custom-call(bf16[8832,768]{1,0:T(8,128)(2,1)S(1)} %shard_map.112.hid_in, bf16[90,96,256]{2,1,0:T(8,128)(2,1)S(1)} %get-tuple-element.18.first_ref, bf16[2,96,256]{2,1,0:T(8,128)(2,1)S(1)} %get-tuple-element.19.own_west, ...), custom_call_target="tpu_custom_call", output_to_operand_aliasing={{1}: (0, {})} | custom-call | tf_op jit(solution)/shard_map/pallas_call | solution.py:448
  (20 shorter events, 0.0 us)
Async XLA Ops:
  8.0 37.7 %all-to-all-start = ((bf16[32,144,128]{2,1,0:T(8,128)(2,1)}), bf16[32,144,128]{2,1,0:T(8,128)(2,1)S(1)}, u32[]{:S(2)}, u32[]{:S(2)}) async-start(bf16[32,144,128]{2,1,0:T(8,128)(2,1)} %shard_map.109), calls=%async_computation | async-start | bytes 2359296 | tf_op jit(solution)/shard_map/all_to_all | solution.py:503
  15.3 2.3 %copy-start.5 = (bf16[90,90,256]{2,1,0:T(8,128)(2,1)S(1)}, bf16[90,90,256]{2,1,0:T(8,128)(2,1)}, u32[]{:S(2)}) copy-start(bf16[90,90,256]{2,1,0:T(8,128)(2,1)} %back_ref.1) | copy-start | bytes 12441604
  17.5 0.9 copy-start.7
  18.4 0.8 copy-start.8
  19.3 0.7 copy-start.9
  22.0 3.4 %copy-start = (f32[8640,256]{1,0:T(8,128)}, f32[8640,256]{1,0:T(8,128)S(1)}, u32[]{:S(2)}) copy-start(f32[8640,256]{1,0:T(8,128)S(1)} %get-tuple-element.15.back_ref) | copy-start | bytes 26542084
  45.7 1.0 copy-start.3
  46.7 3.5 %copy-start.1 = (f32[8640,256]{1,0:T(8,128)S(1)}, f32[8640,256]{1,0:T(8,128)}, u32[]{:S(2)}) copy-start(f32[8640,256]{1,0:T(8,128)} %copy-done) | copy-start | bytes 26542084
  50.2 1.3 %copy-start.4 = (bf16[32,144,128]{2,1,0:T(8,128)(2,1)S(1)}, bf16[32,144,128]{2,1,0:T(8,128)(2,1)}, u32[]{:S(2)}) copy-start(bf16[32,144,128]{2,1,0:T(8,128)(2,1)} %copy-done.3) | copy-start | bytes 3538948
  51.5 33.1 %copy-start.2 = (bf16[3,3,256,256]{3,2,1,0:T(8,128)(2,1)S(1)}, bf16[3,3,256,256]{3,2,1,0:T(8,128)(2,1)}, u32[]{:S(2)}) copy-start(bf16[3,3,256,256]{3,2,1,0:T(8,128)(2,1)} %param.20) | copy-start | bytes 3538948
  64.7 35.5 %collective-permute-start.2 = (bf16[2,96,256]{2,1,0:T(8,128)(2,1)S(1)}, bf16[2,96,256]{2,1,0:T(8,128)(2,1)S(1)}, u32[]{:S(2)}, u32[]{:S(2)}) collective-permute-start(bf16[2,96,256]{2,1,0:T(8,128)(2,1)S(1)} %get-tuple-element.21), channel_id=1, source_target_pairs={{0,8},{8,0},{16,24},{24,16},{1,9},{9,1},{17,25},{25,17},{2,10},{10... | collective-permute-start | bytes 294920 | tf_op jit(solution)/shard_map/ppermute | solution.py:515
  66.8 33.3 %collective-permute-start.3 = (bf16[2,96,256]{2,1,0:T(8,128)(2,1)S(1)}, bf16[2,96,256]{2,1,0:T(8,128)(2,1)S(1)}, u32[]{:S(2)}, u32[]{:S(2)}) collective-permute-start(bf16[2,96,256]{2,1,0:T(8,128)(2,1)S(1)} %get-tuple-element.22), channel_id=1, source_target_pairs={{8,16},{16,8},{0,4},{24,28},{9,17},{17,9},{1,5},{25,29},{10,18},{1... | collective-permute-start | bytes 294920 | tf_op jit(solution)/shard_map/ppermute | solution.py:515
  66.8 33.3 %collective-permute-start.1 = (bf16[2,96,256]{2,1,0:T(8,128)(2,1)S(1)}, bf16[2,96,256]{2,1,0:T(8,128)(2,1)S(1)}, u32[]{:S(2)}, u32[]{:S(2)}) collective-permute-start(bf16[2,96,256]{2,1,0:T(8,128)(2,1)S(1)} %get-tuple-element.19.own_west), channel_id=1, source_target_pairs={{0,7},{1,0},{2,1},{3,2},{4,3},{5,4},{6,5},{7,6},{8,15},{9,8},{10,9... | collective-permute-start | bytes 294920 | tf_op jit(solution)/shard_map/ppermute | solution.py:515
  66.8 33.3 %collective-permute-start = (bf16[2,96,256]{2,1,0:T(8,128)(2,1)S(1)}, bf16[2,96,256]{2,1,0:T(8,128)(2,1)S(1)}, u32[]{:S(2)}, u32[]{:S(2)}) collective-permute-start(bf16[2,96,256]{2,1,0:T(8,128)(2,1)S(1)} %get-tuple-element.20.own_east), channel_id=1, source_target_pairs={{0,1},{1,2},{2,3},{3,4},{4,5},{5,6},{6,7},{7,0},{8,9},{9,10},{10,1... | collective-permute-start | bytes 294920 | tf_op jit(solution)/shard_map/ppermute | solution.py:515
  67.4 5.2 %collective-permute-start.7 = (bf16[2,16,256]{2,1,0:T(8,128)(2,1)S(1)}, bf16[2,16,256]{2,1,0:T(8,128)(2,1)S(1)}, u32[]{:S(2)}, u32[]{:S(2)}) collective-permute-start(bf16[2,16,256]{2,1,0:T(8,128)(2,1)S(1)} %get-tuple-element.25), channel_id=1, source_target_pairs={{8,23},{16,15},{0,3},{24,27},{9,16},{17,8},{1,4},{25,28},{10,17},{... | collective-permute-start | bytes 49160 | tf_op jit(solution)/shard_map/ppermute | solution.py:515
  72.6 5.1 %collective-permute-start.6 = (bf16[2,16,256]{2,1,0:T(8,128)(2,1)S(1)}, bf16[2,16,256]{2,1,0:T(8,128)(2,1)S(1)}, u32[]{:S(2)}, u32[]{:S(2)}) collective-permute-start(bf16[2,16,256]{2,1,0:T(8,128)(2,1)S(1)} %get-tuple-element.26), channel_id=1, source_target_pairs={{8,17},{16,9},{0,5},{24,29},{9,18},{17,10},{1,6},{25,30},{10,19},{... | collective-permute-start | bytes 49160 | tf_op jit(solution)/shard_map/ppermute | solution.py:515
  77.6 6.9 %collective-permute-start.5 = (bf16[2,16,256]{2,1,0:T(8,128)(2,1)S(1)}, bf16[2,16,256]{2,1,0:T(8,128)(2,1)S(1)}, u32[]{:S(2)}, u32[]{:S(2)}) collective-permute-start(bf16[2,16,256]{2,1,0:T(8,128)(2,1)S(1)} %get-tuple-element.27), channel_id=1, source_target_pairs={{0,15},{8,7},{16,31},{24,23},{1,8},{9,0},{17,24},{25,16},{2,9},{10... | collective-permute-start | bytes 49160 | tf_op jit(solution)/shard_map/ppermute | solution.py:515
  84.5 15.6 %collective-permute-start.4 = (bf16[2,16,256]{2,1,0:T(8,128)(2,1)S(1)}, bf16[2,16,256]{2,1,0:T(8,128)(2,1)S(1)}, u32[]{:S(2)}, u32[]{:S(2)}) collective-permute-start(bf16[2,16,256]{2,1,0:T(8,128)(2,1)S(1)} %get-tuple-element.28), channel_id=1, source_target_pairs={{0,9},{8,1},{16,25},{24,17},{1,10},{9,2},{17,26},{25,18},{2,11},{1... | collective-permute-start | bytes 49160 | tf_op jit(solution)/shard_map/ppermute | solution.py:515
  84.5 15.6 %copy-start.6 = (bf16[3,3,256,256]{3,2,1,0:T(8,128)(2,1)S(1)}, bf16[3,3,256,256]{3,2,1,0:T(8,128)(2,1)}, u32[]{:S(2)}) copy-start(bf16[3,3,256,256]{3,2,1,0:T(8,128)(2,1)} %param.21) | copy-start | bytes 3538948

commit v4 on v3

--- a/solution.py
+++ b/solution.py
@@ -128,39 +128,35 @@
     )(count, dest, cells, gauss, feats)
 
 
-def back_kernel(wide, back_ref, w_in_ref, w_bg_ref, w_dens_ref, out_ref, w_in_out, w_dens_out, scr):
-    band = pl.program_id(0)
+def back_kernel(wide, back_ref, w_bg_ref, out_ref, scr):
     rows, cols, chans = back_ref.shape
     for i in range(rows):
         scr[i * wide : i * wide + cols, :] = back_ref[i]
-    begin = pl.multiple_of(band * rows * wide, 16)
-    out_ref[pl.ds(begin, rows * wide), :] = pltpu.roll(dot(scr[...], w_bg_ref[...]), 2, axis=0)
-    w_in_out[...] = w_in_ref[...]
-    w_dens_out[...] = w_dens_ref[...]
-
-
-def projected(background, w_in, w_bg, w_dens, wide):
+    out_ref[...] = pltpu.roll(dot(scr[...], w_bg_ref[...]), 2, axis=0)
+
+
+def projected(background, w_bg, wide):
     lat_rows, cols, chans = background.shape
-    whole = pl.BlockSpec(memory_space=pltpu.VMEM)
+    length = max(lat_rows * wide, 1 << 16) + 16
     return pl.pallas_call(
         functools.partial(back_kernel, wide),
         grid=(lat_rows // BAND,),
-        out_shape=(
-            jax.ShapeDtypeStruct((lat_rows * wide, chans), F32),
-            jax.ShapeDtypeStruct(w_in.shape, BF),
-            jax.ShapeDtypeStruct(w_dens.shape, F32),
-        ),
-        in_specs=[pl.BlockSpec((BAND, cols, chans), lambda g: (g, 0, 0)), whole, whole, whole],
-        out_specs=(whole, whole, whole),
+        out_shape=pltpu.HBM((length, chans), F32),
+        in_specs=[
+            pl.BlockSpec((BAND, cols, chans), lambda g: (g, 0, 0)),
+            pl.BlockSpec(memory_space=pltpu.VMEM),
+        ],
+        out_specs=pl.BlockSpec((BAND * wide, chans), lambda g: (g, 0)),
         scratch_shapes=[pltpu.VMEM((BAND * wide, chans), BF)],
         compiler_params=params(24),
-    )(background, w_in, w_bg, w_dens)
+    )(background, w_bg)
 
 
 def grid_kernel(
-    devices, cap, wide, cols, lat_bands, recv_ref, back_ref, w_in_ref, w_dens_ref,
-    first_ref, west_ref, east_ref, inner_ref, outer_ref, corner_ref,
+    devices, cap, wide, cols, lat_bands, recv_ref, back_hbm, w_in_hbm, w_dens_hbm,
+    first_ref, west_ref, east_ref, inner_ref, outer_ref,
     rows_ref, lats_ref, feat_ref, meta_ref, acc_ref, edge_scr, ends_ref, ends_smem, sem,
+    back_ref, w_in_ref, w_dens_ref, sems,
 ):
     band = pl.program_id(0)
     bands = pl.num_programs(0)
@@ -168,9 +164,20 @@
     lat_rows, _, chans = first_ref.shape
     rows = lat_rows // lat_bands
     slots = devices * cap
+    span = rows * wide
+    fetch = pltpu.make_async_copy(
+        back_hbm.at[pl.ds(pl.multiple_of(band * span, 16), span), :], back_ref, sems.at[0]
+    )
+    fetch.start()
+    loads = [
+        pltpu.make_async_copy(w_in_hbm, w_in_ref, sems.at[1]),
+        pltpu.make_async_copy(w_dens_hbm, w_dens_ref, sems.at[2]),
+    ]
 
     @pl.when(band == 0)
     def _():
+        for load in loads:
+            load.start()
         feat_ref[...] = jnp.zeros(feat_ref.shape, F32)
         rows_ref[slots:, :] = jnp.zeros((rows_ref.shape[0] - slots, nfeat), F32)
 
@@ -237,10 +244,16 @@
         return 0
 
     lax.fori_loop(0, (total + CHUNK - 1) // CHUNK, chunk, 0)
+    fetch.wait()
+
+    @pl.when(band == 0)
+    def _():
+        for load in loads:
+            load.wait()
+
     for g in range(0, rows, GROUP):
         sums = acc_ref[g * wide : (g + GROUP) * wide, :]
-        begin = pl.multiple_of((band * rows + g) * wide, 16)
-        start = back_ref[pl.ds(begin, GROUP * wide), :]
+        start = back_ref[g * wide : (g + GROUP) * wide, :]
         density = sums[:, nfeat:]
         normalized = (sums[:, :nfeat] / (density + 1.0)).astype(BF)
         start = start + dot(normalized, w_in_ref[...])
@@ -262,10 +275,6 @@
             outer = jnp.where(even, top, bottom).astype(BF)
             inner_ref[k] = inner
             outer_ref[k] = outer
-            corner_ref[0, k] = inner[:16]
-            corner_ref[1, k] = inner[wide - 16 :]
-            corner_ref[2, k] = outer[:16]
-            corner_ref[3, k] = outer[wide - 16 :]
 
 
 def gridded(recv, back, w_in, w_dens, cap, wide, lat_rows, cols):
@@ -283,10 +292,9 @@
             jax.ShapeDtypeStruct((2, tall, chans), BF),
             jax.ShapeDtypeStruct((2, wide, chans), BF),
             jax.ShapeDtypeStruct((2, wide, chans), BF),
-            jax.ShapeDtypeStruct((4, 2, 16, chans), BF),
         ),
-        in_specs=[whole] * 4,
-        out_specs=(whole,) * 6,
+        in_specs=[whole] + [pl.BlockSpec(memory_space=pltpu.HBM)] * 3,
+        out_specs=(whole,) * 5,
         scratch_shapes=[
             pltpu.VMEM((slots + cap, nfeat), F32),
             pltpu.VMEM((devices, nfeat), F32),
@@ -297,6 +305,10 @@
             pltpu.VMEM((devices, nfeat), jnp.int32),
             pltpu.SMEM((devices, nfeat), jnp.int32),
             pltpu.SemaphoreType.DMA,
+            pltpu.VMEM((BAND * wide, chans), F32),
+            pltpu.VMEM(w_in.shape, BF),
+            pltpu.VMEM(w_dens.shape, F32),
+            pltpu.SemaphoreType.DMA((3,)),
         ],
         compiler_params=params(32),
     )(recv, back, w_in, w_dens)
@@ -314,7 +326,36 @@
     return dot(field, w_ref[...].reshape(field.shape[1], w_ref.shape[2]))
 
 
-def inside_kernel(split, first_ref, one_ref, hid_ref, field):
+def border_kernel(lat_rows, cols, inner_ref, outer_ref, west_ref, east_ref, inner_out, outer_out):
+    _, wide, chans = inner_ref.shape
+    even = lax.axis_index("lat") % 2 == 0
+    row_id = lax.broadcasted_iota(jnp.int32, (wide, chans), 0)
+    sides = [west_ref[0], west_ref[1], east_ref[0], east_ref[1]]
+    sides = [side.astype(F32) for side in sides]
+    for k in range(2):
+        inner, outer = inner_ref[k].astype(F32), outer_ref[k].astype(F32)
+        for side, col in zip(sides, (0, 1, cols + 2, cols + 3)):
+            top = side[k : k + 1]
+            bottom = side[lat_rows - 1 - k : lat_rows - k]
+            inner = jnp.where(row_id == col, jnp.where(even, bottom, top), inner)
+            outer = jnp.where(row_id == col, jnp.where(even, top, bottom), outer)
+        inner_out[k] = inner.astype(BF)
+        outer_out[k] = outer.astype(BF)
+
+
+def bordered(inner, outer, west, east, lat_rows, cols):
+    whole = pl.BlockSpec(memory_space=pltpu.VMEM)
+    shape = jax.ShapeDtypeStruct(inner.shape, BF)
+    return pl.pallas_call(
+        functools.partial(border_kernel, lat_rows, cols),
+        out_shape=(shape, shape),
+        in_specs=[whole] * 4,
+        out_specs=(whole, whole),
+        compiler_params=params(24),
+    )(inner, outer, west, east)
+
+
+def inside_kernel(split, first_ref, one_ref, after_ref, hid_ref, field):
     lat_rows, wide, chans = first_ref.shape
 
     def load(r, _):
@@ -333,23 +374,23 @@
     lax.fori_loop(0, split, hidden, 0)
 
 
-def inside(first, one):
+def inside(first, one, after):
     lat_rows, wide, chans = first.shape
     whole = pl.BlockSpec(memory_space=pltpu.VMEM)
     split = next(n for n in (4, 2, 1) if (lat_rows - 2) % n == 0)
     return pl.pallas_call(
         functools.partial(inside_kernel, split),
         out_shape=jax.ShapeDtypeStruct(((lat_rows + 2) * wide, 3 * chans), BF),
-        in_specs=[whole] * 2,
+        in_specs=[whole, whole, pl.BlockSpec(memory_space=pl.ANY)],
         out_specs=whole,
         scratch_shapes=[pltpu.VMEM((lat_rows * wide, 3 * chans), BF)],
         compiler_params=params(30),
-    )(first, one)
+    )(first, one, after)
 
 
 def finish_kernel(
     lat_count, hid_in, first_ref, own_west, own_east, west_ref, east_ref, inner_ref, outer_ref,
-    inner_left, inner_right, outer_left, outer_right, one_ref, two_ref, out_ref, hid_ref, rim, cols_scr,
+    one_ref, two_ref, out_ref, hid_ref, rim, cols_scr,
 ):
     group = pl.program_id(0)
     lat_rows, wide, chans = first_ref.shape
@@ -363,17 +404,8 @@
         row_id = lax.broadcasted_iota(jnp.int32, (wide, chans), 0)
         short_id = lax.broadcasted_iota(jnp.int32, (16, chans), 0)
 
-        def edge_row(first_half, k):
-            def pick(inner, outer):
-                return jnp.where(even == first_half, outer[k].astype(F32), inner[k].astype(F32))
-
-            middle = pick(inner_ref, outer_ref)
-            left = pltpu.roll(pick(inner_left, outer_left), (wide - cols) % 16, axis=0)
-            right = pltpu.roll(pick(inner_right, outer_right), (cols - (wide - 16)) % 16, axis=0)
-            head = jnp.where(short_id < 2, left, middle[:16])
-            at = short_id + (wide - 16)
-            tail = jnp.where((at == cols + 2) | (at == cols + 3), right, middle[wide - 16 :])
-            return jnp.concatenate([head, middle[16 : wide - 16], tail], axis=0)
+        def edge_row(north, k):
+            return jnp.where(even == north, outer_ref[k].astype(F32), inner_ref[k].astype(F32))
 
         def own_row(r):
             value = first_ref[r].astype(F32)
@@ -466,13 +498,17 @@
 
 def row_pairs(lat_count, lon_count):
     half = lon_count // 2
+
+    def flat(lat, lon):
+        return lat * lon_count + lon % lon_count
+
     inner, outer = [], []
     for lon in range(lon_count):
         for lat in range(0, lat_count, 2):
-            inner += [((lat, lon), (lat + 1, lon)), ((lat + 1, lon), (lat, lon))]
+            inner += [(flat(lat, lon), flat(lat + 1, lon)), (flat(lat + 1, lon), flat(lat, lon))]
         for lat in range(1, lat_count - 1, 2):
-            outer += [((lat, lon), (lat + 1, lon)), ((lat + 1, lon), (lat, lon))]
-        outer += [((lat, lon), (lat, lon + half)) for lat in (0, lat_count - 1)]
+            outer += [(flat(lat, lon), flat(lat + 1, lon)), (flat(lat + 1, lon), flat(lat, lon))]
+        outer += [(flat(lat, lon), flat(lat, lon + half)) for lat in (0, lat_count - 1)]
     return inner, outer
 
 
@@ -501,35 +537,20 @@
         lat_rows // BAND,
     )
     recv = lax.all_to_all(send, axes, split_axis=0, concat_axis=0, tiled=True)
-    back, w_in, w_dens = projected(background, w_in, w_bg, w_dens.reshape(1, chans), wide)
-    first, own_west, own_east, inner_row, outer_row, corners = gridded(
-        recv, back, w_in, w_dens, cap, wide, lat_rows, cols
+    back = projected(background, w_bg, wide)
+    first, own_west, own_east, inner_row, outer_row = gridded(
+        recv, back, w_in, w_dens.reshape(1, chans), cap, wide, lat_rows, cols
     )
-    inner, outer = row_pairs(lat_count, lon_count)
-
-    def moved(value, pairs, turn):
-        flat = [
-            (source[0] * lon_count + source[1], to[0] * lon_count + (to[1] + turn) % lon_count)
-            for source, to in pairs
-        ]
-        return lax.ppermute(value, axes, flat)
-
-    here = [((lat, lon), (lat, lon)) for lat in range(lat_count) for lon in range(lon_count)]
-    sides = (
-        own_west,
-        own_east,
-        moved(own_east, here, 1),
-        moved(own_west, here, -1),
-        moved(inner_row, inner, 0),
-        moved(outer_row, outer, 0),
-        moved(corners[1], inner, 1),
-        moved(corners[0], inner, -1),
-        moved(corners[3], outer, 1),
-        moved(corners[2], outer, -1),
-    )
+    west = lax.ppermute(own_east, "lon", [(i, (i + 1) % lon_count) for i in range(lon_count)])
+    east = lax.ppermute(own_west, "lon", [((i + 1) % lon_count, i) for i in range(lon_count)])
     one = conv_one.reshape(3, 3 * chans, chans)
     two = conv_two.reshape(3, 3 * chans, chans)
-    hid = inside(first, one)
+    inner_row, outer_row = bordered(inner_row, outer_row, west, east, lat_rows, cols)
+    inner, outer = row_pairs(lat_count, lon_count)
+    hid = inside(first, one, inner_row)
+    inner_row = lax.ppermute(inner_row, axes, inner)
+    outer_row = lax.ppermute(outer_row, axes, outer)
+    sides = (own_west, own_east, west, east, inner_row, outer_row)
     return finished(hid, first, sides, one, two, cols, lat_count)
 
 

time: 116 us -> 99 us (0.85)
  local copies, waits for them, and re-layouts: 13.9 us -> 3.17 us
  starting transfers between devices: 21.8 us -> 13.3 us
  Pallas kernels: 53.3 us -> 57.3 us
    unnamed x20 -> x12, local copies, waits for them, and re-layouts: 13.9 us -> 3.17 us
    ppermute x8 -> x4, starting transfers between devices: 14.4 us -> 6 us  [the longest x1 3.53 us: shards(): lax.ppermute(own_west, 'lon', [((i + 1) % lon_count, i) for i in range(lo...]
    ppermute x8 -> x4, waiting for transfers between devices: 5.4 us -> 2.41 us  [the longest x1 2.4 us: shards(): lax.ppermute(own_east, 'lon', [(i, (i + 1) % lon_count) for i in range(lo...]
    pallas_call x1, Pallas kernels: 2.03 us -> 4.97 us  [projected(): pl.pallas_call(functools.partial(back_kernel, wide), grid=(lat_rows // BA...]
    all_to_all x1, waiting for transfers between devices: 20.2 us -> 22.3 us  [shards(): recv = lax.all_to_all(send, axes, split_axis=0, concat_axis=0, tiled=True)]
  transfers between devices with their start and end apart: 9 -> 5, of which waited for: 4 -> 2; matrix products, arithmetic and copies ran while one was open for 0% -> 0% of each run, Pallas kernels for 15% -> 21%
where the time goes in v4:
time: 99 us; the launch traced here: 99.1 us
  Pallas kernels  57.3 us (58%)
  waiting for transfers between devices  24.7 us (25%)
  starting transfers between devices  13.3 us (13%)
  local copies, waits for them, and re-layouts  3.17 us (3%)
    all_to_all x1, waiting for transfers between devices, shards(): recv = lax.all_to_all(send, axes, split_axis=0, concat_axis=0, tiled=True)  22.3 us
    pallas_call x1, Pallas kernels, inside(): pl.pallas_call(functools.partial(inside_kernel, split), out_shape=jax.Sha...  15.6 us
    pallas_call x1, Pallas kernels, finished(): pl.pallas_call(functools.partial(finish_kernel, lat_count), grid=(lat_row...  15.2 us
    pallas_call x1, Pallas kernels, gridded(): pl.pallas_call(functools.partial(grid_kernel, devices, cap, wide, cols, l...  14.2 us
    pallas_call x1, Pallas kernels, pack(): pl.pallas_call(functools.partial(pack_kernel, devices, cap, cols, bands),...  7.32 us
    all_to_all x1, starting transfers between devices, shards(): recv = lax.all_to_all(send, axes, split_axis=0, concat_axis=0, tiled=True)  7.29 us
    pallas_call x1, Pallas kernels, projected(): pl.pallas_call(functools.partial(back_kernel, wide), grid=(lat_rows // BA...  4.97 us
    ppermute x1, starting transfers between devices, shards(): lax.ppermute(own_west, 'lon', [((i + 1) % lon_count, i) for i in range(lo...  3.53 us
  transfers between devices with their start and end apart: 5, of which 2 were waited for; matrix products, arithmetic and copies ran while one was open for 0% of the time, Pallas kernels for 21%

profile of v4, /device:TPU:0, one launch (start us, length us, event | category | flops | bytes accessed | tf_op | source)
XLA Modules:
  0.0 99.1 jit_solution(15447277017972896819)
XLA Ops:
  0.7 7.3 %shard_map.109 = bf16[32,144,128]{2,1,0:T(8,128)(2,1)} custom-call(s32[1]{0:T(128)S(6)} %copy.14.count_ref, s32[1,2048]{1,0:T(1,128)} %bitcast.12, s32[4,2048]{1,0:T(4,128)} %bitcast.10, s32[4,2048]{1,0:T(4,128)} %bitcast.11, bf16[2048,128]{1,0:T(8,128)(2,1)} %feat_ref.1), custom_call_target="tpu_custom_call" | custom-call | tf_op jit(solution)/shard_map/pallas_call | solution.py:114
  8.0 7.3 %all-to-all-start = ((bf16[32,144,128]{2,1,0:T(8,128)(2,1)}), bf16[32,144,128]{2,1,0:T(8,128)(2,1)S(1)}, u32[]{:S(2)}, u32[]{:S(2)}) async-start(bf16[32,144,128]{2,1,0:T(8,128)(2,1)} %shard_map.109), calls=%async_computation | async-start | bytes 2359296 | tf_op jit(solution)/shard_map/all_to_all | solution.py:539
  15.3 0.0 copy-start.1
  15.3 2.2 %copy-done.1 = bf16[90,90,256]{2,1,0:T(8,128)(2,1)S(1)} copy-done((bf16[90,90,256]{2,1,0:T(8,128)(2,1)S(1)}, bf16[90,90,256]{2,1,0:T(8,128)(2,1)}, u32[]{:S(2)}) %copy-start.1) | copy-done | bytes 4147224
  17.5 0.0 copy-start.3
  17.5 0.9 copy-done.3
  18.4 0.0 copy-start.4
  18.4 5.0 %shard_map.110.back_hbm = f32[65552,256]{1,0:T(8,128)} custom-call(bf16[90,90,256]{2,1,0:T(8,128)(2,1)S(1)} %copy-done.1, bf16[256,256]{1,0:T(8,128)(2,1)S(1)} %copy-done.3), custom_call_target="tpu_custom_call" | custom-call | tf_op jit(solution)/shard_map/pallas_call | solution.py:141
  23.4 22.3 %all-to-all-done.recv_ref = bf16[32,144,128]{2,1,0:T(8,128)(2,1)S(1)} async-done(((bf16[32,144,128]{2,1,0:T(8,128)(2,1)}), bf16[32,144,128]{2,1,0:T(8,128)(2,1)S(1)}, u32[]{:S(2)}, u32[]{:S(2)}) %all-to-all-start) | async-done | bytes 1179680 | tf_op jit(solution)/shard_map/all_to_all | solution.py:539
  45.7 0.0 copy-done.4
  45.7 0.0 copy-done.5
  45.7 14.2 %shard_map.111 = (bf16[90,96,256]{2,1,0:T(8,128)(2,1)S(1)}, bf16[2,96,256]{2,1,0:T(8,128)(2,1)S(1)}, bf16[2,96,256]{2,1,0:T(8,128)(2,1)S(1)}, bf16[2,96,256]{2,1,0:T(8,128)(2,1)S(1)}, bf16[2,96,256]{2,1,0:T(8,128)(2,1)S(1)}) custom-call(bf16[32,144,128]{2,1,0:T(8,128)(2,1)S(1)} %all-to-all-done.recv_ref, f32[65552,256]{1,0:T(8,128)} %shard_map.110.back_hbm, ...), custom_call_target="tpu_custom_call" | custom-call | tf_op jit(solution)/shard_map/pallas_call | solution.py:286
  59.9 0.1 collective-permute-start
  59.9 3.5 %collective-permute-start.1 = (bf16[2,96,256]{2,1,0:T(8,128)(2,1)S(1)}, bf16[2,96,256]{2,1,0:T(8,128)(2,1)S(1)}, u32[]{:S(2)}, u32[]{:S(2)}) collective-permute-start(bf16[2,96,256]{2,1,0:T(8,128)(2,1)S(1)} %get-tuple-element.17.own_west), channel_id=1, source_target_pairs={{1,0},{2,1},{3,2},{4,3},{5,4},{6,5},{7,6},{0,7},{9,8},{10,9},{11,1... | collective-permute-start | bytes 294920 | tf_op jit(solution)/shard_map/ppermute | solution.py:545
  63.5 2.4 %collective-permute-done.west_ref = bf16[2,96,256]{2,1,0:T(8,128)(2,1)S(1)} collective-permute-done((bf16[2,96,256]{2,1,0:T(8,128)(2,1)S(1)}, bf16[2,96,256]{2,1,0:T(8,128)(2,1)S(1)}, u32[]{:S(2)}, u32[]{:S(2)}) %collective-permute-start) | collective-permute-done | bytes 98336 | tf_op jit(solution)/shard_map/ppermute | solution.py:544
  65.9 0.0 collective-permute-done.1.east_ref
  65.9 0.1 collective-permute-start.3
  66.0 2.3 %collective-permute-start.2 = (bf16[2,96,256]{2,1,0:T(8,128)(2,1)S(1)}, bf16[2,96,256]{2,1,0:T(8,128)(2,1)S(1)}, u32[]{:S(2)}, u32[]{:S(2)}) collective-permute-start(bf16[2,96,256]{2,1,0:T(8,128)(2,1)S(1)} %get-tuple-element.18.after_ref), channel_id=1, source_target_pairs={{0,8},{8,0},{16,24},{24,16},{1,9},{9,1},{17,25},{25,17},{2,10},{10... | collective-permute-start | bytes 294920 | tf_op jit(solution)/shard_map/ppermute | solution.py:551
  68.3 0.0 copy-done
  68.4 15.6 %shard_map.113.hid_in = bf16[8832,768]{1,0:T(8,128)(2,1)S(1)} custom-call(bf16[90,96,256]{2,1,0:T(8,128)(2,1)S(1)} %get-tuple-element.13.first_ref, bf16[3,768,256]{2,1,0:T(8,128)(2,1)S(1)} %bitcast.6, bf16[2,96,256]{2,1,0:T(8,128)(2,1)S(1)} %get-tuple-element.18.after_ref), custom_call_target="tpu_custom_call" | custom-call | tf_op jit(solution)/shard_map/pallas_call | solution.py:381
  83.9 0.0 collective-permute-done.3.outer_ref
  83.9 0.0 collective-permute-done.2.inner_ref
  83.9 0.0 copy-done.2
  83.9 15.2 %shard_map.114 = (bf16[90,90,256]{2,1,0:T(8,128)(2,1)}, bf16[8832,768]{1,0:T(8,128)(2,1)S(1)}) custom-call(bf16[8832,768]{1,0:T(8,128)(2,1)S(1)} %shard_map.113.hid_in, bf16[90,96,256]{2,1,0:T(8,128)(2,1)S(1)} %get-tuple-element.13.first_ref, bf16[2,96,256]{2,1,0:T(8,128)(2,1)S(1)} %get-tuple-element.17.own_west, ...), custom_call_target="tpu_custom_call", output_to_operand_aliasing={{1}: (0, {})} | custom-call | tf_op jit(solution)/shard_map/pallas_call | solution.py:480
  (4 shorter events, 0.0 us)
Async XLA Ops:
  8.0 37.7 %all-to-all-start = ((bf16[32,144,128]{2,1,0:T(8,128)(2,1)}), bf16[32,144,128]{2,1,0:T(8,128)(2,1)S(1)}, u32[]{:S(2)}, u32[]{:S(2)}) async-start(bf16[32,144,128]{2,1,0:T(8,128)(2,1)} %shard_map.109), calls=%async_computation | async-start | bytes 2359296 | tf_op jit(solution)/shard_map/all_to_all | solution.py:539
  15.3 2.3 %copy-start.1 = (bf16[90,90,256]{2,1,0:T(8,128)(2,1)S(1)}, bf16[90,90,256]{2,1,0:T(8,128)(2,1)}, u32[]{:S(2)}) copy-start(bf16[90,90,256]{2,1,0:T(8,128)(2,1)} %back_ref.1) | copy-start | bytes 12441604
  17.5 0.9 copy-start.3
  18.4 27.2 %copy-start.4 = (bf16[128,256]{1,0:T(8,128)(2,1)S(1)}, bf16[128,256]{1,0:T(8,128)(2,1)}, u32[]{:S(2)}) copy-start(bf16[128,256]{1,0:T(8,128)(2,1)} %w_in_hbm.1) | copy-start | bytes 196612
  18.4 27.2 %copy-start.5 = (f32[256]{0:T(256)S(1)}, f32[256]{0:T(256)}, u32[]{:S(2)}) copy-start(f32[256]{0:T(256)} %param.19) | copy-start | bytes 3076
  45.7 22.7 %copy-start = (bf16[3,3,256,256]{3,2,1,0:T(8,128)(2,1)S(1)}, bf16[3,3,256,256]{3,2,1,0:T(8,128)(2,1)}, u32[]{:S(2)}) copy-start(bf16[3,3,256,256]{3,2,1,0:T(8,128)(2,1)} %param.20) | copy-start | bytes 3538948
  59.9 6.0 %collective-permute-start = (bf16[2,96,256]{2,1,0:T(8,128)(2,1)S(1)}, bf16[2,96,256]{2,1,0:T(8,128)(2,1)S(1)}, u32[]{:S(2)}, u32[]{:S(2)}) collective-permute-start(bf16[2,96,256]{2,1,0:T(8,128)(2,1)S(1)} %get-tuple-element.16.own_east), channel_id=1, source_target_pairs={{0,1},{1,2},{2,3},{3,4},{4,5},{5,6},{6,7},{7,0},{8,9},{9,10},{10,1... | collective-permute-start | bytes 294920 | tf_op jit(solution)/shard_map/ppermute | solution.py:544
  59.9 5.9 %collective-permute-start.1 = (bf16[2,96,256]{2,1,0:T(8,128)(2,1)S(1)}, bf16[2,96,256]{2,1,0:T(8,128)(2,1)S(1)}, u32[]{:S(2)}, u32[]{:S(2)}) collective-permute-start(bf16[2,96,256]{2,1,0:T(8,128)(2,1)S(1)} %get-tuple-element.17.own_west), channel_id=1, source_target_pairs={{1,0},{2,1},{3,2},{4,3},{5,4},{6,5},{7,6},{0,7},{9,8},{10,9},{11,1... | collective-permute-start | bytes 294920 | tf_op jit(solution)/shard_map/ppermute | solution.py:545
  65.9 18.0 %collective-permute-start.3 = (bf16[2,96,256]{2,1,0:T(8,128)(2,1)S(1)}, bf16[2,96,256]{2,1,0:T(8,128)(2,1)S(1)}, u32[]{:S(2)}, u32[]{:S(2)}) collective-permute-start(bf16[2,96,256]{2,1,0:T(8,128)(2,1)S(1)} %get-tuple-element.19), channel_id=1, source_target_pairs={{8,16},{16,8},{0,4},{24,28},{9,17},{17,9},{1,5},{25,29},{10,18},{1... | collective-permute-start | bytes 294920 | tf_op jit(solution)/shard_map/ppermute | solution.py:552
  66.0 17.9 %collective-permute-start.2 = (bf16[2,96,256]{2,1,0:T(8,128)(2,1)S(1)}, bf16[2,96,256]{2,1,0:T(8,128)(2,1)S(1)}, u32[]{:S(2)}, u32[]{:S(2)}) collective-permute-start(bf16[2,96,256]{2,1,0:T(8,128)(2,1)S(1)} %get-tuple-element.18.after_ref), channel_id=1, source_target_pairs={{0,8},{8,0},{16,24},{24,16},{1,9},{9,1},{17,25},{25,17},{2,10},{10... | collective-permute-start | bytes 294920 | tf_op jit(solution)/shard_map/ppermute | solution.py:551
  68.3 15.6 %copy-start.2 = (bf16[3,3,256,256]{3,2,1,0:T(8,128)(2,1)S(1)}, bf16[3,3,256,256]{3,2,1,0:T(8,128)(2,1)}, u32[]{:S(2)}) copy-start(bf16[3,3,256,256]{3,2,1,0:T(8,128)(2,1)} %param.21) | copy-start | bytes 3538948

commit v5 on v4

--- a/solution.py
+++ b/solution.py
@@ -9,10 +9,11 @@
 
 KCELL = 4
 GBINS = 32
-META = 16
+META = 8
 GROUP = 6
 BAND = 18
 CHUNK = 256
+HEAD = 768
 FINISH = 15
 BF = jnp.bfloat16
 F32 = jnp.float32
@@ -22,12 +23,18 @@
     return pltpu.CompilerParams(vmem_limit_bytes=mib * 1024 * 1024)
 
 
+def gelu(x):
+    scale = 0.7978845608028654
+    half = 0.5 * x
+    return half + half * jnp.tanh(x * (scale + (scale * 0.044715) * (x * x)))
+
+
 def dot(a, b):
     return jnp.dot(a, b, preferred_element_type=F32)
 
 
 def pack_kernel(
-    devices, cap, cols, bands, count_ref, dest_ref, cells_ref, gauss_ref, feat_ref, send_ref,
+    devices, lon_count, cap, cols, bands, count_ref, dest_ref, cells_ref, gauss_ref, feat_ref, send_ref,
     ext_ref, hot_ref, sorted_ref, place_ref, place_smem, sem,
 ):
     nrows, nfeat = feat_ref.shape
@@ -92,28 +99,33 @@
     sorted_ref[tail:span, :] = jnp.zeros((span - tail, 2 * nfeat), F32)
     copy.wait()
     side_lane = lax.broadcasted_iota(jnp.int32, (META, nfeat), 1)
-
-    def one(d, _):
+    odd = (lax.axis_index("lat") * lon_count + lax.axis_index("lon")) % 2 == 1
+
+    def one(d):
         begin = pl.multiple_of(place_smem[0, d], 8)
         got = sorted_ref[pl.ds(begin, cap), :]
-        send_ref[d, 0:cap, :] = got[:, :nfeat].astype(BF)
         side = got[:, nfeat:]
         if cap < nfeat:
             side = jnp.concatenate([side, jnp.zeros((nfeat - cap, nfeat), F32)], axis=0)
-        side = jnp.where(side_lane < place_smem[1, d], side.T[0:META], 0.0)
-        send_ref[d, cap : cap + META, :] = side.astype(BF)
+        return got[:, :nfeat], jnp.where(side_lane < place_smem[1, d], side.T[0:META], 0.0)
+
+    def pair(p, _):
+        (rows_a, side_a), (rows_b, side_b) = one(2 * p), one(2 * p + 1)
+        plain = jnp.concatenate([rows_a, side_a, rows_b, side_b], axis=0)
+        turned = jnp.concatenate([side_a, rows_a, side_b, rows_b], axis=0)
+        send_ref[p] = jnp.where(odd, turned, plain).astype(BF)
         return 0
 
-    lax.fori_loop(0, devices, one, 0, unroll=4)
-
-
-def pack(count, dest, cells, gauss, feats, devices, cap, cols, bands):
+    lax.fori_loop(0, devices // 2, pair, 0, unroll=2)
+
+
+def pack(count, dest, cells, gauss, feats, devices, lon_count, cap, cols, bands):
     nrows, nfeat = feats.shape
     span = -(-(nrows + 8 * devices) // 256) * 256 + cap
     kinds = devices * 2 * bands
     return pl.pallas_call(
-        functools.partial(pack_kernel, devices, cap, cols, bands),
-        out_shape=jax.ShapeDtypeStruct((devices, cap + META, nfeat), BF),
+        functools.partial(pack_kernel, devices, lon_count, cap, cols, bands),
+        out_shape=jax.ShapeDtypeStruct((devices // 2, 2 * (cap + META), nfeat), BF),
         in_specs=[pl.BlockSpec(memory_space=pltpu.SMEM)] + [pl.BlockSpec(memory_space=pltpu.VMEM)] * 4,
         out_specs=pl.BlockSpec(memory_space=pltpu.VMEM),
         scratch_shapes=[
@@ -155,7 +167,7 @@
 def grid_kernel(
     devices, cap, wide, cols, lat_bands, recv_ref, back_hbm, w_in_hbm, w_dens_hbm,
     first_ref, west_ref, east_ref, inner_ref, outer_ref,
-    rows_ref, lats_ref, feat_ref, meta_ref, acc_ref, edge_scr, ends_ref, ends_smem, sem,
+    rows_ref, sides_ref, lats_ref, feat_ref, meta_ref, acc_ref, edge_scr, ends_ref, ends_smem, sem,
     back_ref, w_in_ref, w_dens_ref, sems,
 ):
     band = pl.program_id(0)
@@ -178,16 +190,15 @@
     def _():
         for load in loads:
             load.start()
-        feat_ref[...] = jnp.zeros(feat_ref.shape, F32)
-        rows_ref[slots:, :] = jnp.zeros((rows_ref.shape[0] - slots, nfeat), F32)
-
-        def widen(s, _):
-            rows_ref[pl.ds(pl.multiple_of(s * cap, cap), cap), :] = recv_ref[s, 0:cap, :].astype(F32)
-            side = recv_ref[s, cap : cap + META, :].astype(F32)
-            lats_ref[pl.ds(s, 1), :] = jnp.where(side[2:3] > 0, side[0:1], 1e6)
+
+        def read(p, _):
+            both = recv_ref[p, cap : cap + 2 * META, :].astype(F32)
+            for s, side in ((2 * p, both[:META]), (2 * p + 1, both[META:])):
+                sides_ref[s] = side
+                lats_ref[pl.ds(s, 1), :] = jnp.where(side[2:3] > 0, side[0:1], 1e6)
             return 0
 
-        lax.fori_loop(0, devices, widen, 0, unroll=4)
+        lax.fori_loop(0, devices // 2, read, 0, unroll=8)
         lats = lats_ref[...]
         lane = lax.broadcasted_iota(jnp.int32, (devices, nfeat), 1)
         ends = jnp.zeros((devices, nfeat), F32)
@@ -198,17 +209,27 @@
         ends_ref[...] = ends.astype(jnp.int32)
         copy = pltpu.make_async_copy(ends_ref, ends_smem, sem)
         copy.start()
+        feat_ref[...] = jnp.zeros(feat_ref.shape, F32)
+        rows_ref[slots:, :] = jnp.zeros((rows_ref.shape[0] - slots, nfeat), F32)
+
+        def widen(p, _):
+            begin = pl.multiple_of(2 * p * cap, cap)
+            rows_ref[pl.ds(begin, cap), :] = recv_ref[p, 0:cap, :].astype(F32)
+            rows_ref[pl.ds(begin + cap, cap), :] = recv_ref[p, cap + 2 * META :, :].astype(F32)
+            return 0
+
+        lax.fori_loop(0, devices // 2, widen, 0, unroll=2)
         copy.wait()
 
     meta_ref[...] = jnp.zeros(meta_ref.shape, F32)
-    lane = lax.broadcasted_iota(jnp.int32, (8, nfeat), 1)
+    lane = lax.broadcasted_iota(jnp.int32, (META, nfeat), 1)
 
     def compact(s, out):
         out = pl.multiple_of(out, 8)
         low, high = ends_smem[s, 2 * band], ends_smem[s, 2 * band + 1]
         source = pl.multiple_of(low // 8 * 8, 8)
         feat_ref[pl.ds(out, cap), :] = rows_ref[pl.ds(pl.multiple_of(s * cap + source, 8), cap), :]
-        side = recv_ref[s, cap : cap + META, :].astype(F32)[0:8]
+        side = sides_ref[s]
         side = jnp.where((lane >= low) & (lane < high), side, 0.0)
         shift = out - source + nfeat
         tile, shift = shift // nfeat, shift % nfeat
@@ -217,14 +238,12 @@
         meta_ref[tile + 1] += jnp.where(lane < shift, moved, 0.0)
         return out + (high - source + 7) // 8 * 8
 
-    total = lax.fori_loop(0, devices, compact, 0, unroll=4)
-    acc_ref[...] = jnp.zeros(acc_ref.shape, F32)
-    col_id = lax.broadcasted_iota(jnp.int32, (wide, CHUNK), 0).astype(F32)
-
-    def chunk(k, _):
-        side = jnp.concatenate(
-            [meta_ref[1 + k * (CHUNK // nfeat) + q] for q in range(CHUNK // nfeat)], axis=1
-        )
+    total = lax.fori_loop(0, devices, compact, 0, unroll=16)
+
+    def piece(begin, size):
+        begin = pl.multiple_of(begin, CHUNK)
+        col_id = lax.broadcasted_iota(jnp.int32, (wide, size), 0).astype(F32)
+        side = jnp.concatenate([meta_ref[1 + begin // nfeat + q] for q in range(size // nfeat)], axis=1)
         lat, lon = side[0:1], side[1:2]
         here = (col_id == lon + 2.0).astype(F32).astype(BF)
         after = (col_id == lon + 3.0).astype(F32).astype(BF)
@@ -236,14 +255,17 @@
             right = jnp.where(same, side[3:4], jnp.where(above, side[5:6], 0.0)).astype(BF)
             parts.append(here * left + after * right)
         spread = jnp.concatenate(parts, axis=0)
-        begin = pl.multiple_of(k * CHUNK, CHUNK)
         values = jnp.concatenate(
-            [feat_ref[pl.ds(begin, CHUNK), :].astype(BF), jnp.ones((CHUNK, nfeat), BF)], axis=1
+            [feat_ref[pl.ds(begin, size), :].astype(BF), jnp.ones((size, nfeat), BF)], axis=1
         )
-        acc_ref[...] += dot(spread, values)
+        return dot(spread, values)
+
+    def more(k, _):
+        acc_ref[...] += piece(k * CHUNK, CHUNK)
         return 0
 
-    lax.fori_loop(0, (total + CHUNK - 1) // CHUNK, chunk, 0)
+    acc_ref[...] = piece(0, HEAD)
+    lax.fori_loop(HEAD // CHUNK, (total + CHUNK - 1) // CHUNK, more, 0)
     fetch.wait()
 
     @pl.when(band == 0)
@@ -278,7 +300,7 @@
 
 
 def gridded(recv, back, w_in, w_dens, cap, wide, lat_rows, cols):
-    devices, _, nfeat = recv.shape
+    devices, nfeat = 2 * recv.shape[0], recv.shape[2]
     chans = back.shape[1]
     slots = devices * cap
     tall = -(-lat_rows // 16) * 16
@@ -297,9 +319,10 @@
         out_specs=(whole,) * 5,
         scratch_shapes=[
             pltpu.VMEM((slots + cap, nfeat), F32),
+            pltpu.VMEM((devices, META, nfeat), F32),
             pltpu.VMEM((devices, nfeat), F32),
-            pltpu.VMEM((slots + cap + CHUNK, nfeat), F32),
-            pltpu.VMEM((slots // nfeat + 6, 8, nfeat), F32),
+            pltpu.VMEM((slots + cap + HEAD, nfeat), F32),
+            pltpu.VMEM((slots // nfeat + 8, META, nfeat), F32),
             pltpu.VMEM((BAND * wide, 2 * nfeat), F32),
             pltpu.VMEM((4, tall, chans), F32),
             pltpu.VMEM((devices, nfeat), jnp.int32),
@@ -368,7 +391,7 @@
     def hidden(g, _):
         begin = pl.multiple_of(g * size, 16)
         total = taps(field, begin, size, wide, one_ref)
-        put(hid_ref, pl.multiple_of(begin + 2 * wide, 16), jax.nn.gelu(total))
+        put(hid_ref, pl.multiple_of(begin + 2 * wide, 16), gelu(total))
         return 0
 
     lax.fori_loop(0, split, hidden, 0)
@@ -423,12 +446,12 @@
             for a in range(3):
                 tap = jnp.where(pole, 2 - a, a)
                 total = total + dot(rim[(begin + a) * wide : (begin + a + 1) * wide, :], one_ref[tap])
-            put(hid_ref, index * wide, jax.nn.gelu(total))
+            put(hid_ref, index * wide, gelu(total))
         total = jnp.zeros((2 * wide, chans), F32)
         for a in range(3):
             pair = [rim[(n + a) * wide : (n + a + 1) * wide, :] for n in (1, 4)]
             total = total + dot(jnp.concatenate(pair, axis=0), one_ref[a])
-        total = jax.nn.gelu(total)
+        total = gelu(total)
         put(hid_ref, wide, total[:wide])
         put(hid_ref, lat_rows * wide, total[wide:])
 
@@ -439,7 +462,7 @@
         size = windows.shape[0]
         total = pltpu.roll(dot(windows, one_ref[0]), 1, axis=0) + dot(windows, one_ref[1])
         total = total + pltpu.roll(dot(windows, one_ref[2]), size - 1, axis=0)
-        total = jax.nn.gelu(total)
+        total = gelu(total)
         tall = size // 4
         for n in range(4):
             cols_scr[n] = total[n * tall : (n + 1) * tall]
@@ -533,10 +556,12 @@
     cap = 2 * nrows // devices
     wide = -(-(cols + 4) // 16) * 16
     send = pack(
-        row_counts, obs_dest.reshape(1, nrows), obs_cells.T, obs_gauss.T, obs_features, devices, cap, cols,
+        row_counts, obs_dest.reshape(1, nrows), obs_cells.T, obs_gauss.T, obs_features, devices, lon_count, cap, cols,
         lat_rows // BAND,
     )
-    recv = lax.all_to_all(send, axes, split_axis=0, concat_axis=0, tiled=True)
+    paired = send.shape
+    send = send.reshape(devices, cap + META, nfeat)
+    recv = lax.all_to_all(send, axes, split_axis=0, concat_axis=0, tiled=True).reshape(paired)
     back = projected(background, w_bg, wide)
     first, own_west, own_east, inner_row, outer_row = gridded(
         recv, back, w_in, w_dens.reshape(1, chans), cap, wide, lat_rows, cols

time: 99 us -> 95.5 us (0.965)
  Pallas kernels: 57.3 us -> 54.6 us
    pallas_call x1, Pallas kernels: 14.2 us -> 11.8 us  [gridded(): pl.pallas_call(functools.partial(grid_kernel, devices, cap, wide, cols, l...]
    all_to_all x1, waiting for transfers between devices: 22.3 us -> 20.9 us  [shards(): lax.all_to_all(send, axes, split_axis=0, concat_axis=0, tiled=True)]
  transfers between devices with their start and end apart: 5 -> 5, of which waited for: 2 -> 3; matrix products, arithmetic and copies ran while one was open for 0% -> 0% of each run, Pallas kernels for 21% -> 21%
where the time goes in v5:
time: 95.5 us; the launch traced here: 95.2 us
  Pallas kernels  54.6 us (57%)
  waiting for transfers between devices  23.9 us (25%)
  starting transfers between devices  12.8 us (13%)
  local copies, waits for them, and re-layouts  3.17 us (3%)
    all_to_all x1, waiting for transfers between devices, shards(): lax.all_to_all(send, axes, split_axis=0, concat_axis=0, tiled=True)  20.9 us
    pallas_call x1, Pallas kernels, inside(): pl.pallas_call(functools.partial(inside_kernel, split), out_shape=jax.Sha...  15.4 us
    pallas_call x1, Pallas kernels, finished(): pl.pallas_call(functools.partial(finish_kernel, lat_count), grid=(lat_row...  15.2 us
    pallas_call x1, Pallas kernels, gridded(): pl.pallas_call(functools.partial(grid_kernel, devices, cap, wide, cols, l...  11.8 us
    all_to_all x1, starting transfers between devices, shards(): lax.all_to_all(send, axes, split_axis=0, concat_axis=0, tiled=True)  7.3 us
    pallas_call x1, Pallas kernels, pack(): pl.pallas_call(functools.partial(pack_kernel, devices, lon_count, cap, co...  7.24 us
    pallas_call x1, Pallas kernels, projected(): pl.pallas_call(functools.partial(back_kernel, wide), grid=(lat_rows // BA...  4.97 us
    ppermute x1, starting transfers between devices, shards(): lax.ppermute(own_west, 'lon', [((i + 1) % lon_count, i) for i in range(lo...  3.53 us
  transfers between devices with their start and end apart: 5, of which 3 were waited for; matrix products, arithmetic and copies ran while one was open for 0% of the time, Pallas kernels for 21%

profile of v5, /device:TPU:0, one launch (start us, length us, event | category | flops | bytes accessed | tf_op | source)
XLA Modules:
  0.0 95.2 jit_solution(13674661906548939550)
XLA Ops:
  0.7 7.2 %shard_map.109 = bf16[16,272,128]{2,1,0:T(8,128)(2,1)} custom-call(s32[1]{0:T(128)S(6)} %copy.14.count_ref, s32[1,2048]{1,0:T(1,128)} %bitcast.16, s32[4,2048]{1,0:T(4,128)} %bitcast.14, s32[4,2048]{1,0:T(4,128)} %bitcast.15, bf16[2048,128]{1,0:T(8,128)(2,1)} %feat_ref.1), custom_call_target="tpu_custom_call" | custom-call | tf_op jit(solution)/shard_map/pallas_call | solution.py:126
  7.9 7.3 %all-to-all-start = ((bf16[32,136,128]{2,1,0:T(8,128)(2,1)}), bf16[32,136,128]{2,1,0:T(8,128)(2,1)S(1)}, u32[]{:S(2)}, u32[]{:S(2)}) async-start(bf16[32,136,128]{2,1,0:T(8,128)(2,1)} %bitcast.13), calls=%async_computation | async-start | bytes 2228224 | tf_op jit(solution)/shard_map/all_to_all | solution.py:564
  15.2 0.0 copy-start.1
  15.2 2.2 %copy-done.1 = bf16[90,90,256]{2,1,0:T(8,128)(2,1)S(1)} copy-done((bf16[90,90,256]{2,1,0:T(8,128)(2,1)S(1)}, bf16[90,90,256]{2,1,0:T(8,128)(2,1)}, u32[]{:S(2)}) %copy-start.1) | copy-done | bytes 4147224
  17.5 0.0 copy-start.3
  17.5 0.9 copy-done.3
  18.4 0.0 copy-start.4
  18.4 5.0 %shard_map.110.back_hbm = f32[65552,256]{1,0:T(8,128)} custom-call(bf16[90,90,256]{2,1,0:T(8,128)(2,1)S(1)} %copy-done.1, bf16[256,256]{1,0:T(8,128)(2,1)S(1)} %copy-done.3), custom_call_target="tpu_custom_call" | custom-call | tf_op jit(solution)/shard_map/pallas_call | solution.py:153
  23.3 20.9 %all-to-all-done = bf16[32,136,128]{2,1,0:T(8,128)(2,1)S(1)} async-done(((bf16[32,136,128]{2,1,0:T(8,128)(2,1)}), bf16[32,136,128]{2,1,0:T(8,128)(2,1)S(1)}, u32[]{:S(2)}, u32[]{:S(2)}) %all-to-all-start) | async-done | bytes 1114144 | tf_op jit(solution)/shard_map/all_to_all | solution.py:564
  44.2 0.0 copy-done.4
  44.2 0.0 copy-done.5
  44.2 11.8 %shard_map.111 = (bf16[90,96,256]{2,1,0:T(8,128)(2,1)S(1)}, bf16[2,96,256]{2,1,0:T(8,128)(2,1)S(1)}, bf16[2,96,256]{2,1,0:T(8,128)(2,1)S(1)}, bf16[2,96,256]{2,1,0:T(8,128)(2,1)S(1)}, bf16[2,96,256]{2,1,0:T(8,128)(2,1)S(1)}) custom-call(bf16[16,272,128]{2,1,0:T(8,128)(2,1)S(1)} %bitcast.10, f32[65552,256]{1,0:T(8,128)} %shard_map.110.back_hbm, ...), custom_call_target="tpu_custom_call" | custom-call | tf_op jit(solution)/shard_map/pallas_call | solution.py:308
  56.0 0.1 collective-permute-start
  56.1 3.5 %collective-permute-start.1 = (bf16[2,96,256]{2,1,0:T(8,128)(2,1)S(1)}, bf16[2,96,256]{2,1,0:T(8,128)(2,1)S(1)}, u32[]{:S(2)}, u32[]{:S(2)}) collective-permute-start(bf16[2,96,256]{2,1,0:T(8,128)(2,1)S(1)} %get-tuple-element.17.own_west), channel_id=1, source_target_pairs={{1,0},{2,1},{3,2},{4,3},{5,4},{6,5},{7,6},{0,7},{9,8},{10,9},{11,1... | collective-permute-start | bytes 294920 | tf_op jit(solution)/shard_map/ppermute | solution.py:570
  59.6 2.3 %collective-permute-done.west_ref = bf16[2,96,256]{2,1,0:T(8,128)(2,1)S(1)} collective-permute-done((bf16[2,96,256]{2,1,0:T(8,128)(2,1)S(1)}, bf16[2,96,256]{2,1,0:T(8,128)(2,1)S(1)}, u32[]{:S(2)}, u32[]{:S(2)}) %collective-permute-start) | collective-permute-done | bytes 98336 | tf_op jit(solution)/shard_map/ppermute | solution.py:569
  61.9 0.7 collective-permute-done.1.east_ref
  62.7 0.1 collective-permute-start.3
  62.8 1.8 %collective-permute-start.2 = (bf16[2,96,256]{2,1,0:T(8,128)(2,1)S(1)}, bf16[2,96,256]{2,1,0:T(8,128)(2,1)S(1)}, u32[]{:S(2)}, u32[]{:S(2)}) collective-permute-start(bf16[2,96,256]{2,1,0:T(8,128)(2,1)S(1)} %get-tuple-element.18.after_ref), channel_id=1, source_target_pairs={{0,8},{8,0},{16,24},{24,16},{1,9},{9,1},{17,25},{25,17},{2,10},{10... | collective-permute-start | bytes 294920 | tf_op jit(solution)/shard_map/ppermute | solution.py:576
  64.6 0.0 copy-done
  64.6 15.4 %shard_map.113.hid_in = bf16[8832,768]{1,0:T(8,128)(2,1)S(1)} custom-call(bf16[90,96,256]{2,1,0:T(8,128)(2,1)S(1)} %get-tuple-element.13.first_ref, bf16[3,768,256]{2,1,0:T(8,128)(2,1)S(1)} %bitcast.8, bf16[2,96,256]{2,1,0:T(8,128)(2,1)S(1)} %get-tuple-element.18.after_ref), custom_call_target="tpu_custom_call" | custom-call | tf_op jit(solution)/shard_map/pallas_call | solution.py:404
  80.0 0.0 collective-permute-done.3.outer_ref
  80.0 0.0 collective-permute-done.2.inner_ref
  80.0 0.0 copy-done.2
  80.0 15.2 %shard_map.114 = (bf16[90,90,256]{2,1,0:T(8,128)(2,1)}, bf16[8832,768]{1,0:T(8,128)(2,1)S(1)}) custom-call(bf16[8832,768]{1,0:T(8,128)(2,1)S(1)} %shard_map.113.hid_in, bf16[90,96,256]{2,1,0:T(8,128)(2,1)S(1)} %get-tuple-element.13.first_ref, bf16[2,96,256]{2,1,0:T(8,128)(2,1)S(1)} %get-tuple-element.17.own_west, ...), custom_call_target="tpu_custom_call", output_to_operand_aliasing={{1}: (0, {})} | custom-call | tf_op jit(solution)/shard_map/pallas_call | solution.py:503
  (4 shorter events, 0.0 us)
Async XLA Ops:
  7.9 36.3 %all-to-all-start = ((bf16[32,136,128]{2,1,0:T(8,128)(2,1)}), bf16[32,136,128]{2,1,0:T(8,128)(2,1)S(1)}, u32[]{:S(2)}, u32[]{:S(2)}) async-start(bf16[32,136,128]{2,1,0:T(8,128)(2,1)} %bitcast.13), calls=%async_computation | async-start | bytes 2228224 | tf_op jit(solution)/shard_map/all_to_all | solution.py:564
  15.2 2.3 %copy-start.1 = (bf16[90,90,256]{2,1,0:T(8,128)(2,1)S(1)}, bf16[90,90,256]{2,1,0:T(8,128)(2,1)}, u32[]{:S(2)}) copy-start(bf16[90,90,256]{2,1,0:T(8,128)(2,1)} %back_ref.1) | copy-start | bytes 12441604
  17.5 0.9 copy-start.3
  18.4 25.8 %copy-start.4 = (bf16[128,256]{1,0:T(8,128)(2,1)S(1)}, bf16[128,256]{1,0:T(8,128)(2,1)}, u32[]{:S(2)}) copy-start(bf16[128,256]{1,0:T(8,128)(2,1)} %w_in_hbm.1) | copy-start | bytes 196612
  18.4 25.8 %copy-start.5 = (f32[256]{0:T(256)S(1)}, f32[256]{0:T(256)}, u32[]{:S(2)}) copy-start(f32[256]{0:T(256)} %param.19) | copy-start | bytes 3076
  44.2 20.4 %copy-start = (bf16[3,3,256,256]{3,2,1,0:T(8,128)(2,1)S(1)}, bf16[3,3,256,256]{3,2,1,0:T(8,128)(2,1)}, u32[]{:S(2)}) copy-start(bf16[3,3,256,256]{3,2,1,0:T(8,128)(2,1)} %param.20) | copy-start | bytes 3538948
  56.0 5.9 %collective-permute-start = (bf16[2,96,256]{2,1,0:T(8,128)(2,1)S(1)}, bf16[2,96,256]{2,1,0:T(8,128)(2,1)S(1)}, u32[]{:S(2)}, u32[]{:S(2)}) collective-permute-start(bf16[2,96,256]{2,1,0:T(8,128)(2,1)S(1)} %get-tuple-element.16.own_east), channel_id=1, source_target_pairs={{0,1},{1,2},{2,3},{3,4},{4,5},{5,6},{6,7},{7,0},{8,9},{9,10},{10,1... | collective-permute-start | bytes 294920 | tf_op jit(solution)/shard_map/ppermute | solution.py:569
  56.1 6.6 %collective-permute-start.1 = (bf16[2,96,256]{2,1,0:T(8,128)(2,1)S(1)}, bf16[2,96,256]{2,1,0:T(8,128)(2,1)S(1)}, u32[]{:S(2)}, u32[]{:S(2)}) collective-permute-start(bf16[2,96,256]{2,1,0:T(8,128)(2,1)S(1)} %get-tuple-element.17.own_west), channel_id=1, source_target_pairs={{1,0},{2,1},{3,2},{4,3},{5,4},{6,5},{7,6},{0,7},{9,8},{10,9},{11,1... | collective-permute-start | bytes 294920 | tf_op jit(solution)/shard_map/ppermute | solution.py:570
  62.7 17.3 %collective-permute-start.3 = (bf16[2,96,256]{2,1,0:T(8,128)(2,1)S(1)}, bf16[2,96,256]{2,1,0:T(8,128)(2,1)S(1)}, u32[]{:S(2)}, u32[]{:S(2)}) collective-permute-start(bf16[2,96,256]{2,1,0:T(8,128)(2,1)S(1)} %get-tuple-element.19), channel_id=1, source_target_pairs={{8,16},{16,8},{0,4},{24,28},{9,17},{17,9},{1,5},{25,29},{10,18},{1... | collective-permute-start | bytes 294920 | tf_op jit(solution)/shard_map/ppermute | solution.py:577
  62.8 17.2 %collective-permute-start.2 = (bf16[2,96,256]{2,1,0:T(8,128)(2,1)S(1)}, bf16[2,96,256]{2,1,0:T(8,128)(2,1)S(1)}, u32[]{:S(2)}, u32[]{:S(2)}) collective-permute-start(bf16[2,96,256]{2,1,0:T(8,128)(2,1)S(1)} %get-tuple-element.18.after_ref), channel_id=1, source_target_pairs={{0,8},{8,0},{16,24},{24,16},{1,9},{9,1},{17,25},{25,17},{2,10},{10... | collective-permute-start | bytes 294920 | tf_op jit(solution)/shard_map/ppermute | solution.py:576
  64.6 15.4 %copy-start.2 = (bf16[3,3,256,256]{3,2,1,0:T(8,128)(2,1)S(1)}, bf16[3,3,256,256]{3,2,1,0:T(8,128)(2,1)}, u32[]{:S(2)}) copy-start(bf16[3,3,256,256]{3,2,1,0:T(8,128)(2,1)} %param.21) | copy-start | bytes 3538948

commit v6 on v5

--- a/solution.py
+++ b/solution.py
@@ -349,7 +349,7 @@
     return dot(field, w_ref[...].reshape(field.shape[1], w_ref.shape[2]))
 
 
-def border_kernel(lat_rows, cols, inner_ref, outer_ref, west_ref, east_ref, inner_out, outer_out):
+def border_kernel(lat_rows, cols, inner_ref, outer_ref, west_ref, east_ref, after_ref, inner_out, outer_out):
     _, wide, chans = inner_ref.shape
     even = lax.axis_index("lat") % 2 == 0
     row_id = lax.broadcasted_iota(jnp.int32, (wide, chans), 0)
@@ -366,59 +366,61 @@
         outer_out[k] = outer.astype(BF)
 
 
-def bordered(inner, outer, west, east, lat_rows, cols):
+def bordered(inner, outer, west, east, after, lat_rows, cols):
     whole = pl.BlockSpec(memory_space=pltpu.VMEM)
     shape = jax.ShapeDtypeStruct(inner.shape, BF)
     return pl.pallas_call(
         functools.partial(border_kernel, lat_rows, cols),
         out_shape=(shape, shape),
-        in_specs=[whole] * 4,
+        in_specs=[whole] * 4 + [pl.BlockSpec(memory_space=pl.ANY)],
         out_specs=(whole, whole),
         compiler_params=params(24),
-    )(inner, outer, west, east)
-
-
-def inside_kernel(split, first_ref, one_ref, after_ref, hid_ref, field):
+    )(inner, outer, west, east, after)
+
+
+def inside_kernel(lead, place, first_ref, one_ref, after_ref, hid_ref, field):
     lat_rows, wide, chans = first_ref.shape
+    half = lat_rows // 2
 
     def load(r, _):
-        put(field, pl.multiple_of(r * wide, 16), first_ref[r].astype(F32))
+        put(field, pl.multiple_of(r * wide, 16), first_ref[lead + r].astype(F32))
         return 0
 
-    lax.fori_loop(0, lat_rows, load, 0, unroll=6)
-    size = (lat_rows - 2) // split * wide
+    lax.fori_loop(0, half + 2, load, 0)
+    size = FINISH * wide
 
     def hidden(g, _):
         begin = pl.multiple_of(g * size, 16)
         total = taps(field, begin, size, wide, one_ref)
-        put(hid_ref, pl.multiple_of(begin + 2 * wide, 16), gelu(total))
+        put(hid_ref, pl.multiple_of(begin + place * wide, 16), gelu(total))
         return 0
 
-    lax.fori_loop(0, split, hidden, 0)
-
-
-def inside(first, one, after):
+    lax.fori_loop(0, half // FINISH, hidden, 0)
+
+
+def inside(first, one, after, lead, place):
     lat_rows, wide, chans = first.shape
+    size = (lat_rows // 2 + 2) * wide
     whole = pl.BlockSpec(memory_space=pltpu.VMEM)
-    split = next(n for n in (4, 2, 1) if (lat_rows - 2) % n == 0)
     return pl.pallas_call(
-        functools.partial(inside_kernel, split),
-        out_shape=jax.ShapeDtypeStruct(((lat_rows + 2) * wide, 3 * chans), BF),
+        functools.partial(inside_kernel, lead, place),
+        out_shape=jax.ShapeDtypeStruct((size, 3 * chans), BF),
         in_specs=[whole, whole, pl.BlockSpec(memory_space=pl.ANY)],
         out_specs=whole,
-        scratch_shapes=[pltpu.VMEM((lat_rows * wide, 3 * chans), BF)],
-        compiler_params=params(30),
+        scratch_shapes=[pltpu.VMEM((size, 3 * chans), BF)],
+        compiler_params=params(24),
     )(first, one, after)
 
 
 def finish_kernel(
-    lat_count, hid_in, first_ref, own_west, own_east, west_ref, east_ref, inner_ref, outer_ref,
-    one_ref, two_ref, out_ref, hid_ref, rim, cols_scr,
+    lat_count, upper_in, lower_in, first_ref, own_west, own_east, west_ref, east_ref, inner_ref, outer_ref,
+    one_ref, two_ref, out_ref, upper_ref, lower_ref, rim, cols_scr,
 ):
     group = pl.program_id(0)
     lat_rows, wide, chans = first_ref.shape
     rows, cols, _ = out_ref.shape
     block = rows * wide
+    half = lat_rows // 2
 
     @pl.when(group == 0)
     def _():
@@ -441,19 +443,23 @@
         lines += [own_row(lat_rows - 2), own_row(lat_rows - 1), edge_row(False, 0), edge_row(False, 1)]
         for n, line in enumerate(lines):
             put(rim, n * wide, line)
-        for begin, index, pole in ((0, 0, lat_index == 0), (5, lat_rows + 1, lat_index == lat_count - 1)):
+        ends = (
+            (0, upper_ref, 0, lat_index == 0),
+            (5, lower_ref, half + 1, lat_index == lat_count - 1),
+        )
+        for begin, ref, index, pole in ends:
             total = jnp.zeros((wide, chans), F32)
             for a in range(3):
                 tap = jnp.where(pole, 2 - a, a)
                 total = total + dot(rim[(begin + a) * wide : (begin + a + 1) * wide, :], one_ref[tap])
-            put(hid_ref, index * wide, gelu(total))
+            put(ref, index * wide, gelu(total))
         total = jnp.zeros((2 * wide, chans), F32)
         for a in range(3):
             pair = [rim[(n + a) * wide : (n + a + 1) * wide, :] for n in (1, 4)]
             total = total + dot(jnp.concatenate(pair, axis=0), one_ref[a])
         total = gelu(total)
-        put(hid_ref, wide, total[:wide])
-        put(hid_ref, lat_rows * wide, total[wide:])
+        put(upper_ref, wide, total[:wide])
+        put(lower_ref, half * wide, total[wide:])
 
         lines = [west_ref[0], west_ref[1], own_west[0], own_west[1]]
         lines += [own_east[0], own_east[1], east_ref[0], east_ref[1]]
@@ -468,9 +474,9 @@
             cols_scr[n] = total[n * tall : (n + 1) * tall]
         last = wide - 16
 
-        def patch(r, _):
+        def patch(ref, shift, r, _):
             fixes = [cols_scr[n, pl.ds(r, 1), :] for n in range(4)]
-            begin = pl.multiple_of((r + 1) * wide, 16)
+            begin = pl.multiple_of((r - shift) * wide, 16)
             for b in range(3):
                 lanes = slice(b * chans, (b + 1) * chans)
                 for start in (0, last):
@@ -480,42 +486,48 @@
                         if 0 <= col - b - start < 16
                     ]
                     if edits:
-                        value = hid_ref[pl.ds(begin + start, 16), lanes].astype(F32)
+                        value = ref[pl.ds(begin + start, 16), lanes].astype(F32)
                         for at, fix in edits:
                             value = jnp.where(short_id == at, fix, value)
-                        hid_ref[pl.ds(begin + start, 16), lanes] = value.astype(BF)
+                        ref[pl.ds(begin + start, 16), lanes] = value.astype(BF)
             return 0
 
-        lax.fori_loop(1, lat_rows - 1, patch, 0, unroll=8)
-
-    begin = pl.multiple_of(group * block, 16)
-    total = taps(hid_ref, begin, block, wide, two_ref)
-    own = first_ref[pl.ds(group * rows, rows)].reshape(block, chans).astype(F32)
-    total = total + pltpu.roll(own, block - 2, axis=0)
-    result = total.astype(BF)
-    for i in range(rows):
-        out_ref[i] = result[i * wide : i * wide + cols]
-
-
-def finished(hid, first, sides, one, two, cols, lat_count):
+        lax.fori_loop(1, half + 1, functools.partial(patch, upper_ref, -1), 0, unroll=9)
+        lax.fori_loop(half - 1, lat_rows - 1, functools.partial(patch, lower_ref, half - 1), 0, unroll=9)
+
+    def second(ref, first_group):
+        begin = pl.multiple_of((group - first_group) * block, 16)
+        total = taps(ref, begin, block, wide, two_ref)
+        own = first_ref[pl.ds(group * rows, rows)].reshape(block, chans).astype(F32)
+        total = total + pltpu.roll(own, block - 2, axis=0)
+        result = total.astype(BF)
+        for i in range(rows):
+            out_ref[i] = result[i * wide : i * wide + cols]
+
+    pl.when(group < half // rows)(lambda: second(upper_ref, 0))
+    pl.when(group >= half // rows)(lambda: second(lower_ref, half // rows))
+
+
+def finished(upper, lower, first, sides, one, two, cols, lat_count):
     lat_rows, wide, chans = first.shape
     whole = pl.BlockSpec(memory_space=pltpu.VMEM)
-    out, _ = pl.pallas_call(
+    out, _, _ = pl.pallas_call(
         functools.partial(finish_kernel, lat_count),
         grid=(lat_rows // FINISH,),
         out_shape=(
             jax.ShapeDtypeStruct((lat_rows, cols, chans), BF),
-            jax.ShapeDtypeStruct(hid.shape, BF),
+            jax.ShapeDtypeStruct(upper.shape, BF),
+            jax.ShapeDtypeStruct(lower.shape, BF),
         ),
-        in_specs=[whole] * (4 + len(sides)),
-        out_specs=(pl.BlockSpec((FINISH, cols, chans), lambda g: (g, 0, 0)), whole),
-        input_output_aliases={0: 1},
+        in_specs=[whole] * (5 + len(sides)),
+        out_specs=(pl.BlockSpec((FINISH, cols, chans), lambda g: (g, 0, 0)), whole, whole),
+        input_output_aliases={0: 1, 1: 2},
         scratch_shapes=[
             pltpu.VMEM((8 * wide, 3 * chans), BF),
             pltpu.VMEM((4, sides[0].shape[1], chans), F32),
         ],
         compiler_params=params(26),
-    )(hid, first, *sides, one, two)
+    )(upper, lower, first, *sides, one, two)
     return out
 
 
@@ -570,13 +582,15 @@
     east = lax.ppermute(own_west, "lon", [((i + 1) % lon_count, i) for i in range(lon_count)])
     one = conv_one.reshape(3, 3 * chans, chans)
     two = conv_two.reshape(3, 3 * chans, chans)
-    inner_row, outer_row = bordered(inner_row, outer_row, west, east, lat_rows, cols)
+    half = lat_rows // 2
+    upper = inside(first, one, own_west, 0, 2)
+    inner_row, outer_row = bordered(inner_row, outer_row, west, east, upper, lat_rows, cols)
     inner, outer = row_pairs(lat_count, lon_count)
-    hid = inside(first, one, inner_row)
+    lower = inside(first, one, inner_row, half - 2, 0)
     inner_row = lax.ppermute(inner_row, axes, inner)
     outer_row = lax.ppermute(outer_row, axes, outer)
     sides = (own_west, own_east, west, east, inner_row, outer_row)
-    return finished(hid, first, sides, one, two, cols, lat_count)
+    return finished(upper, lower, first, sides, one, two, cols, lat_count)
 
 
 def solution(mesh):

time: 95.5 us -> 93.4 us (0.978)
  waiting for transfers between devices: 23.9 us -> 20.9 us
    ppermute x1, waiting for transfers between devices: 2.29 us -> 0.01 us  [shards(): lax.ppermute(own_east, 'lon', [(i, (i + 1) % lon_count) for i in range(lo...]
    pallas_call x1 -> x2, Pallas kernels: 15.4 us -> 16.1 us  [inside(): pl.pallas_call(functools.partial(inside_kernel, lead, place), out_shape=j...]
  transfers between devices with their start and end apart: 5 -> 5, of which waited for: 3 -> 1; matrix products, arithmetic and copies ran while one was open for 0% -> 0% of each run, Pallas kernels for 21% -> 23%
where the time goes in v6:
time: 93.4 us; the launch traced here: 93.1 us
  Pallas kernels  55.4 us (59%)
  waiting for transfers between devices  20.9 us (22%)
  starting transfers between devices  12.9 us (14%)
  local copies, waits for them, and re-layouts  3.17 us (3%)
    all_to_all x1, waiting for transfers between devices, shards(): lax.all_to_all(send, axes, split_axis=0, concat_axis=0, tiled=True)  20.9 us
    pallas_call x2, Pallas kernels, inside(): pl.pallas_call(functools.partial(inside_kernel, lead, place), out_shape=j...  16.1 us
    pallas_call x1, Pallas kernels, finished(): pl.pallas_call(functools.partial(finish_kernel, lat_count), grid=(lat_row...  15.2 us
    pallas_call x1, Pallas kernels, gridded(): pl.pallas_call(functools.partial(grid_kernel, devices, cap, wide, cols, l...  11.8 us
    all_to_all x1, starting transfers between devices, shards(): lax.all_to_all(send, axes, split_axis=0, concat_axis=0, tiled=True)  7.31 us
    pallas_call x1, Pallas kernels, pack(): pl.pallas_call(functools.partial(pack_kernel, devices, lon_count, cap, co...  7.24 us
    pallas_call x1, Pallas kernels, projected(): pl.pallas_call(functools.partial(back_kernel, wide), grid=(lat_rows // BA...  4.97 us
    ppermute x1, starting transfers between devices, shards(): lax.ppermute(own_west, 'lon', [((i + 1) % lon_count, i) for i in range(lo...  3.53 us
  transfers between devices with their start and end apart: 5, of which 1 were waited for; matrix products, arithmetic and copies ran while one was open for 0% of the time, Pallas kernels for 23%

profile of v6, /device:TPU:0, one launch (start us, length us, event | category | flops | bytes accessed | tf_op | source)
XLA Modules:
  0.0 93.1 jit_solution(9391181046943795122)
XLA Ops:
  0.7 7.2 %shard_map.109 = bf16[16,272,128]{2,1,0:T(8,128)(2,1)} custom-call(s32[1]{0:T(128)S(6)} %copy.16.count_ref, s32[1,2048]{1,0:T(1,128)} %bitcast.17, s32[4,2048]{1,0:T(4,128)} %bitcast.15, s32[4,2048]{1,0:T(4,128)} %bitcast.16, bf16[2048,128]{1,0:T(8,128)(2,1)} %feat_ref.1), custom_call_target="tpu_custom_call" | custom-call | tf_op jit(solution)/shard_map/pallas_call | solution.py:126
  7.9 7.3 %all-to-all-start = ((bf16[32,136,128]{2,1,0:T(8,128)(2,1)}), bf16[32,136,128]{2,1,0:T(8,128)(2,1)S(1)}, u32[]{:S(2)}, u32[]{:S(2)}) async-start(bf16[32,136,128]{2,1,0:T(8,128)(2,1)} %bitcast.14), calls=%async_computation | async-start | bytes 2228224 | tf_op jit(solution)/shard_map/all_to_all | solution.py:576
  15.2 0.0 copy-start.1
  15.2 2.2 %copy-done.1 = bf16[90,90,256]{2,1,0:T(8,128)(2,1)S(1)} copy-done((bf16[90,90,256]{2,1,0:T(8,128)(2,1)S(1)}, bf16[90,90,256]{2,1,0:T(8,128)(2,1)}, u32[]{:S(2)}) %copy-start.1) | copy-done | bytes 4147224
  17.5 0.9 copy-done.3
  18.4 5.0 %shard_map.110.back_hbm = f32[65552,256]{1,0:T(8,128)} custom-call(bf16[90,90,256]{2,1,0:T(8,128)(2,1)S(1)} %copy-done.1, bf16[256,256]{1,0:T(8,128)(2,1)S(1)} %copy-done.3), custom_call_target="tpu_custom_call" | custom-call | tf_op jit(solution)/shard_map/pallas_call | solution.py:153
  23.3 20.9 %all-to-all-done = bf16[32,136,128]{2,1,0:T(8,128)(2,1)S(1)} async-done(((bf16[32,136,128]{2,1,0:T(8,128)(2,1)}), bf16[32,136,128]{2,1,0:T(8,128)(2,1)S(1)}, u32[]{:S(2)}, u32[]{:S(2)}) %all-to-all-start) | async-done | bytes 1114144 | tf_op jit(solution)/shard_map/all_to_all | solution.py:576
  44.2 0.0 copy-done.4
  44.2 0.0 copy-done.5
  44.2 11.8 %shard_map.111 = (bf16[90,96,256]{2,1,0:T(8,128)(2,1)S(1)}, bf16[2,96,256]{2,1,0:T(8,128)(2,1)S(1)}, bf16[2,96,256]{2,1,0:T(8,128)(2,1)S(1)}, bf16[2,96,256]{2,1,0:T(8,128)(2,1)S(1)}, bf16[2,96,256]{2,1,0:T(8,128)(2,1)S(1)}) custom-call(bf16[16,272,128]{2,1,0:T(8,128)(2,1)S(1)} %bitcast.11, f32[65552,256]{1,0:T(8,128)} %shard_map.110.back_hbm, ...), custom_call_target="tpu_custom_call" | custom-call | tf_op jit(solution)/shard_map/pallas_call | solution.py:308
  56.1 0.1 collective-permute-start
  56.1 3.5 %collective-permute-start.1 = (bf16[2,96,256]{2,1,0:T(8,128)(2,1)S(1)}, bf16[2,96,256]{2,1,0:T(8,128)(2,1)S(1)}, u32[]{:S(2)}, u32[]{:S(2)}) collective-permute-start(bf16[2,96,256]{2,1,0:T(8,128)(2,1)S(1)} %get-tuple-element.14.after_ref.own_west), channel_id=1, source_target_pairs={{1,0},{2,1},{3,2},{4,3},{5,4},{6,5},{7,6},{0,7},{9,8},{10,9},{11,1... | collective-permute-start | bytes 294920 | tf_op jit(solution)/shard_map/ppermute | solution.py:582
  59.7 0.0 copy-done
  59.7 8.0 %shard_map.112.after_ref.upper_in = bf16[4512,768]{1,0:T(8,128)(2,1)S(1)} custom-call(bf16[90,96,256]{2,1,0:T(8,128)(2,1)S(1)} %get-tuple-element.13.first_ref, bf16[3,768,256]{2,1,0:T(8,128)(2,1)S(1)} %bitcast.8, bf16[2,96,256]{2,1,0:T(8,128)(2,1)S(1)} %get-tuple-element.14.after_ref.own_west), custom_call_target="tpu_custom_call" | custom-call | tf_op jit(solution)/shard_map/pallas_call | solution.py:405
  67.7 0.0 collective-permute-done.west_ref
  67.7 0.0 collective-permute-done.1.east_ref
  67.8 0.1 collective-permute-start.3
  67.8 0.0 copy-start.2
  67.8 2.0 %collective-permute-start.2 = (bf16[2,96,256]{2,1,0:T(8,128)(2,1)S(1)}, bf16[2,96,256]{2,1,0:T(8,128)(2,1)S(1)}, u32[]{:S(2)}, u32[]{:S(2)}) collective-permute-start(bf16[2,96,256]{2,1,0:T(8,128)(2,1)S(1)} %get-tuple-element.18.after_ref), channel_id=1, source_target_pairs={{0,8},{8,0},{16,24},{24,16},{1,9},{9,1},{17,25},{25,17},{2,10},{10... | collective-permute-start | bytes 294920 | tf_op jit(solution)/shard_map/ppermute | solution.py:590
  69.8 8.0 %shard_map.114.lower_in = bf16[4512,768]{1,0:T(8,128)(2,1)S(1)} custom-call(bf16[90,96,256]{2,1,0:T(8,128)(2,1)S(1)} %get-tuple-element.13.first_ref, bf16[3,768,256]{2,1,0:T(8,128)(2,1)S(1)} %bitcast.9, bf16[2,96,256]{2,1,0:T(8,128)(2,1)S(1)} %get-tuple-element.18.after_ref), custom_call_target="tpu_custom_call" | custom-call | tf_op jit(solution)/shard_map/pallas_call | solution.py:405
  77.8 0.0 collective-permute-done.3.outer_ref
  77.8 0.0 collective-permute-done.2.inner_ref
  77.9 0.0 copy-done.2
  77.9 15.2 %shard_map.115 = (bf16[90,90,256]{2,1,0:T(8,128)(2,1)}, bf16[4512,768]{1,0:T(8,128)(2,1)S(1)}, bf16[4512,768]{1,0:T(8,128)(2,1)S(1)}) custom-call(bf16[4512,768]{1,0:T(8,128)(2,1)S(1)} %shard_map.112.after_ref.upper_in, bf16[4512,768]{1,0:T(8,128)(2,1)S(1)} %shard_map.114.lower_in, ...), custom_call_target="tpu_custom_call", output_to_operand_aliasing={{1}: (0, {}), {2}: (1, {})} | custom-call | tf_op jit(solution)/shard_map/pallas_call | solution.py:514
  (5 shorter events, 0.0 us)
Async XLA Ops:
  7.9 36.3 %all-to-all-start = ((bf16[32,136,128]{2,1,0:T(8,128)(2,1)}), bf16[32,136,128]{2,1,0:T(8,128)(2,1)S(1)}, u32[]{:S(2)}, u32[]{:S(2)}) async-start(bf16[32,136,128]{2,1,0:T(8,128)(2,1)} %bitcast.14), calls=%async_computation | async-start | bytes 2228224 | tf_op jit(solution)/shard_map/all_to_all | solution.py:576
  15.2 2.3 %copy-start.1 = (bf16[90,90,256]{2,1,0:T(8,128)(2,1)S(1)}, bf16[90,90,256]{2,1,0:T(8,128)(2,1)}, u32[]{:S(2)}) copy-start(bf16[90,90,256]{2,1,0:T(8,128)(2,1)} %back_ref.1) | copy-start | bytes 12441604
  17.5 0.9 copy-start.3
  18.4 25.8 %copy-start.4 = (bf16[128,256]{1,0:T(8,128)(2,1)S(1)}, bf16[128,256]{1,0:T(8,128)(2,1)}, u32[]{:S(2)}) copy-start(bf16[128,256]{1,0:T(8,128)(2,1)} %w_in_hbm.1) | copy-start | bytes 196612
  18.4 25.8 %copy-start.5 = (f32[256]{0:T(256)S(1)}, f32[256]{0:T(256)}, u32[]{:S(2)}) copy-start(f32[256]{0:T(256)} %param.19) | copy-start | bytes 3076
  44.2 15.4 %copy-start = (bf16[3,3,256,256]{3,2,1,0:T(8,128)(2,1)S(1)}, bf16[3,3,256,256]{3,2,1,0:T(8,128)(2,1)}, u32[]{:S(2)}) copy-start(bf16[3,3,256,256]{3,2,1,0:T(8,128)(2,1)} %param.20) | copy-start | bytes 3538948
  56.1 11.6 %collective-permute-start = (bf16[2,96,256]{2,1,0:T(8,128)(2,1)S(1)}, bf16[2,96,256]{2,1,0:T(8,128)(2,1)S(1)}, u32[]{:S(2)}, u32[]{:S(2)}) collective-permute-start(bf16[2,96,256]{2,1,0:T(8,128)(2,1)S(1)} %get-tuple-element.17.own_east), channel_id=1, source_target_pairs={{0,1},{1,2},{2,3},{3,4},{4,5},{5,6},{6,7},{7,0},{8,9},{9,10},{10,1... | collective-permute-start | bytes 294920 | tf_op jit(solution)/shard_map/ppermute | solution.py:581
  56.1 11.6 %collective-permute-start.1 = (bf16[2,96,256]{2,1,0:T(8,128)(2,1)S(1)}, bf16[2,96,256]{2,1,0:T(8,128)(2,1)S(1)}, u32[]{:S(2)}, u32[]{:S(2)}) collective-permute-start(bf16[2,96,256]{2,1,0:T(8,128)(2,1)S(1)} %get-tuple-element.14.after_ref.own_west), channel_id=1, source_target_pairs={{1,0},{2,1},{3,2},{4,3},{5,4},{6,5},{7,6},{0,7},{9,8},{10,9},{11,1... | collective-permute-start | bytes 294920 | tf_op jit(solution)/shard_map/ppermute | solution.py:582
  67.8 10.1 %collective-permute-start.3 = (bf16[2,96,256]{2,1,0:T(8,128)(2,1)S(1)}, bf16[2,96,256]{2,1,0:T(8,128)(2,1)S(1)}, u32[]{:S(2)}, u32[]{:S(2)}) collective-permute-start(bf16[2,96,256]{2,1,0:T(8,128)(2,1)S(1)} %get-tuple-element.19), channel_id=1, source_target_pairs={{8,16},{16,8},{0,4},{24,28},{9,17},{17,9},{1,5},{25,29},{10,18},{1... | collective-permute-start | bytes 294920 | tf_op jit(solution)/shard_map/ppermute | solution.py:591
  67.8 10.0 %copy-start.2 = (bf16[3,3,256,256]{3,2,1,0:T(8,128)(2,1)S(1)}, bf16[3,3,256,256]{3,2,1,0:T(8,128)(2,1)}, u32[]{:S(2)}) copy-start(bf16[3,3,256,256]{3,2,1,0:T(8,128)(2,1)} %param.21) | copy-start | bytes 3538948
  67.8 10.0 %collective-permute-start.2 = (bf16[2,96,256]{2,1,0:T(8,128)(2,1)S(1)}, bf16[2,96,256]{2,1,0:T(8,128)(2,1)S(1)}, u32[]{:S(2)}, u32[]{:S(2)}) collective-permute-start(bf16[2,96,256]{2,1,0:T(8,128)(2,1)S(1)} %get-tuple-element.18.after_ref), channel_id=1, source_target_pairs={{0,8},{8,0},{16,24},{24,16},{1,9},{9,1},{17,25},{25,17},{2,10},{10... | collective-permute-start | bytes 294920 | tf_op jit(solution)/shard_map/ppermute | solution.py:590

commit v7 on v6

--- a/solution.py
+++ b/solution.py
@@ -15,6 +15,7 @@
 CHUNK = 256
 HEAD = 768
 FINISH = 15
+UPPER = 30
 BF = jnp.bfloat16
 F32 = jnp.float32
 
@@ -378,15 +379,18 @@
     )(inner, outer, west, east, after)
 
 
-def inside_kernel(lead, place, first_ref, one_ref, after_ref, hid_ref, field):
-    lat_rows, wide, chans = first_ref.shape
-    half = lat_rows // 2
-
-    def load(r, _):
-        put(field, pl.multiple_of(r * wide, 16), first_ref[lead + r].astype(F32))
-        return 0
-
-    lax.fori_loop(0, half + 2, load, 0)
+def with_sides(value, sides, cols):
+    wide, chans = value.shape
+    last = wide - 16
+    row_id = lax.broadcasted_iota(jnp.int32, (16, chans), 0)
+    head, tail = value[:16], value[last:]
+    for k in range(2):
+        head = jnp.where(row_id == k, sides[k], head)
+        tail = jnp.where(row_id == cols + 2 + k - last, sides[2 + k], tail)
+    return jnp.concatenate([head, value[16:last], tail], axis=0)
+
+
+def convolve_rows(field, one_ref, hid_ref, place, count, wide):
     size = FINISH * wide
 
     def hidden(g, _):
@@ -395,21 +399,64 @@
         put(hid_ref, pl.multiple_of(begin + place * wide, 16), gelu(total))
         return 0
 
-    lax.fori_loop(0, half // FINISH, hidden, 0)
-
-
-def inside(first, one, after, lead, place):
-    lat_rows, wide, chans = first.shape
-    size = (lat_rows // 2 + 2) * wide
+    lax.fori_loop(0, count // FINISH, hidden, 0)
+
+
+def upper_kernel(first_ref, one_ref, after_ref, hid_ref, field):
+    wide = first_ref.shape[1]
+    count = field.shape[0] // wide
+
+    def load(r, _):
+        put(field, pl.multiple_of(r * wide, 16), first_ref[r].astype(F32))
+        return 0
+
+    lax.fori_loop(0, count, load, 0, unroll=4)
+    convolve_rows(field, one_ref, hid_ref, 2, count - 2, wide)
+
+
+def lower_kernel(cols, first_ref, one_ref, west_ref, east_ref, after_ref, hid_ref, field, side_scr):
+    lat_rows, wide, _ = first_ref.shape
+    count = field.shape[0] // wide
+    lead = lat_rows - count
+    side_scr[0:2] = west_ref[...].astype(F32)
+    side_scr[2:4] = east_ref[...].astype(F32)
+
+    def load(r, _):
+        sides = [side_scr[k, pl.ds(lead + r, 1), :] for k in range(4)]
+        value = with_sides(first_ref[lead + r].astype(F32), sides, cols)
+        put(field, pl.multiple_of(r * wide, 16), value)
+        return 0
+
+    lax.fori_loop(0, count, load, 0, unroll=2)
+    convolve_rows(field, one_ref, hid_ref, 0, count - 2, wide)
+
+
+def upper_part(first, one, after, rows):
+    _, wide, chans = first.shape
     whole = pl.BlockSpec(memory_space=pltpu.VMEM)
+    shape = ((rows + 2) * wide, 3 * chans)
     return pl.pallas_call(
-        functools.partial(inside_kernel, lead, place),
-        out_shape=jax.ShapeDtypeStruct((size, 3 * chans), BF),
+        upper_kernel,
+        out_shape=jax.ShapeDtypeStruct(shape, BF),
         in_specs=[whole, whole, pl.BlockSpec(memory_space=pl.ANY)],
         out_specs=whole,
-        scratch_shapes=[pltpu.VMEM((size, 3 * chans), BF)],
+        scratch_shapes=[pltpu.VMEM(shape, BF)],
         compiler_params=params(24),
     )(first, one, after)
+
+
+def lower_part(first, one, west, east, after, rows, cols):
+    _, wide, chans = first.shape
+    whole = pl.BlockSpec(memory_space=pltpu.VMEM)
+    shape = ((rows + 2) * wide, 3 * chans)
+    return pl.pallas_call(
+        functools.partial(lower_kernel, cols),
+        out_shape=jax.ShapeDtypeStruct(shape, BF),
+        in_specs=[whole] * 4 + [pl.BlockSpec(memory_space=pl.ANY)],
+        out_specs=whole,
+        scratch_shapes=[pltpu.VMEM(shape, BF), pltpu.VMEM((4, west.shape[1], chans), F32)],
+        compiler_params=params(24),
+    )(first, one, west, east, after)
 
 
 def finish_kernel(
@@ -420,63 +467,56 @@
     lat_rows, wide, chans = first_ref.shape
     rows, cols, _ = out_ref.shape
     block = rows * wide
-    half = lat_rows // 2
+    above = upper_ref.shape[0] // wide - 2
+    below = lat_rows - above
 
     @pl.when(group == 0)
     def _():
         lat_index = lax.axis_index("lat")
         even = lat_index % 2 == 0
-        row_id = lax.broadcasted_iota(jnp.int32, (wide, chans), 0)
         short_id = lax.broadcasted_iota(jnp.int32, (16, chans), 0)
+        lines = [west_ref[0], west_ref[1], own_west[0], own_west[1]]
+        lines += [own_east[0], own_east[1], east_ref[0], east_ref[1]]
+        lines = [line.astype(F32) for line in lines]
 
         def edge_row(north, k):
             return jnp.where(even == north, outer_ref[k].astype(F32), inner_ref[k].astype(F32))
 
         def own_row(r):
-            value = first_ref[r].astype(F32)
-            sides = [west_ref[0], west_ref[1], east_ref[0], east_ref[1]]
-            for side, col in zip(sides, (0, 1, cols + 2, cols + 3)):
-                value = jnp.where(row_id == col, side.astype(F32)[r : r + 1], value)
-            return value
-
-        lines = [edge_row(True, 1), edge_row(True, 0), own_row(0), own_row(1)]
-        lines += [own_row(lat_rows - 2), own_row(lat_rows - 1), edge_row(False, 0), edge_row(False, 1)]
-        for n, line in enumerate(lines):
+            sides = [lines[n][r : r + 1] for n in (0, 1, 6, 7)]
+            return with_sides(first_ref[r].astype(F32), sides, cols)
+
+        rims = [edge_row(True, 1), edge_row(True, 0), own_row(0), own_row(1)]
+        rims += [own_row(lat_rows - 2), own_row(lat_rows - 1), edge_row(False, 0), edge_row(False, 1)]
+        for n, line in enumerate(rims):
             put(rim, n * wide, line)
-        ends = (
-            (0, upper_ref, 0, lat_index == 0),
-            (5, lower_ref, half + 1, lat_index == lat_count - 1),
-        )
-        for begin, ref, index, pole in ends:
-            total = jnp.zeros((wide, chans), F32)
-            for a in range(3):
-                tap = jnp.where(pole, 2 - a, a)
-                total = total + dot(rim[(begin + a) * wide : (begin + a + 1) * wide, :], one_ref[tap])
-            put(ref, index * wide, gelu(total))
-        total = jnp.zeros((2 * wide, chans), F32)
+        size = cols_scr.shape[1]
+        fields = []
         for a in range(3):
-            pair = [rim[(n + a) * wide : (n + a + 1) * wide, :] for n in (1, 4)]
-            total = total + dot(jnp.concatenate(pair, axis=0), one_ref[a])
+            top = jnp.where(lat_index == 0, 2 - a, a)
+            bottom = jnp.where(lat_index == lat_count - 1, 7 - a, 5 + a)
+            parts = [
+                rim[pl.ds(pl.multiple_of(n * wide, 16), wide), :] for n in (top, 1 + a, 4 + a, bottom)
+            ]
+            for n in (0, 1, 4, 5):
+                window = [lines[n + b][a : a + size].astype(BF) for b in range(3)]
+                parts.append(jnp.concatenate(window, axis=1))
+            fields.append(jnp.concatenate(parts, axis=0))
+        total = jnp.zeros((4 * wide + 4 * size, chans), F32)
+        for a in range(3):
+            total = total + dot(fields[a], one_ref[a])
         total = gelu(total)
-        put(upper_ref, wide, total[:wide])
-        put(lower_ref, half * wide, total[wide:])
-
-        lines = [west_ref[0], west_ref[1], own_west[0], own_west[1]]
-        lines += [own_east[0], own_east[1], east_ref[0], east_ref[1]]
-        windows = [jnp.concatenate(lines[n : n + 3], axis=1) for n in (0, 1, 4, 5)]
-        windows = jnp.concatenate(windows, axis=0)
-        size = windows.shape[0]
-        total = pltpu.roll(dot(windows, one_ref[0]), 1, axis=0) + dot(windows, one_ref[1])
-        total = total + pltpu.roll(dot(windows, one_ref[2]), size - 1, axis=0)
-        total = gelu(total)
-        tall = size // 4
+        put(upper_ref, 0, total[:wide])
+        put(upper_ref, wide, total[wide : 2 * wide])
+        put(lower_ref, below * wide, total[2 * wide : 3 * wide])
+        put(lower_ref, (below + 1) * wide, total[3 * wide : 4 * wide])
         for n in range(4):
-            cols_scr[n] = total[n * tall : (n + 1) * tall]
+            cols_scr[n] = total[4 * wide + n * size : 4 * wide + (n + 1) * size]
         last = wide - 16
 
-        def patch(ref, shift, r, _):
+        def patch(r, _):
             fixes = [cols_scr[n, pl.ds(r, 1), :] for n in range(4)]
-            begin = pl.multiple_of((r - shift) * wide, 16)
+            begin = pl.multiple_of((r + 2) * wide, 16)
             for b in range(3):
                 lanes = slice(b * chans, (b + 1) * chans)
                 for start in (0, last):
@@ -486,14 +526,13 @@
                         if 0 <= col - b - start < 16
                     ]
                     if edits:
-                        value = ref[pl.ds(begin + start, 16), lanes].astype(F32)
+                        value = upper_ref[pl.ds(begin + start, 16), lanes].astype(F32)
                         for at, fix in edits:
                             value = jnp.where(short_id == at, fix, value)
-                        ref[pl.ds(begin + start, 16), lanes] = value.astype(BF)
+                        upper_ref[pl.ds(begin + start, 16), lanes] = value.astype(BF)
             return 0
 
-        lax.fori_loop(1, half + 1, functools.partial(patch, upper_ref, -1), 0, unroll=9)
-        lax.fori_loop(half - 1, lat_rows - 1, functools.partial(patch, lower_ref, half - 1), 0, unroll=9)
+        lax.fori_loop(0, above, patch, 0, unroll=10)
 
     def second(ref, first_group):
         begin = pl.multiple_of((group - first_group) * block, 16)
@@ -504,8 +543,8 @@
         for i in range(rows):
             out_ref[i] = result[i * wide : i * wide + cols]
 
-    pl.when(group < half // rows)(lambda: second(upper_ref, 0))
-    pl.when(group >= half // rows)(lambda: second(lower_ref, half // rows))
+    pl.when(group < above // rows)(lambda: second(upper_ref, 0))
+    pl.when(group >= above // rows)(lambda: second(lower_ref, above // rows))
 
 
 def finished(upper, lower, first, sides, one, two, cols, lat_count):
@@ -524,7 +563,7 @@
         input_output_aliases={0: 1, 1: 2},
         scratch_shapes=[
             pltpu.VMEM((8 * wide, 3 * chans), BF),
-            pltpu.VMEM((4, sides[0].shape[1], chans), F32),
+            pltpu.VMEM((4, -(-UPPER // 16) * 16, chans), F32),
         ],
         compiler_params=params(26),
     )(upper, lower, first, *sides, one, two)
@@ -582,11 +621,10 @@
     east = lax.ppermute(own_west, "lon", [((i + 1) % lon_count, i) for i in range(lon_count)])
     one = conv_one.reshape(3, 3 * chans, chans)
     two = conv_two.reshape(3, 3 * chans, chans)
-    half = lat_rows // 2
-    upper = inside(first, one, own_west, 0, 2)
+    upper = upper_part(first, one, own_west, UPPER)
     inner_row, outer_row = bordered(inner_row, outer_row, west, east, upper, lat_rows, cols)
     inner, outer = row_pairs(lat_count, lon_count)
-    lower = inside(first, one, inner_row, half - 2, 0)
+    lower = lower_part(first, one, west, east, inner_row, lat_rows - UPPER, cols)
     inner_row = lax.ppermute(inner_row, axes, inner)
     outer_row = lax.ppermute(outer_row, axes, outer)
     sides = (own_west, own_east, west, east, inner_row, outer_row)

time: 93.4 us -> 92.2 us (0.987)
  Pallas kernels: 55.4 us -> 54.2 us
    pallas_call x1, Pallas kernels: 15.2 us -> 13.9 us  [finished(): pl.pallas_call(functools.partial(finish_kernel, lat_count), grid=(lat_row...]
where the time goes in v7:
time: 92.2 us; the launch traced here: 91.9 us
  Pallas kernels  54.2 us (59%)
  waiting for transfers between devices  20.9 us (23%)
  starting transfers between devices  12.9 us (14%)
  local copies, waits for them, and re-layouts  3.17 us (3%)
    all_to_all x1, waiting for transfers between devices, shards(): lax.all_to_all(send, axes, split_axis=0, concat_axis=0, tiled=True)  20.8 us
    pallas_call x1, Pallas kernels, finished(): pl.pallas_call(functools.partial(finish_kernel, lat_count), grid=(lat_row...  13.9 us
    pallas_call x1, Pallas kernels, gridded(): pl.pallas_call(functools.partial(grid_kernel, devices, cap, wide, cols, l...  11.8 us
    pallas_call x1, Pallas kernels, lower_part(): pl.pallas_call(functools.partial(lower_kernel, cols), out_shape=jax.Shape...  11 us
    all_to_all x1, starting transfers between devices, shards(): lax.all_to_all(send, axes, split_axis=0, concat_axis=0, tiled=True)  7.3 us
    pallas_call x1, Pallas kernels, pack(): pl.pallas_call(functools.partial(pack_kernel, devices, lon_count, cap, co...  7.24 us
    pallas_call x1, Pallas kernels, upper_part(): pl.pallas_call(upper_kernel, out_shape=jax.ShapeDtypeStruct(shape, BF), i...  5.27 us
    pallas_call x1, Pallas kernels, projected(): pl.pallas_call(functools.partial(back_kernel, wide), grid=(lat_rows // BA...  4.98 us
  transfers between devices with their start and end apart: 5, of which 1 were waited for; matrix products, arithmetic and copies ran while one was open for 0% of the time, Pallas kernels for 23%

profile of v7, /device:TPU:0, one launch (start us, length us, event | category | flops | bytes accessed | tf_op | source)
XLA Modules:
  0.0 91.9 jit_solution(9684499539400176421)
XLA Ops:
  0.7 7.2 %shard_map.109 = bf16[16,272,128]{2,1,0:T(8,128)(2,1)} custom-call(s32[1]{0:T(128)S(6)} %copy.16.count_ref, s32[1,2048]{1,0:T(1,128)} %bitcast.17, s32[4,2048]{1,0:T(4,128)} %bitcast.15, s32[4,2048]{1,0:T(4,128)} %bitcast.16, bf16[2048,128]{1,0:T(8,128)(2,1)} %feat_ref.1), custom_call_target="tpu_custom_call" | custom-call | tf_op jit(solution)/shard_map/pallas_call | solution.py:127
  7.9 7.3 %all-to-all-start = ((bf16[32,136,128]{2,1,0:T(8,128)(2,1)}), bf16[32,136,128]{2,1,0:T(8,128)(2,1)S(1)}, u32[]{:S(2)}, u32[]{:S(2)}) async-start(bf16[32,136,128]{2,1,0:T(8,128)(2,1)} %bitcast.14), calls=%async_computation | async-start | bytes 2228224 | tf_op jit(solution)/shard_map/all_to_all | solution.py:615
  15.2 0.0 copy-start.1
  15.2 2.2 %copy-done.1 = bf16[90,90,256]{2,1,0:T(8,128)(2,1)S(1)} copy-done((bf16[90,90,256]{2,1,0:T(8,128)(2,1)S(1)}, bf16[90,90,256]{2,1,0:T(8,128)(2,1)}, u32[]{:S(2)}) %copy-start.1) | copy-done | bytes 4147224
  17.5 0.9 copy-done.3
  18.4 5.0 %shard_map.110.back_hbm = f32[65552,256]{1,0:T(8,128)} custom-call(bf16[90,90,256]{2,1,0:T(8,128)(2,1)S(1)} %copy-done.1, bf16[256,256]{1,0:T(8,128)(2,1)S(1)} %copy-done.3), custom_call_target="tpu_custom_call" | custom-call | tf_op jit(solution)/shard_map/pallas_call | solution.py:154
  23.4 20.8 %all-to-all-done = bf16[32,136,128]{2,1,0:T(8,128)(2,1)S(1)} async-done(((bf16[32,136,128]{2,1,0:T(8,128)(2,1)}), bf16[32,136,128]{2,1,0:T(8,128)(2,1)S(1)}, u32[]{:S(2)}, u32[]{:S(2)}) %all-to-all-start) | async-done | bytes 1114144 | tf_op jit(solution)/shard_map/all_to_all | solution.py:615
  44.2 0.0 copy-done.4
  44.2 0.0 copy-done.5
  44.2 11.8 %shard_map.111 = (bf16[90,96,256]{2,1,0:T(8,128)(2,1)S(1)}, bf16[2,96,256]{2,1,0:T(8,128)(2,1)S(1)}, bf16[2,96,256]{2,1,0:T(8,128)(2,1)S(1)}, bf16[2,96,256]{2,1,0:T(8,128)(2,1)S(1)}, bf16[2,96,256]{2,1,0:T(8,128)(2,1)S(1)}) custom-call(bf16[16,272,128]{2,1,0:T(8,128)(2,1)S(1)} %bitcast.11, f32[65552,256]{1,0:T(8,128)} %shard_map.110.back_hbm, ...), custom_call_target="tpu_custom_call" | custom-call | tf_op jit(solution)/shard_map/pallas_call | solution.py:309
  56.0 0.1 collective-permute-start
  56.1 3.5 %collective-permute-start.1 = (bf16[2,96,256]{2,1,0:T(8,128)(2,1)S(1)}, bf16[2,96,256]{2,1,0:T(8,128)(2,1)S(1)}, u32[]{:S(2)}, u32[]{:S(2)}) collective-permute-start(bf16[2,96,256]{2,1,0:T(8,128)(2,1)S(1)} %get-tuple-element.14.after_ref.own_west), channel_id=1, source_target_pairs={{1,0},{2,1},{3,2},{4,3},{5,4},{6,5},{7,6},{0,7},{9,8},{10,9},{11,1... | collective-permute-start | bytes 294920 | tf_op jit(solution)/shard_map/ppermute | solution.py:621
  59.6 0.0 copy-done
  59.6 5.3 %shard_map.112.after_ref.upper_in = bf16[3072,768]{1,0:T(8,128)(2,1)S(1)} custom-call(bf16[90,96,256]{2,1,0:T(8,128)(2,1)S(1)} %get-tuple-element.13.first_ref, bf16[3,768,256]{2,1,0:T(8,128)(2,1)S(1)} %bitcast.8, bf16[2,96,256]{2,1,0:T(8,128)(2,1)S(1)} %get-tuple-element.14.after_ref.own_west), custom_call_target="tpu_custom_call" | custom-call | tf_op jit(solution)/shard_map/pallas_call | solution.py:438
  64.9 0.0 collective-permute-done.west_ref
  64.9 0.0 collective-permute-done.1.east_ref
  65.0 0.1 collective-permute-start.3
  65.1 0.0 copy-start.2
  65.1 2.0 %collective-permute-start.2 = (bf16[2,96,256]{2,1,0:T(8,128)(2,1)S(1)}, bf16[2,96,256]{2,1,0:T(8,128)(2,1)S(1)}, u32[]{:S(2)}, u32[]{:S(2)}) collective-permute-start(bf16[2,96,256]{2,1,0:T(8,128)(2,1)S(1)} %get-tuple-element.18.after_ref), channel_id=1, source_target_pairs={{0,8},{8,0},{16,24},{24,16},{1,9},{9,1},{17,25},{25,17},{2,10},{10... | collective-permute-start | bytes 294920 | tf_op jit(solution)/shard_map/ppermute | solution.py:628
  67.0 11.0 %shard_map.114.lower_in = bf16[5952,768]{1,0:T(8,128)(2,1)S(1)} custom-call(bf16[90,96,256]{2,1,0:T(8,128)(2,1)S(1)} %get-tuple-element.13.first_ref, bf16[3,768,256]{2,1,0:T(8,128)(2,1)S(1)} %bitcast.9, bf16[2,96,256]{2,1,0:T(8,128)(2,1)S(1)} %collective-permute-done.west_ref, bf16[2,96,256]{2,1,0:T(8,128)(2,1)S(1)} %collective-permute-done.1.east_ref, ...), custom_call_target="tpu_custom_call" | custom-call | tf_op jit(solution)/shard_map/pallas_call | solution.py:452
  78.0 0.0 collective-permute-done.3.outer_ref
  78.0 0.0 collective-permute-done.2.inner_ref
  78.0 0.0 copy-done.2
  78.1 13.9 %shard_map.115 = (bf16[90,90,256]{2,1,0:T(8,128)(2,1)}, bf16[3072,768]{1,0:T(8,128)(2,1)S(1)}, bf16[5952,768]{1,0:T(8,128)(2,1)S(1)}) custom-call(bf16[3072,768]{1,0:T(8,128)(2,1)S(1)} %shard_map.112.after_ref.upper_in, bf16[5952,768]{1,0:T(8,128)(2,1)S(1)} %shard_map.114.lower_in, ...), custom_call_target="tpu_custom_call", output_to_operand_aliasing={{1}: (0, {}), {2}: (1, {})} | custom-call | tf_op jit(solution)/shard_map/pallas_call | solution.py:553
  (5 shorter events, 0.0 us)
Async XLA Ops:
  7.9 36.3 %all-to-all-start = ((bf16[32,136,128]{2,1,0:T(8,128)(2,1)}), bf16[32,136,128]{2,1,0:T(8,128)(2,1)S(1)}, u32[]{:S(2)}, u32[]{:S(2)}) async-start(bf16[32,136,128]{2,1,0:T(8,128)(2,1)} %bitcast.14), calls=%async_computation | async-start | bytes 2228224 | tf_op jit(solution)/shard_map/all_to_all | solution.py:615
  15.2 2.3 %copy-start.1 = (bf16[90,90,256]{2,1,0:T(8,128)(2,1)S(1)}, bf16[90,90,256]{2,1,0:T(8,128)(2,1)}, u32[]{:S(2)}) copy-start(bf16[90,90,256]{2,1,0:T(8,128)(2,1)} %back_ref.1) | copy-start | bytes 12441604
  17.5 0.9 copy-start.3
  18.4 25.8 %copy-start.4 = (bf16[128,256]{1,0:T(8,128)(2,1)S(1)}, bf16[128,256]{1,0:T(8,128)(2,1)}, u32[]{:S(2)}) copy-start(bf16[128,256]{1,0:T(8,128)(2,1)} %w_in_hbm.1) | copy-start | bytes 196612
  18.4 25.8 %copy-start.5 = (f32[256]{0:T(256)S(1)}, f32[256]{0:T(256)}, u32[]{:S(2)}) copy-start(f32[256]{0:T(256)} %param.19) | copy-start | bytes 3076
  44.2 15.4 %copy-start = (bf16[3,3,256,256]{3,2,1,0:T(8,128)(2,1)S(1)}, bf16[3,3,256,256]{3,2,1,0:T(8,128)(2,1)}, u32[]{:S(2)}) copy-start(bf16[3,3,256,256]{3,2,1,0:T(8,128)(2,1)} %param.20) | copy-start | bytes 3538948
  56.0 8.9 %collective-permute-start = (bf16[2,96,256]{2,1,0:T(8,128)(2,1)S(1)}, bf16[2,96,256]{2,1,0:T(8,128)(2,1)S(1)}, u32[]{:S(2)}, u32[]{:S(2)}) collective-permute-start(bf16[2,96,256]{2,1,0:T(8,128)(2,1)S(1)} %get-tuple-element.15.own_east), channel_id=1, source_target_pairs={{0,1},{1,2},{2,3},{3,4},{4,5},{5,6},{6,7},{7,0},{8,9},{9,10},{10,1... | collective-permute-start | bytes 294920 | tf_op jit(solution)/shard_map/ppermute | solution.py:620
  56.1 8.8 %collective-permute-start.1 = (bf16[2,96,256]{2,1,0:T(8,128)(2,1)S(1)}, bf16[2,96,256]{2,1,0:T(8,128)(2,1)S(1)}, u32[]{:S(2)}, u32[]{:S(2)}) collective-permute-start(bf16[2,96,256]{2,1,0:T(8,128)(2,1)S(1)} %get-tuple-element.14.after_ref.own_west), channel_id=1, source_target_pairs={{1,0},{2,1},{3,2},{4,3},{5,4},{6,5},{7,6},{0,7},{9,8},{10,9},{11,1... | collective-permute-start | bytes 294920 | tf_op jit(solution)/shard_map/ppermute | solution.py:621
  65.0 13.0 %collective-permute-start.3 = (bf16[2,96,256]{2,1,0:T(8,128)(2,1)S(1)}, bf16[2,96,256]{2,1,0:T(8,128)(2,1)S(1)}, u32[]{:S(2)}, u32[]{:S(2)}) collective-permute-start(bf16[2,96,256]{2,1,0:T(8,128)(2,1)S(1)} %get-tuple-element.19), channel_id=1, source_target_pairs={{8,16},{16,8},{0,4},{24,28},{9,17},{17,9},{1,5},{25,29},{10,18},{1... | collective-permute-start | bytes 294920 | tf_op jit(solution)/shard_map/ppermute | solution.py:629
  65.1 13.0 %copy-start.2 = (bf16[3,3,256,256]{3,2,1,0:T(8,128)(2,1)S(1)}, bf16[3,3,256,256]{3,2,1,0:T(8,128)(2,1)}, u32[]{:S(2)}) copy-start(bf16[3,3,256,256]{3,2,1,0:T(8,128)(2,1)} %param.21) | copy-start | bytes 3538948
  65.1 13.0 %collective-permute-start.2 = (bf16[2,96,256]{2,1,0:T(8,128)(2,1)S(1)}, bf16[2,96,256]{2,1,0:T(8,128)(2,1)S(1)}, u32[]{:S(2)}, u32[]{:S(2)}) collective-permute-start(bf16[2,96,256]{2,1,0:T(8,128)(2,1)S(1)} %get-tuple-element.18.after_ref), channel_id=1, source_target_pairs={{0,8},{8,0},{16,24},{24,16},{1,9},{9,1},{17,25},{25,17},{2,10},{10... | collective-permute-start | bytes 294920 | tf_op jit(solution)/shard_map/ppermute | solution.py:628

commit v8 on v7

--- a/solution.py
+++ b/solution.py
@@ -35,10 +35,12 @@
 
 
 def pack_kernel(
-    devices, lon_count, cap, cols, bands, count_ref, dest_ref, cells_ref, gauss_ref, feat_ref, send_ref,
-    ext_ref, hot_ref, sorted_ref, place_ref, place_smem, sem,
+    devices, lon_count, cap, cols, bands, count_ref, dest_ref, cells_ref, gauss_ref, feat_hbm, send_hbm,
+    ext_ref, hot_ref, sorted_ref, place_ref, place_smem, send_ref, sem, feat_sem, send_sems,
 ):
-    nrows, nfeat = feat_ref.shape
+    nrows, nfeat = feat_hbm.shape
+    fetch = pltpu.make_async_copy(feat_hbm, ext_ref.at[:, pl.ds(0, nfeat)], feat_sem)
+    fetch.start()
     step = 256
     classes = 2 * bands
     kinds = devices * classes
@@ -54,7 +56,6 @@
     ratio = gauss_ref[...].astype(F32) * (1.0 / GBINS)
     weight = jnp.exp(-3.0 * ratio * ratio)
     meta = jnp.concatenate([lat, lon, weight, jnp.zeros((nfeat - 2 - KCELL, nrows), F32)], axis=0)
-    ext_ref[:, :nfeat] = feat_ref[...]
     ext_ref[:, nfeat:] = meta.T.astype(BF)
     hot_ref[...] = (lax.broadcasted_iota(jnp.int32, (kinds, nrows), 0) == kind).astype(F32).astype(BF)
     counts = dot(hot_ref[...], jnp.ones((nrows, nfeat), BF))
@@ -93,6 +94,7 @@
     place = jnp.where(live, place, -1.0)
     slot = lax.broadcasted_iota(jnp.int32, (step, nrows), 0).astype(F32)
     span = sorted_ref.shape[0]
+    fetch.wait()
     for k in range(-(-(nrows + 8 * devices) // step)):
         pick = (slot == place - k * step).astype(F32).astype(BF)
         sorted_ref[k * step : (k + 1) * step, :] = dot(pick, ext_ref[...])
@@ -115,9 +117,15 @@
         plain = jnp.concatenate([rows_a, side_a, rows_b, side_b], axis=0)
         turned = jnp.concatenate([side_a, rows_a, side_b, rows_b], axis=0)
         send_ref[p] = jnp.where(odd, turned, plain).astype(BF)
+        pltpu.make_async_copy(send_ref.at[p], send_hbm.at[p], send_sems.at[p]).start()
         return 0
 
+    def sent(p, _):
+        pltpu.make_async_copy(send_ref.at[p], send_hbm.at[p], send_sems.at[p]).wait()
+        return 0
+
     lax.fori_loop(0, devices // 2, pair, 0, unroll=2)
+    lax.fori_loop(0, devices // 2, sent, 0)
 
 
 def pack(count, dest, cells, gauss, feats, devices, lon_count, cap, cols, bands):
@@ -127,15 +135,19 @@
     return pl.pallas_call(
         functools.partial(pack_kernel, devices, lon_count, cap, cols, bands),
         out_shape=jax.ShapeDtypeStruct((devices // 2, 2 * (cap + META), nfeat), BF),
-        in_specs=[pl.BlockSpec(memory_space=pltpu.SMEM)] + [pl.BlockSpec(memory_space=pltpu.VMEM)] * 4,
-        out_specs=pl.BlockSpec(memory_space=pltpu.VMEM),
+        in_specs=[pl.BlockSpec(memory_space=pltpu.SMEM)] + [pl.BlockSpec(memory_space=pltpu.VMEM)] * 3
+        + [pl.BlockSpec(memory_space=pl.ANY)],
+        out_specs=pl.BlockSpec(memory_space=pl.ANY),
         scratch_shapes=[
             pltpu.VMEM((nrows, 2 * nfeat), BF),
             pltpu.VMEM((kinds, nrows), BF),
             pltpu.VMEM((span, 2 * nfeat), F32),
             pltpu.VMEM((8, nfeat), jnp.int32),
             pltpu.SMEM((8, nfeat), jnp.int32),
+            pltpu.VMEM((devices // 2, 2 * (cap + META), nfeat), BF),
             pltpu.SemaphoreType.DMA,
+            pltpu.SemaphoreType.DMA,
+            pltpu.SemaphoreType.DMA((devices // 2,)),
         ],
         compiler_params=params(56),
     )(count, dest, cells, gauss, feats)
@@ -178,17 +190,20 @@
     rows = lat_rows // lat_bands
     slots = devices * cap
     span = rows * wide
-    fetch = pltpu.make_async_copy(
-        back_hbm.at[pl.ds(pl.multiple_of(band * span, 16), span), :], back_ref, sems.at[0]
-    )
-    fetch.start()
+
+    def fetch(b):
+        begin = pl.multiple_of(b * span, 16)
+        return pltpu.make_async_copy(back_hbm.at[pl.ds(begin, span), :], back_ref.at[b], sems.at[b])
+
     loads = [
-        pltpu.make_async_copy(w_in_hbm, w_in_ref, sems.at[1]),
-        pltpu.make_async_copy(w_dens_hbm, w_dens_ref, sems.at[2]),
+        pltpu.make_async_copy(w_in_hbm, w_in_ref, sems.at[lat_bands]),
+        pltpu.make_async_copy(w_dens_hbm, w_dens_ref, sems.at[lat_bands + 1]),
     ]
 
     @pl.when(band == 0)
     def _():
+        for b in range(lat_bands):
+            fetch(b).start()
         for load in loads:
             load.start()
 
@@ -267,7 +282,7 @@
 
     acc_ref[...] = piece(0, HEAD)
     lax.fori_loop(HEAD // CHUNK, (total + CHUNK - 1) // CHUNK, more, 0)
-    fetch.wait()
+    fetch(band).wait()
 
     @pl.when(band == 0)
     def _():
@@ -276,7 +291,7 @@
 
     for g in range(0, rows, GROUP):
         sums = acc_ref[g * wide : (g + GROUP) * wide, :]
-        start = back_ref[g * wide : (g + GROUP) * wide, :]
+        start = back_ref[band, g * wide : (g + GROUP) * wide, :]
         density = sums[:, nfeat:]
         normalized = (sums[:, :nfeat] / (density + 1.0)).astype(BF)
         start = start + dot(normalized, w_in_ref[...])
@@ -329,12 +344,12 @@
             pltpu.VMEM((devices, nfeat), jnp.int32),
             pltpu.SMEM((devices, nfeat), jnp.int32),
             pltpu.SemaphoreType.DMA,
-            pltpu.VMEM((BAND * wide, chans), F32),
+            pltpu.VMEM((lat_rows // BAND, BAND * wide, chans), F32),
             pltpu.VMEM(w_in.shape, BF),
             pltpu.VMEM(w_dens.shape, F32),
-            pltpu.SemaphoreType.DMA((3,)),
+            pltpu.SemaphoreType.DMA((lat_rows // BAND + 2,)),
         ],
-        compiler_params=params(32),
+        compiler_params=params(42),
     )(recv, back, w_in, w_dens)
 
 

time: 92.2 us -> 92.2 us (level)
  no operation moved by 1% of the time
where the time goes in v8:
time: 92.2 us; the launch traced here: 91.9 us
  Pallas kernels  54.1 us (59%)
  waiting for transfers between devices  20.9 us (23%)
  starting transfers between devices  12.9 us (14%)
  local copies, waits for them, and re-layouts  3.17 us (3%)
    all_to_all x1, waiting for transfers between devices, shards(): lax.all_to_all(send, axes, split_axis=0, concat_axis=0, tiled=True)  20.9 us
    pallas_call x1, Pallas kernels, finished(): pl.pallas_call(functools.partial(finish_kernel, lat_count), grid=(lat_row...  13.9 us
    pallas_call x1, Pallas kernels, gridded(): pl.pallas_call(functools.partial(grid_kernel, devices, cap, wide, cols, l...  11.9 us
    pallas_call x1, Pallas kernels, lower_part(): pl.pallas_call(functools.partial(lower_kernel, cols), out_shape=jax.Shape...  11 us
    all_to_all x1, starting transfers between devices, shards(): lax.all_to_all(send, axes, split_axis=0, concat_axis=0, tiled=True)  7.31 us
    pallas_call x1, Pallas kernels, pack(): pl.pallas_call(functools.partial(pack_kernel, devices, lon_count, cap, co...  7.1 us
    pallas_call x1, Pallas kernels, upper_part(): pl.pallas_call(upper_kernel, out_shape=jax.ShapeDtypeStruct(shape, BF), i...  5.26 us
    pallas_call x1, Pallas kernels, projected(): pl.pallas_call(functools.partial(back_kernel, wide), grid=(lat_rows // BA...  4.97 us
  transfers between devices with their start and end apart: 5, of which 1 were waited for; matrix products, arithmetic and copies ran while one was open for 0% of the time, Pallas kernels for 23%

profile of v8, /device:TPU:0, one launch (start us, length us, event | category | flops | bytes accessed | tf_op | source)
XLA Modules:
  0.0 91.9 jit_solution(5704112018882938635)
XLA Ops:
  0.7 7.1 %shard_map.109 = bf16[16,272,128]{2,1,0:T(8,128)(2,1)} custom-call(s32[1]{0:T(128)S(6)} %copy.16.count_ref, s32[1,2048]{1,0:T(1,128)} %bitcast.17, s32[4,2048]{1,0:T(4,128)} %bitcast.15, s32[4,2048]{1,0:T(4,128)} %bitcast.16, bf16[2048,128]{1,0:T(8,128)(2,1)} %feat_hbm.1), custom_call_target="tpu_custom_call" | custom-call | tf_op jit(solution)/shard_map/pallas_call | solution.py:135
  7.8 7.3 %all-to-all-start = ((bf16[32,136,128]{2,1,0:T(8,128)(2,1)}), bf16[32,136,128]{2,1,0:T(8,128)(2,1)S(1)}, u32[]{:S(2)}, u32[]{:S(2)}) async-start(bf16[32,136,128]{2,1,0:T(8,128)(2,1)} %bitcast.14), calls=%async_computation | async-start | bytes 2228224 | tf_op jit(solution)/shard_map/all_to_all | solution.py:630
  15.1 0.0 copy-start.1
  15.1 2.2 %copy-done.1 = bf16[90,90,256]{2,1,0:T(8,128)(2,1)S(1)} copy-done((bf16[90,90,256]{2,1,0:T(8,128)(2,1)S(1)}, bf16[90,90,256]{2,1,0:T(8,128)(2,1)}, u32[]{:S(2)}) %copy-start.1) | copy-done | bytes 4147224
  17.3 0.9 copy-done.3
  18.2 5.0 %shard_map.110.back_hbm = f32[65552,256]{1,0:T(8,128)} custom-call(bf16[90,90,256]{2,1,0:T(8,128)(2,1)S(1)} %copy-done.1, bf16[256,256]{1,0:T(8,128)(2,1)S(1)} %copy-done.3), custom_call_target="tpu_custom_call" | custom-call | tf_op jit(solution)/shard_map/pallas_call | solution.py:166
  23.2 20.9 %all-to-all-done = bf16[32,136,128]{2,1,0:T(8,128)(2,1)S(1)} async-done(((bf16[32,136,128]{2,1,0:T(8,128)(2,1)}), bf16[32,136,128]{2,1,0:T(8,128)(2,1)S(1)}, u32[]{:S(2)}, u32[]{:S(2)}) %all-to-all-start) | async-done | bytes 1114144 | tf_op jit(solution)/shard_map/all_to_all | solution.py:630
  44.1 0.0 copy-done.4
  44.1 0.0 copy-done.5
  44.1 11.9 %shard_map.111 = (bf16[90,96,256]{2,1,0:T(8,128)(2,1)S(1)}, bf16[2,96,256]{2,1,0:T(8,128)(2,1)S(1)}, bf16[2,96,256]{2,1,0:T(8,128)(2,1)S(1)}, bf16[2,96,256]{2,1,0:T(8,128)(2,1)S(1)}, bf16[2,96,256]{2,1,0:T(8,128)(2,1)S(1)}) custom-call(bf16[16,272,128]{2,1,0:T(8,128)(2,1)S(1)} %bitcast.11, f32[65552,256]{1,0:T(8,128)} %shard_map.110.back_hbm, ...), custom_call_target="tpu_custom_call" | custom-call | tf_op jit(solution)/shard_map/pallas_call | solution.py:324
  56.0 0.1 collective-permute-start
  56.0 3.5 %collective-permute-start.1 = (bf16[2,96,256]{2,1,0:T(8,128)(2,1)S(1)}, bf16[2,96,256]{2,1,0:T(8,128)(2,1)S(1)}, u32[]{:S(2)}, u32[]{:S(2)}) collective-permute-start(bf16[2,96,256]{2,1,0:T(8,128)(2,1)S(1)} %get-tuple-element.14.after_ref.own_west), channel_id=1, source_target_pairs={{1,0},{2,1},{3,2},{4,3},{5,4},{6,5},{7,6},{0,7},{9,8},{10,9},{11,1... | collective-permute-start | bytes 294920 | tf_op jit(solution)/shard_map/ppermute | solution.py:636
  59.6 0.0 copy-done
  59.6 5.3 %shard_map.112.after_ref.upper_in = bf16[3072,768]{1,0:T(8,128)(2,1)S(1)} custom-call(bf16[90,96,256]{2,1,0:T(8,128)(2,1)S(1)} %get-tuple-element.13.first_ref, bf16[3,768,256]{2,1,0:T(8,128)(2,1)S(1)} %bitcast.8, bf16[2,96,256]{2,1,0:T(8,128)(2,1)S(1)} %get-tuple-element.14.after_ref.own_west), custom_call_target="tpu_custom_call" | custom-call | tf_op jit(solution)/shard_map/pallas_call | solution.py:453
  64.8 0.0 collective-permute-done.west_ref
  64.9 0.0 collective-permute-done.1.east_ref
  64.9 0.1 collective-permute-start.3
  65.0 0.0 copy-start.2
  65.0 2.0 %collective-permute-start.2 = (bf16[2,96,256]{2,1,0:T(8,128)(2,1)S(1)}, bf16[2,96,256]{2,1,0:T(8,128)(2,1)S(1)}, u32[]{:S(2)}, u32[]{:S(2)}) collective-permute-start(bf16[2,96,256]{2,1,0:T(8,128)(2,1)S(1)} %get-tuple-element.18.after_ref), channel_id=1, source_target_pairs={{0,8},{8,0},{16,24},{24,16},{1,9},{9,1},{17,25},{25,17},{2,10},{10... | collective-permute-start | bytes 294920 | tf_op jit(solution)/shard_map/ppermute | solution.py:643
  67.0 11.0 %shard_map.114.lower_in = bf16[5952,768]{1,0:T(8,128)(2,1)S(1)} custom-call(bf16[90,96,256]{2,1,0:T(8,128)(2,1)S(1)} %get-tuple-element.13.first_ref, bf16[3,768,256]{2,1,0:T(8,128)(2,1)S(1)} %bitcast.9, bf16[2,96,256]{2,1,0:T(8,128)(2,1)S(1)} %collective-permute-done.west_ref, bf16[2,96,256]{2,1,0:T(8,128)(2,1)S(1)} %collective-permute-done.1.east_ref, ...), custom_call_target="tpu_custom_call" | custom-call | tf_op jit(solution)/shard_map/pallas_call | solution.py:467
  78.0 0.0 collective-permute-done.3.outer_ref
  78.0 0.0 collective-permute-done.2.inner_ref
  78.0 0.0 copy-done.2
  78.0 13.9 %shard_map.115 = (bf16[90,90,256]{2,1,0:T(8,128)(2,1)}, bf16[3072,768]{1,0:T(8,128)(2,1)S(1)}, bf16[5952,768]{1,0:T(8,128)(2,1)S(1)}) custom-call(bf16[3072,768]{1,0:T(8,128)(2,1)S(1)} %shard_map.112.after_ref.upper_in, bf16[5952,768]{1,0:T(8,128)(2,1)S(1)} %shard_map.114.lower_in, ...), custom_call_target="tpu_custom_call", output_to_operand_aliasing={{1}: (0, {}), {2}: (1, {})} | custom-call | tf_op jit(solution)/shard_map/pallas_call | solution.py:568
  (5 shorter events, 0.0 us)
Async XLA Ops:
  7.8 36.3 %all-to-all-start = ((bf16[32,136,128]{2,1,0:T(8,128)(2,1)}), bf16[32,136,128]{2,1,0:T(8,128)(2,1)S(1)}, u32[]{:S(2)}, u32[]{:S(2)}) async-start(bf16[32,136,128]{2,1,0:T(8,128)(2,1)} %bitcast.14), calls=%async_computation | async-start | bytes 2228224 | tf_op jit(solution)/shard_map/all_to_all | solution.py:630
  15.1 2.3 %copy-start.1 = (bf16[90,90,256]{2,1,0:T(8,128)(2,1)S(1)}, bf16[90,90,256]{2,1,0:T(8,128)(2,1)}, u32[]{:S(2)}) copy-start(bf16[90,90,256]{2,1,0:T(8,128)(2,1)} %back_ref.1) | copy-start | bytes 12441604
  17.3 0.9 copy-start.3
  18.2 25.8 %copy-start.4 = (bf16[128,256]{1,0:T(8,128)(2,1)S(1)}, bf16[128,256]{1,0:T(8,128)(2,1)}, u32[]{:S(2)}) copy-start(bf16[128,256]{1,0:T(8,128)(2,1)} %w_in_hbm.1) | copy-start | bytes 196612
  18.2 25.8 %copy-start.5 = (f32[256]{0:T(256)S(1)}, f32[256]{0:T(256)}, u32[]{:S(2)}) copy-start(f32[256]{0:T(256)} %param.19) | copy-start | bytes 3076
  44.1 15.5 %copy-start = (bf16[3,3,256,256]{3,2,1,0:T(8,128)(2,1)S(1)}, bf16[3,3,256,256]{3,2,1,0:T(8,128)(2,1)}, u32[]{:S(2)}) copy-start(bf16[3,3,256,256]{3,2,1,0:T(8,128)(2,1)} %param.20) | copy-start | bytes 3538948
  56.0 8.9 %collective-permute-start = (bf16[2,96,256]{2,1,0:T(8,128)(2,1)S(1)}, bf16[2,96,256]{2,1,0:T(8,128)(2,1)S(1)}, u32[]{:S(2)}, u32[]{:S(2)}) collective-permute-start(bf16[2,96,256]{2,1,0:T(8,128)(2,1)S(1)} %get-tuple-element.15.own_east), channel_id=1, source_target_pairs={{0,1},{1,2},{2,3},{3,4},{4,5},{5,6},{6,7},{7,0},{8,9},{9,10},{10,1... | collective-permute-start | bytes 294920 | tf_op jit(solution)/shard_map/ppermute | solution.py:635
  56.0 8.8 %collective-permute-start.1 = (bf16[2,96,256]{2,1,0:T(8,128)(2,1)S(1)}, bf16[2,96,256]{2,1,0:T(8,128)(2,1)S(1)}, u32[]{:S(2)}, u32[]{:S(2)}) collective-permute-start(bf16[2,96,256]{2,1,0:T(8,128)(2,1)S(1)} %get-tuple-element.14.after_ref.own_west), channel_id=1, source_target_pairs={{1,0},{2,1},{3,2},{4,3},{5,4},{6,5},{7,6},{0,7},{9,8},{10,9},{11,1... | collective-permute-start | bytes 294920 | tf_op jit(solution)/shard_map/ppermute | solution.py:636
  64.9 13.0 %collective-permute-start.3 = (bf16[2,96,256]{2,1,0:T(8,128)(2,1)S(1)}, bf16[2,96,256]{2,1,0:T(8,128)(2,1)S(1)}, u32[]{:S(2)}, u32[]{:S(2)}) collective-permute-start(bf16[2,96,256]{2,1,0:T(8,128)(2,1)S(1)} %get-tuple-element.19), channel_id=1, source_target_pairs={{8,16},{16,8},{0,4},{24,28},{9,17},{17,9},{1,5},{25,29},{10,18},{1... | collective-permute-start | bytes 294920 | tf_op jit(solution)/shard_map/ppermute | solution.py:644
  65.0 13.0 %copy-start.2 = (bf16[3,3,256,256]{3,2,1,0:T(8,128)(2,1)S(1)}, bf16[3,3,256,256]{3,2,1,0:T(8,128)(2,1)}, u32[]{:S(2)}) copy-start(bf16[3,3,256,256]{3,2,1,0:T(8,128)(2,1)} %param.21) | copy-start | bytes 3538948
  65.0 13.0 %collective-permute-start.2 = (bf16[2,96,256]{2,1,0:T(8,128)(2,1)S(1)}, bf16[2,96,256]{2,1,0:T(8,128)(2,1)S(1)}, u32[]{:S(2)}, u32[]{:S(2)}) collective-permute-start(bf16[2,96,256]{2,1,0:T(8,128)(2,1)S(1)} %get-tuple-element.18.after_ref), channel_id=1, source_target_pairs={{0,8},{8,0},{16,24},{24,16},{1,9},{9,1},{17,25},{25,17},{2,10},{10... | collective-permute-start | bytes 294920 | tf_op jit(solution)/shard_map/ppermute | solution.py:643

commit v9 on v8

--- a/solution.py
+++ b/solution.py
@@ -61,10 +61,12 @@
     counts = dot(hot_ref[...], jnp.ones((nrows, nfeat), BF))
     ka = lax.broadcasted_iota(jnp.int32, (kinds, kinds), 0)
     kb = lax.broadcasted_iota(jnp.int32, (kinds, kinds), 1)
-    da, db = ka // classes, kb // classes
+    da = lax.broadcasted_iota(jnp.int32, (kinds, 1), 0) // classes
+    row = lax.broadcasted_iota(jnp.int32, (1, kinds), 1)
+    db = row // classes
     within = ((da == db) & (kb < ka)).astype(F32).astype(BF)
     together = (da == db).astype(F32).astype(BF)
-    ahead = ((db < da) & (kb % classes == 0)).astype(F32).astype(BF)
+    ahead = ((db < da) & (row == db * classes)).astype(F32).astype(BF)
     loads = dot(together, counts.astype(BF))
     padded = jnp.floor((loads + 7.0) * 0.125) * 8.0
     begins = dot(ahead, padded.astype(BF))
@@ -243,18 +245,19 @@
     def compact(s, out):
         out = pl.multiple_of(out, 8)
         low, high = ends_smem[s, 2 * band], ends_smem[s, 2 * band + 1]
-        source = pl.multiple_of(low // 8 * 8, 8)
+        source = pl.multiple_of(low & -8, 8)
         feat_ref[pl.ds(out, cap), :] = rows_ref[pl.ds(pl.multiple_of(s * cap + source, 8), cap), :]
         side = sides_ref[s]
         side = jnp.where((lane >= low) & (lane < high), side, 0.0)
         shift = out - source + nfeat
-        tile, shift = shift // nfeat, shift % nfeat
+        tile, shift = shift >> (nfeat.bit_length() - 1), shift & (nfeat - 1)
         moved = pltpu.roll(side, shift, axis=1)
-        meta_ref[tile] += jnp.where(lane >= shift, moved, 0.0)
-        meta_ref[tile + 1] += jnp.where(lane < shift, moved, 0.0)
-        return out + (high - source + 7) // 8 * 8
-
-    total = lax.fori_loop(0, devices, compact, 0, unroll=16)
+        near, far = meta_ref[tile], meta_ref[tile + 1]
+        meta_ref[tile] = near + jnp.where(lane >= shift, moved, 0.0)
+        meta_ref[tile + 1] = far + jnp.where(lane < shift, moved, 0.0)
+        return out + ((high - source + 7) & -8)
+
+    total = lax.fori_loop(0, devices, compact, 0, unroll=32)
 
     def piece(begin, size):
         begin = pl.multiple_of(begin, CHUNK)

time: 92.2 us -> 90.2 us (0.978)
  Pallas kernels: 54.1 us -> 52.5 us
    pallas_call x1, Pallas kernels: 11.9 us -> 10.3 us  [gridded(): pl.pallas_call(functools.partial(grid_kernel, devices, cap, wide, cols, l...]
  transfers between devices with their start and end apart: 5 -> 5, of which waited for: 1 -> 1; matrix products, arithmetic and copies ran while one was open for 0% -> 0% of each run, Pallas kernels for 23% -> 24%
where the time goes in v9:
time: 90.2 us; the launch traced here: 89.9 us
  Pallas kernels  52.5 us (58%)
  waiting for transfers between devices  20.9 us (23%)
  starting transfers between devices  12.6 us (14%)
  local copies, waits for them, and re-layouts  3.17 us (4%)
    all_to_all x1, waiting for transfers between devices, shards(): lax.all_to_all(send, axes, split_axis=0, concat_axis=0, tiled=True)  20.9 us
    pallas_call x1, Pallas kernels, finished(): pl.pallas_call(functools.partial(finish_kernel, lat_count), grid=(lat_row...  13.9 us
    pallas_call x1, Pallas kernels, lower_part(): pl.pallas_call(functools.partial(lower_kernel, cols), out_shape=jax.Shape...  11 us
    pallas_call x1, Pallas kernels, gridded(): pl.pallas_call(functools.partial(grid_kernel, devices, cap, wide, cols, l...  10.3 us
    all_to_all x1, starting transfers between devices, shards(): lax.all_to_all(send, axes, split_axis=0, concat_axis=0, tiled=True)  7.31 us
    pallas_call x1, Pallas kernels, pack(): pl.pallas_call(functools.partial(pack_kernel, devices, lon_count, cap, co...  7.09 us
    pallas_call x1, Pallas kernels, upper_part(): pl.pallas_call(upper_kernel, out_shape=jax.ShapeDtypeStruct(shape, BF), i...  5.27 us
    pallas_call x1, Pallas kernels, projected(): pl.pallas_call(functools.partial(back_kernel, wide), grid=(lat_rows // BA...  4.97 us
  transfers between devices with their start and end apart: 5, of which 1 were waited for; matrix products, arithmetic and copies ran while one was open for 0% of the time, Pallas kernels for 24%

profile of v9, /device:TPU:0, one launch (start us, length us, event | category | flops | bytes accessed | tf_op | source)
XLA Modules:
  0.0 89.9 jit_solution(18037384964530882756)
XLA Ops:
  0.7 7.1 %shard_map.109 = bf16[16,272,128]{2,1,0:T(8,128)(2,1)} custom-call(s32[1]{0:T(128)S(6)} %copy.16.count_ref, s32[1,2048]{1,0:T(1,128)} %bitcast.17, s32[4,2048]{1,0:T(4,128)} %bitcast.15, s32[4,2048]{1,0:T(4,128)} %bitcast.16, bf16[2048,128]{1,0:T(8,128)(2,1)} %feat_hbm.1), custom_call_target="tpu_custom_call" | custom-call | tf_op jit(solution)/shard_map/pallas_call | solution.py:137
  7.8 7.3 %all-to-all-start = ((bf16[32,136,128]{2,1,0:T(8,128)(2,1)}), bf16[32,136,128]{2,1,0:T(8,128)(2,1)S(1)}, u32[]{:S(2)}, u32[]{:S(2)}) async-start(bf16[32,136,128]{2,1,0:T(8,128)(2,1)} %bitcast.14), calls=%async_computation | async-start | bytes 2228224 | tf_op jit(solution)/shard_map/all_to_all | solution.py:633
  15.1 0.0 copy-start.1
  15.1 2.2 %copy-done.1 = bf16[90,90,256]{2,1,0:T(8,128)(2,1)S(1)} copy-done((bf16[90,90,256]{2,1,0:T(8,128)(2,1)S(1)}, bf16[90,90,256]{2,1,0:T(8,128)(2,1)}, u32[]{:S(2)}) %copy-start.1) | copy-done | bytes 4147224
  17.3 0.9 %copy-done.3 = bf16[256,256]{1,0:T(8,128)(2,1)S(1)} copy-done((bf16[256,256]{1,0:T(8,128)(2,1)S(1)}, bf16[256,256]{1,0:T(8,128)(2,1)}, u32[]{:S(2)}) %copy-start.3) | copy-done | bytes 131096
  18.2 5.0 %shard_map.110.back_hbm = f32[65552,256]{1,0:T(8,128)} custom-call(bf16[90,90,256]{2,1,0:T(8,128)(2,1)S(1)} %copy-done.1, bf16[256,256]{1,0:T(8,128)(2,1)S(1)} %copy-done.3), custom_call_target="tpu_custom_call" | custom-call | tf_op jit(solution)/shard_map/pallas_call | solution.py:168
  23.2 20.9 %all-to-all-done = bf16[32,136,128]{2,1,0:T(8,128)(2,1)S(1)} async-done(((bf16[32,136,128]{2,1,0:T(8,128)(2,1)}), bf16[32,136,128]{2,1,0:T(8,128)(2,1)S(1)}, u32[]{:S(2)}, u32[]{:S(2)}) %all-to-all-start) | async-done | bytes 1114144 | tf_op jit(solution)/shard_map/all_to_all | solution.py:633
  44.1 0.0 copy-done.4
  44.1 0.0 copy-done.5
  44.1 10.3 %shard_map.111 = (bf16[90,96,256]{2,1,0:T(8,128)(2,1)S(1)}, bf16[2,96,256]{2,1,0:T(8,128)(2,1)S(1)}, bf16[2,96,256]{2,1,0:T(8,128)(2,1)S(1)}, bf16[2,96,256]{2,1,0:T(8,128)(2,1)S(1)}, bf16[2,96,256]{2,1,0:T(8,128)(2,1)S(1)}) custom-call(bf16[16,272,128]{2,1,0:T(8,128)(2,1)S(1)} %bitcast.11, f32[65552,256]{1,0:T(8,128)} %shard_map.110.back_hbm, ...), custom_call_target="tpu_custom_call" | custom-call | tf_op jit(solution)/shard_map/pallas_call | solution.py:327
  54.4 0.1 collective-permute-start
  54.5 3.5 %collective-permute-start.1 = (bf16[2,96,256]{2,1,0:T(8,128)(2,1)S(1)}, bf16[2,96,256]{2,1,0:T(8,128)(2,1)S(1)}, u32[]{:S(2)}, u32[]{:S(2)}) collective-permute-start(bf16[2,96,256]{2,1,0:T(8,128)(2,1)S(1)} %get-tuple-element.14.after_ref.own_west), channel_id=1, source_target_pairs={{1,0},{2,1},{3,2},{4,3},{5,4},{6,5},{7,6},{0,7},{9,8},{10,9},{11,1... | collective-permute-start | bytes 294920 | tf_op jit(solution)/shard_map/ppermute | solution.py:639
  58.0 0.0 copy-done
  58.0 5.3 %shard_map.112.after_ref.upper_in = bf16[3072,768]{1,0:T(8,128)(2,1)S(1)} custom-call(bf16[90,96,256]{2,1,0:T(8,128)(2,1)S(1)} %get-tuple-element.13.first_ref, bf16[3,768,256]{2,1,0:T(8,128)(2,1)S(1)} %bitcast.8, bf16[2,96,256]{2,1,0:T(8,128)(2,1)S(1)} %get-tuple-element.14.after_ref.own_west), custom_call_target="tpu_custom_call" | custom-call | tf_op jit(solution)/shard_map/pallas_call | solution.py:456
  63.3 0.0 collective-permute-done.west_ref
  63.3 0.0 collective-permute-done.1.east_ref
  63.3 0.1 collective-permute-start.3
  63.4 0.0 copy-start.2
  63.4 1.6 %collective-permute-start.2 = (bf16[2,96,256]{2,1,0:T(8,128)(2,1)S(1)}, bf16[2,96,256]{2,1,0:T(8,128)(2,1)S(1)}, u32[]{:S(2)}, u32[]{:S(2)}) collective-permute-start(bf16[2,96,256]{2,1,0:T(8,128)(2,1)S(1)} %get-tuple-element.18.after_ref), channel_id=1, source_target_pairs={{0,8},{8,0},{16,24},{24,16},{1,9},{9,1},{17,25},{25,17},{2,10},{10... | collective-permute-start | bytes 294920 | tf_op jit(solution)/shard_map/ppermute | solution.py:646
  65.0 11.0 %shard_map.114.lower_in = bf16[5952,768]{1,0:T(8,128)(2,1)S(1)} custom-call(bf16[90,96,256]{2,1,0:T(8,128)(2,1)S(1)} %get-tuple-element.13.first_ref, bf16[3,768,256]{2,1,0:T(8,128)(2,1)S(1)} %bitcast.9, bf16[2,96,256]{2,1,0:T(8,128)(2,1)S(1)} %collective-permute-done.west_ref, bf16[2,96,256]{2,1,0:T(8,128)(2,1)S(1)} %collective-permute-done.1.east_ref, ...), custom_call_target="tpu_custom_call" | custom-call | tf_op jit(solution)/shard_map/pallas_call | solution.py:470
  76.0 0.0 collective-permute-done.3.outer_ref
  76.0 0.0 collective-permute-done.2.inner_ref
  76.0 0.0 copy-done.2
  76.0 13.9 %shard_map.115 = (bf16[90,90,256]{2,1,0:T(8,128)(2,1)}, bf16[3072,768]{1,0:T(8,128)(2,1)S(1)}, bf16[5952,768]{1,0:T(8,128)(2,1)S(1)}) custom-call(bf16[3072,768]{1,0:T(8,128)(2,1)S(1)} %shard_map.112.after_ref.upper_in, bf16[5952,768]{1,0:T(8,128)(2,1)S(1)} %shard_map.114.lower_in, ...), custom_call_target="tpu_custom_call", output_to_operand_aliasing={{1}: (0, {}), {2}: (1, {})} | custom-call | tf_op jit(solution)/shard_map/pallas_call | solution.py:571
  (5 shorter events, 0.0 us)
Async XLA Ops:
  7.8 36.3 %all-to-all-start = ((bf16[32,136,128]{2,1,0:T(8,128)(2,1)}), bf16[32,136,128]{2,1,0:T(8,128)(2,1)S(1)}, u32[]{:S(2)}, u32[]{:S(2)}) async-start(bf16[32,136,128]{2,1,0:T(8,128)(2,1)} %bitcast.14), calls=%async_computation | async-start | bytes 2228224 | tf_op jit(solution)/shard_map/all_to_all | solution.py:633
  15.1 2.3 %copy-start.1 = (bf16[90,90,256]{2,1,0:T(8,128)(2,1)S(1)}, bf16[90,90,256]{2,1,0:T(8,128)(2,1)}, u32[]{:S(2)}) copy-start(bf16[90,90,256]{2,1,0:T(8,128)(2,1)} %back_ref.1) | copy-start | bytes 12441604
  17.3 0.9 %copy-start.3 = (bf16[256,256]{1,0:T(8,128)(2,1)S(1)}, bf16[256,256]{1,0:T(8,128)(2,1)}, u32[]{:S(2)}) copy-start(bf16[256,256]{1,0:T(8,128)(2,1)} %w_bg_ref.1) | copy-start | bytes 393220
  18.2 25.8 %copy-start.4 = (bf16[128,256]{1,0:T(8,128)(2,1)S(1)}, bf16[128,256]{1,0:T(8,128)(2,1)}, u32[]{:S(2)}) copy-start(bf16[128,256]{1,0:T(8,128)(2,1)} %w_in_hbm.1) | copy-start | bytes 196612
  18.2 25.8 %copy-start.5 = (f32[256]{0:T(256)S(1)}, f32[256]{0:T(256)}, u32[]{:S(2)}) copy-start(f32[256]{0:T(256)} %param.19) | copy-start | bytes 3076
  44.1 13.9 %copy-start = (bf16[3,3,256,256]{3,2,1,0:T(8,128)(2,1)S(1)}, bf16[3,3,256,256]{3,2,1,0:T(8,128)(2,1)}, u32[]{:S(2)}) copy-start(bf16[3,3,256,256]{3,2,1,0:T(8,128)(2,1)} %param.20) | copy-start | bytes 3538948
  54.4 8.9 %collective-permute-start = (bf16[2,96,256]{2,1,0:T(8,128)(2,1)S(1)}, bf16[2,96,256]{2,1,0:T(8,128)(2,1)S(1)}, u32[]{:S(2)}, u32[]{:S(2)}) collective-permute-start(bf16[2,96,256]{2,1,0:T(8,128)(2,1)S(1)} %get-tuple-element.15.own_east), channel_id=1, source_target_pairs={{0,1},{1,2},{2,3},{3,4},{4,5},{5,6},{6,7},{7,0},{8,9},{9,10},{10,1... | collective-permute-start | bytes 294920 | tf_op jit(solution)/shard_map/ppermute | solution.py:638
  54.5 8.8 %collective-permute-start.1 = (bf16[2,96,256]{2,1,0:T(8,128)(2,1)S(1)}, bf16[2,96,256]{2,1,0:T(8,128)(2,1)S(1)}, u32[]{:S(2)}, u32[]{:S(2)}) collective-permute-start(bf16[2,96,256]{2,1,0:T(8,128)(2,1)S(1)} %get-tuple-element.14.after_ref.own_west), channel_id=1, source_target_pairs={{1,0},{2,1},{3,2},{4,3},{5,4},{6,5},{7,6},{0,7},{9,8},{10,9},{11,1... | collective-permute-start | bytes 294920 | tf_op jit(solution)/shard_map/ppermute | solution.py:639
  63.3 12.7 %collective-permute-start.3 = (bf16[2,96,256]{2,1,0:T(8,128)(2,1)S(1)}, bf16[2,96,256]{2,1,0:T(8,128)(2,1)S(1)}, u32[]{:S(2)}, u32[]{:S(2)}) collective-permute-start(bf16[2,96,256]{2,1,0:T(8,128)(2,1)S(1)} %get-tuple-element.19), channel_id=1, source_target_pairs={{8,16},{16,8},{0,4},{24,28},{9,17},{17,9},{1,5},{25,29},{10,18},{1... | collective-permute-start | bytes 294920 | tf_op jit(solution)/shard_map/ppermute | solution.py:647
  63.4 12.6 %copy-start.2 = (bf16[3,3,256,256]{3,2,1,0:T(8,128)(2,1)S(1)}, bf16[3,3,256,256]{3,2,1,0:T(8,128)(2,1)}, u32[]{:S(2)}) copy-start(bf16[3,3,256,256]{3,2,1,0:T(8,128)(2,1)} %param.21) | copy-start | bytes 3538948
  63.4 12.6 %collective-permute-start.2 = (bf16[2,96,256]{2,1,0:T(8,128)(2,1)S(1)}, bf16[2,96,256]{2,1,0:T(8,128)(2,1)S(1)}, u32[]{:S(2)}, u32[]{:S(2)}) collective-permute-start(bf16[2,96,256]{2,1,0:T(8,128)(2,1)S(1)} %get-tuple-element.18.after_ref), channel_id=1, source_target_pairs={{0,8},{8,0},{16,24},{24,16},{1,9},{9,1},{17,25},{25,17},{2,10},{10... | collective-permute-start | bytes 294920 | tf_op jit(solution)/shard_map/ppermute | solution.py:646

commit v10 on v9

--- a/solution.py
+++ b/solution.py
@@ -358,9 +358,10 @@
 
 def put(ref, begin, value):
     size, chans = value.shape
-    for b in range(3):
-        part = value if b == 0 else pltpu.roll(value, size - b, axis=0)
-        ref[pl.ds(begin, size), b * chans : (b + 1) * chans] = part.astype(BF)
+    plain = value.astype(BF)
+    parts = plain, pltpu.roll(value, size - 1, axis=0).astype(BF), pltpu.roll(plain, size - 2, axis=0)
+    for b, part in enumerate(parts):
+        ref[pl.ds(begin, size), b * chans : (b + 1) * chans] = part
 
 
 def taps(ref, begin, size, wide, w_ref):

time: 90.2 us -> 89.9 us (level)
  transfers between devices with their start and end apart: 5 -> 5, of which waited for: 1 -> 1; matrix products, arithmetic and copies ran while one was open for 0% -> 0% of each run, Pallas kernels for 24% -> 23%
where the time goes in v10:
time: 89.9 us; the launch traced here: 89.6 us
  Pallas kernels  51.8 us (58%)
  waiting for transfers between devices  20.9 us (23%)
  starting transfers between devices  13 us (14%)
  local copies, waits for them, and re-layouts  3.17 us (4%)
    all_to_all x1, waiting for transfers between devices, shards(): lax.all_to_all(send, axes, split_axis=0, concat_axis=0, tiled=True)  20.9 us
    pallas_call x1, Pallas kernels, finished(): pl.pallas_call(functools.partial(finish_kernel, lat_count), grid=(lat_row...  13.9 us
    pallas_call x1, Pallas kernels, lower_part(): pl.pallas_call(functools.partial(lower_kernel, cols), out_shape=jax.Shape...  10.7 us
    pallas_call x1, Pallas kernels, gridded(): pl.pallas_call(functools.partial(grid_kernel, devices, cap, wide, cols, l...  9.93 us
    all_to_all x1, starting transfers between devices, shards(): lax.all_to_all(send, axes, split_axis=0, concat_axis=0, tiled=True)  7.32 us
    pallas_call x1, Pallas kernels, pack(): pl.pallas_call(functools.partial(pack_kernel, devices, lon_count, cap, co...  7.09 us
    pallas_call x1, Pallas kernels, upper_part(): pl.pallas_call(upper_kernel, out_shape=jax.ShapeDtypeStruct(shape, BF), i...  5.16 us
    pallas_call x1, Pallas kernels, projected(): pl.pallas_call(functools.partial(back_kernel, wide), grid=(lat_rows // BA...  4.97 us
  transfers between devices with their start and end apart: 5, of which 1 were waited for; matrix products, arithmetic and copies ran while one was open for 0% of the time, Pallas kernels for 23%

profile of v10, /device:TPU:0, one launch (start us, length us, event | category | flops | bytes accessed | tf_op | source)
XLA Modules:
  0.0 89.6 jit_solution(1509731759489713743)
XLA Ops:
  0.7 7.1 %shard_map.109 = bf16[16,272,128]{2,1,0:T(8,128)(2,1)} custom-call(s32[1]{0:T(128)S(6)} %copy.16.count_ref, s32[1,2048]{1,0:T(1,128)} %bitcast.17, s32[4,2048]{1,0:T(4,128)} %bitcast.15, s32[4,2048]{1,0:T(4,128)} %bitcast.16, bf16[2048,128]{1,0:T(8,128)(2,1)} %feat_hbm.1), custom_call_target="tpu_custom_call" | custom-call | tf_op jit(solution)/shard_map/pallas_call | solution.py:137
  7.8 7.3 %all-to-all-start = ((bf16[32,136,128]{2,1,0:T(8,128)(2,1)}), bf16[32,136,128]{2,1,0:T(8,128)(2,1)S(1)}, u32[]{:S(2)}, u32[]{:S(2)}) async-start(bf16[32,136,128]{2,1,0:T(8,128)(2,1)} %bitcast.14), calls=%async_computation | async-start | bytes 2228224 | tf_op jit(solution)/shard_map/all_to_all | solution.py:634
  15.1 0.0 copy-start.1
  15.1 2.2 %copy-done.1 = bf16[90,90,256]{2,1,0:T(8,128)(2,1)S(1)} copy-done((bf16[90,90,256]{2,1,0:T(8,128)(2,1)S(1)}, bf16[90,90,256]{2,1,0:T(8,128)(2,1)}, u32[]{:S(2)}) %copy-start.1) | copy-done | bytes 4147224
  17.3 0.9 %copy-done.3 = bf16[256,256]{1,0:T(8,128)(2,1)S(1)} copy-done((bf16[256,256]{1,0:T(8,128)(2,1)S(1)}, bf16[256,256]{1,0:T(8,128)(2,1)}, u32[]{:S(2)}) %copy-start.3) | copy-done | bytes 131096
  18.2 5.0 %shard_map.110.back_hbm = f32[65552,256]{1,0:T(8,128)} custom-call(bf16[90,90,256]{2,1,0:T(8,128)(2,1)S(1)} %copy-done.1, bf16[256,256]{1,0:T(8,128)(2,1)S(1)} %copy-done.3), custom_call_target="tpu_custom_call" | custom-call | tf_op jit(solution)/shard_map/pallas_call | solution.py:168
  23.2 20.9 %all-to-all-done = bf16[32,136,128]{2,1,0:T(8,128)(2,1)S(1)} async-done(((bf16[32,136,128]{2,1,0:T(8,128)(2,1)}), bf16[32,136,128]{2,1,0:T(8,128)(2,1)S(1)}, u32[]{:S(2)}, u32[]{:S(2)}) %all-to-all-start) | async-done | bytes 1114144 | tf_op jit(solution)/shard_map/all_to_all | solution.py:634
  44.1 0.0 copy-done.4
  44.1 0.0 copy-done.5
  44.1 9.9 %shard_map.111 = (bf16[90,96,256]{2,1,0:T(8,128)(2,1)S(1)}, bf16[2,96,256]{2,1,0:T(8,128)(2,1)S(1)}, bf16[2,96,256]{2,1,0:T(8,128)(2,1)S(1)}, bf16[2,96,256]{2,1,0:T(8,128)(2,1)S(1)}, bf16[2,96,256]{2,1,0:T(8,128)(2,1)S(1)}) custom-call(bf16[16,272,128]{2,1,0:T(8,128)(2,1)S(1)} %bitcast.11, f32[65552,256]{1,0:T(8,128)} %shard_map.110.back_hbm, ...), custom_call_target="tpu_custom_call" | custom-call | tf_op jit(solution)/shard_map/pallas_call | solution.py:327
  54.0 0.1 collective-permute-start
  54.1 3.5 %collective-permute-start.1 = (bf16[2,96,256]{2,1,0:T(8,128)(2,1)S(1)}, bf16[2,96,256]{2,1,0:T(8,128)(2,1)S(1)}, u32[]{:S(2)}, u32[]{:S(2)}) collective-permute-start(bf16[2,96,256]{2,1,0:T(8,128)(2,1)S(1)} %get-tuple-element.14.after_ref.own_west), channel_id=1, source_target_pairs={{1,0},{2,1},{3,2},{4,3},{5,4},{6,5},{7,6},{0,7},{9,8},{10,9},{11,1... | collective-permute-start | bytes 294920 | tf_op jit(solution)/shard_map/ppermute | solution.py:640
  57.6 0.0 copy-done
  57.6 5.2 %shard_map.112.after_ref.upper_in = bf16[3072,768]{1,0:T(8,128)(2,1)S(1)} custom-call(bf16[90,96,256]{2,1,0:T(8,128)(2,1)S(1)} %get-tuple-element.13.first_ref, bf16[3,768,256]{2,1,0:T(8,128)(2,1)S(1)} %bitcast.8, bf16[2,96,256]{2,1,0:T(8,128)(2,1)S(1)} %get-tuple-element.14.after_ref.own_west), custom_call_target="tpu_custom_call" | custom-call | tf_op jit(solution)/shard_map/pallas_call | solution.py:457
  62.8 0.0 collective-permute-done.west_ref
  62.8 0.0 collective-permute-done.1.east_ref
  62.9 0.1 collective-permute-start.3
  62.9 0.0 copy-start.2
  62.9 2.0 %collective-permute-start.2 = (bf16[2,96,256]{2,1,0:T(8,128)(2,1)S(1)}, bf16[2,96,256]{2,1,0:T(8,128)(2,1)S(1)}, u32[]{:S(2)}, u32[]{:S(2)}) collective-permute-start(bf16[2,96,256]{2,1,0:T(8,128)(2,1)S(1)} %get-tuple-element.18.after_ref), channel_id=1, source_target_pairs={{0,8},{8,0},{16,24},{24,16},{1,9},{9,1},{17,25},{25,17},{2,10},{10... | collective-permute-start | bytes 294920 | tf_op jit(solution)/shard_map/ppermute | solution.py:647
  64.9 10.7 %shard_map.114.lower_in = bf16[5952,768]{1,0:T(8,128)(2,1)S(1)} custom-call(bf16[90,96,256]{2,1,0:T(8,128)(2,1)S(1)} %get-tuple-element.13.first_ref, bf16[3,768,256]{2,1,0:T(8,128)(2,1)S(1)} %bitcast.9, bf16[2,96,256]{2,1,0:T(8,128)(2,1)S(1)} %collective-permute-done.west_ref, bf16[2,96,256]{2,1,0:T(8,128)(2,1)S(1)} %collective-permute-done.1.east_ref, ...), custom_call_target="tpu_custom_call" | custom-call | tf_op jit(solution)/shard_map/pallas_call | solution.py:471
  75.7 0.0 collective-permute-done.3.outer_ref
  75.7 0.0 collective-permute-done.2.inner_ref
  75.7 0.0 copy-done.2
  75.7 13.9 %shard_map.115 = (bf16[90,90,256]{2,1,0:T(8,128)(2,1)}, bf16[3072,768]{1,0:T(8,128)(2,1)S(1)}, bf16[5952,768]{1,0:T(8,128)(2,1)S(1)}) custom-call(bf16[3072,768]{1,0:T(8,128)(2,1)S(1)} %shard_map.112.after_ref.upper_in, bf16[5952,768]{1,0:T(8,128)(2,1)S(1)} %shard_map.114.lower_in, ...), custom_call_target="tpu_custom_call", output_to_operand_aliasing={{1}: (0, {}), {2}: (1, {})} | custom-call | tf_op jit(solution)/shard_map/pallas_call | solution.py:572
  (5 shorter events, 0.0 us)
Async XLA Ops:
  7.8 36.3 %all-to-all-start = ((bf16[32,136,128]{2,1,0:T(8,128)(2,1)}), bf16[32,136,128]{2,1,0:T(8,128)(2,1)S(1)}, u32[]{:S(2)}, u32[]{:S(2)}) async-start(bf16[32,136,128]{2,1,0:T(8,128)(2,1)} %bitcast.14), calls=%async_computation | async-start | bytes 2228224 | tf_op jit(solution)/shard_map/all_to_all | solution.py:634
  15.1 2.3 %copy-start.1 = (bf16[90,90,256]{2,1,0:T(8,128)(2,1)S(1)}, bf16[90,90,256]{2,1,0:T(8,128)(2,1)}, u32[]{:S(2)}) copy-start(bf16[90,90,256]{2,1,0:T(8,128)(2,1)} %back_ref.1) | copy-start | bytes 12441604
  17.3 0.9 %copy-start.3 = (bf16[256,256]{1,0:T(8,128)(2,1)S(1)}, bf16[256,256]{1,0:T(8,128)(2,1)}, u32[]{:S(2)}) copy-start(bf16[256,256]{1,0:T(8,128)(2,1)} %w_bg_ref.1) | copy-start | bytes 393220
  18.2 25.8 %copy-start.4 = (bf16[128,256]{1,0:T(8,128)(2,1)S(1)}, bf16[128,256]{1,0:T(8,128)(2,1)}, u32[]{:S(2)}) copy-start(bf16[128,256]{1,0:T(8,128)(2,1)} %w_in_hbm.1) | copy-start | bytes 196612
  18.2 25.8 %copy-start.5 = (f32[256]{0:T(256)S(1)}, f32[256]{0:T(256)}, u32[]{:S(2)}) copy-start(f32[256]{0:T(256)} %param.19) | copy-start | bytes 3076
  44.1 13.5 %copy-start = (bf16[3,3,256,256]{3,2,1,0:T(8,128)(2,1)S(1)}, bf16[3,3,256,256]{3,2,1,0:T(8,128)(2,1)}, u32[]{:S(2)}) copy-start(bf16[3,3,256,256]{3,2,1,0:T(8,128)(2,1)} %param.20) | copy-start | bytes 3538948
  54.0 8.8 %collective-permute-start = (bf16[2,96,256]{2,1,0:T(8,128)(2,1)S(1)}, bf16[2,96,256]{2,1,0:T(8,128)(2,1)S(1)}, u32[]{:S(2)}, u32[]{:S(2)}) collective-permute-start(bf16[2,96,256]{2,1,0:T(8,128)(2,1)S(1)} %get-tuple-element.15.own_east), channel_id=1, source_target_pairs={{0,1},{1,2},{2,3},{3,4},{4,5},{5,6},{6,7},{7,0},{8,9},{9,10},{10,1... | collective-permute-start | bytes 294920 | tf_op jit(solution)/shard_map/ppermute | solution.py:639
  54.1 8.7 %collective-permute-start.1 = (bf16[2,96,256]{2,1,0:T(8,128)(2,1)S(1)}, bf16[2,96,256]{2,1,0:T(8,128)(2,1)S(1)}, u32[]{:S(2)}, u32[]{:S(2)}) collective-permute-start(bf16[2,96,256]{2,1,0:T(8,128)(2,1)S(1)} %get-tuple-element.14.after_ref.own_west), channel_id=1, source_target_pairs={{1,0},{2,1},{3,2},{4,3},{5,4},{6,5},{7,6},{0,7},{9,8},{10,9},{11,1... | collective-permute-start | bytes 294920 | tf_op jit(solution)/shard_map/ppermute | solution.py:640
  62.9 12.8 %collective-permute-start.3 = (bf16[2,96,256]{2,1,0:T(8,128)(2,1)S(1)}, bf16[2,96,256]{2,1,0:T(8,128)(2,1)S(1)}, u32[]{:S(2)}, u32[]{:S(2)}) collective-permute-start(bf16[2,96,256]{2,1,0:T(8,128)(2,1)S(1)} %get-tuple-element.19), channel_id=1, source_target_pairs={{8,16},{16,8},{0,4},{24,28},{9,17},{17,9},{1,5},{25,29},{10,18},{1... | collective-permute-start | bytes 294920 | tf_op jit(solution)/shard_map/ppermute | solution.py:648
  62.9 12.8 %copy-start.2 = (bf16[3,3,256,256]{3,2,1,0:T(8,128)(2,1)S(1)}, bf16[3,3,256,256]{3,2,1,0:T(8,128)(2,1)}, u32[]{:S(2)}) copy-start(bf16[3,3,256,256]{3,2,1,0:T(8,128)(2,1)} %param.21) | copy-start | bytes 3538948
  62.9 12.7 %collective-permute-start.2 = (bf16[2,96,256]{2,1,0:T(8,128)(2,1)S(1)}, bf16[2,96,256]{2,1,0:T(8,128)(2,1)S(1)}, u32[]{:S(2)}, u32[]{:S(2)}) collective-permute-start(bf16[2,96,256]{2,1,0:T(8,128)(2,1)S(1)} %get-tuple-element.18.after_ref), channel_id=1, source_target_pairs={{0,8},{8,0},{16,24},{24,16},{1,9},{9,1},{17,25},{25,17},{2,10},{10... | collective-permute-start | bytes 294920 | tf_op jit(solution)/shard_map/ppermute | solution.py:647
